TPU v7x, 128 devices: a whole 4x4x4 slice. The times are simulated.
128 devices in a mesh: frame: 16 (over x, y), row: 8 (over z, core).
Axes of the slice: x: 4, y: 4, z: 4, core: 2. Of those that a mesh axis runs over, the one named last changes fastest.
Arguments:
- hidden_states: bfloat16 [32, 225, 3072], P('frame', None, 'row'), may hold values from -6 to 6
- timestep_index: int32 [32], P('frame'), may hold values from 0 to 999, as said below
- window_offsets: int32 [32, 2], P('frame'), may hold values from 1 to 4, as said below
- mod_weight: bfloat16 [512, 3, 3072], P('frame', None, 'row'), may hold values from -0.25 to 0.25
- qkv_weight: bfloat16 [3072, 3, 3072], P('frame', None, 'row')
- query_gain: float32 [64], replicated
- key_gain: float32 [64], replicated
- out_weight: bfloat16 [3072, 3072], P('row', 'frame'), may hold values from -0.109375 to 0.109375
- fresh_frame: bfloat16 [225, 3072], P(None, 'row'), may hold values from -6 to 6
Outputs:
- queue_out: bfloat16 [32, 225, 3072], P('frame', None, 'row')
Inputs may be any that keep to these rules, and one draw needn't show every extreme that they name: `timestep_index`: levels rise strictly from slot to slot, from 0 at the head slot to 999 at the tail slot. `window_offsets`: some slot has 4 in both columns.
All inputs are finite; a program needn't handle non-finite values.
Results may differ from a plain program's by a relative error of at most 0.009.
Values may be sent and summed in bfloat16 or wider, within the bound.
No kernel may reach another device: no remote copies, remote signals or barrier semaphores. Data moves between devices by JAX's collectives and lax.ppermute only.
A program may use at most 128 MiB of HBM per device.

v0:
```python
import math

import jax
import jax.numpy as jnp
from jax import lax
from jax.sharding import PartitionSpec as P

HEAD = 64
D = 3072
TEMB = 512
REACH = 4


def shifted(array, axis, by):
    peers = lax.axis_size(axis)
    pairs = [(i, i + by) for i in range(peers) if 0 <= i + by < peers]
    return lax.ppermute(array, axis, pairs)


def level_embedding(levels):
    half = TEMB // 2
    freqs = jnp.exp(-math.log(10000.0) * jnp.arange(half).astype(jnp.float32) / half)
    angles = levels.astype(jnp.float32)[:, None] * freqs[None, :]
    waves = jnp.concatenate([jnp.cos(angles), jnp.sin(angles)], axis=1)
    return jax.nn.silu(waves).astype(jnp.bfloat16)


def head_norm(values, gain):
    center = jnp.mean(values, axis=-1, keepdims=True)
    spread = jnp.mean((values - center) ** 2, axis=-1, keepdims=True)
    return ((values - center) * lax.rsqrt(spread + 1e-06) * gain).astype(jnp.bfloat16)


def add_columns(left, piece):
    count = piece.shape[0]
    return jnp.dot(left, piece.reshape(count, -1), preferred_element_type=jnp.float32)


def per_device(
    hidden_states,
    timestep_index,
    window_offsets,
    mod_weight,
    qkv_weight,
    query_gain,
    key_gain,
    out_weight,
    fresh_frame,
):
    frames_dev = hidden_states.shape[0]
    tokens = hidden_states.shape[1]
    width_dev = hidden_states.shape[2]
    group = lax.axis_size("frame")
    place = lax.axis_index("frame")
    first_slot = place * frames_dev
    all_slots = frames_dev * group
    embedded = level_embedding(timestep_index)
    modulation = add_columns(embedded, lax.all_gather(mod_weight, "frame", axis=0, tiled=True))
    modulation = modulation.reshape(frames_dev, 3, width_dev)
    shift = modulation[:, 0]
    scale = modulation[:, 1]
    gate = modulation[:, 2]
    states = hidden_states.astype(jnp.float32)
    sums, squares = lax.psum((jnp.sum(states, axis=2), jnp.sum(states * states, axis=2)), "row")
    mean = (sums / D)[:, :, None]
    meansq = (squares / D)[:, :, None]
    normed = (states - mean) * lax.rsqrt(meansq - mean * mean + 1e-05)
    modulated = (normed * (1.0 + scale[:, None, :]) + shift[:, None, :]).astype(jnp.bfloat16)
    whole = lax.all_gather(modulated, "row", axis=2, tiled=True)
    flat = whole.reshape(frames_dev * tokens, D)
    head_cols = qkv_weight.shape[2]
    heads_dev = head_cols // HEAD
    projected = add_columns(flat, lax.all_gather(qkv_weight, "frame", axis=0, tiled=True))
    projected = projected.reshape(frames_dev, tokens, 3, heads_dev, HEAD)
    queries = head_norm(projected[:, :, 0], query_gain)
    keys = head_norm(projected[:, :, 1], key_gain).reshape(frames_dev, tokens, head_cols)
    values = projected[:, :, 2].astype(jnp.bfloat16).reshape(frames_dev, tokens, head_cols)
    stacked = jnp.stack([keys, values])
    hops = (REACH + frames_dev - 1) // frames_dev
    lower_parts = []
    upper_parts = []
    moving = stacked
    for step in range(hops):
        moving = shifted(moving, "frame", 1)
        lower_parts.insert(0, moving)
    moving = stacked
    for step in range(hops):
        moving = shifted(moving, "frame", -1)
        upper_parts.append(moving)
    lower = jnp.concatenate(lower_parts, axis=1)
    upper = jnp.concatenate(upper_parts, axis=1)
    window = jnp.concatenate([lower, stacked, upper], axis=1)
    block = min(frames_dev, REACH)
    key_frames = block + 2 * REACH
    query_blk = queries.reshape(block * tokens, heads_dev, HEAD)
    key_blk = window[0, 0:key_frames].reshape(key_frames * tokens, heads_dev, HEAD)
    value_blk = window[1, 0:key_frames].reshape(key_frames * tokens, heads_dev, HEAD)
    scores = jnp.einsum(
        "qhd,khd->hqk", query_blk, key_blk, preferred_element_type=jnp.float32
    ) / math.sqrt(HEAD)
    query_slot = first_slot + 0 + jnp.arange(block)
    key_slot = first_slot + 0 - REACH + jnp.arange(key_frames)
    offsets = key_slot[None, :] - query_slot[:, None]
    back = window_offsets[0:block, 0][:, None]
    ahead = window_offsets[0:block, 1][:, None]
    seen = (
        (key_slot[None, :] >= 0)
        & (key_slot[None, :] < all_slots)
        & (offsets >= -back)
        & (offsets <= ahead)
    )
    seen = jnp.repeat(jnp.repeat(seen, tokens, axis=0), tokens, axis=1)
    scores = jnp.where(seen[None, :, :], scores, -jnp.inf)
    top = jnp.max(scores, axis=2, keepdims=True)
    expo = jnp.exp(scores - top)
    total = jnp.sum(expo, axis=2, keepdims=True)
    weights = expo.astype(jnp.bfloat16)
    mixed = jnp.einsum("hqk,khd->qhd", weights, value_blk, preferred_element_type=jnp.float32)
    mixed = mixed / jnp.transpose(total, (1, 0, 2))
    mixed_blocks = mixed.astype(jnp.bfloat16).reshape(block * tokens, head_cols)
    partial_out = jnp.dot(
        mixed_blocks,
        lax.all_gather(out_weight, "frame", axis=1, tiled=True),
        preferred_element_type=jnp.float32,
    )
    attended = (
        lax.psum_scatter(partial_out.astype(jnp.bfloat16), "row", scatter_dimension=1, tiled=True)
        .astype(jnp.float32)
        .reshape(frames_dev, tokens, width_dev)
    )
    updated = (states + gate[:, None, :] * attended).astype(jnp.bfloat16)
    incoming = shifted(updated[0], "frame", -1)
    tail = jnp.where(place == group - 1, fresh_frame, incoming)
    return jnp.concatenate([updated[1:], tail[None]], axis=0)


def solution(mesh):
    return jax.shard_map(
        per_device,
        mesh=mesh,
        in_specs=(
            P("frame", None, "row"),
            P("frame"),
            P("frame", None),
            P("frame", None, "row"),
            P("frame", None, "row"),
            P(),
            P(),
            P("row", "frame"),
            P(None, "row"),
        ),
        out_specs=P("frame", None, "row"),
        check_vma=False,
    )
```

profile of v0, /device:TPU:30, one launch (start us, length us, event | category | flops | bytes accessed | tf_op | source)
XLA Modules:
  0.0 333.3 jit_solution(2864576858802958509)
XLA Ops:
  9.9 15.9 %all-reduce = (f32[2,225]{1,0:T(2,128)S(1)}, f32[2,225]{1,0:T(2,128)S(1)}) all-reduce(f32[2,225]{1,0:T(2,128)S(1)} %get-tuple-element.10, f32[2,225]{1,0:T(2,128)S(1)} %get-tuple-element.9), channel_id=1, replica_groups=mesh['frame'=16,'row'=8] {'row'}, use_global_device_ids=true, to_apply=%region_3.4 | all-reduce | flops 900 | bytes 7200 | tf_op jit(solution)/shard_map/psum | solution.py:64
  26.0 26.4 %all-gather.5.cloned.1.call-done = bf16[512,3,384]{2,0,1:T(8,128)(2,1)} async-done(((bf16[32,3,384]{2,0,1:T(8,128)(2,1)}), bf16[512,3,384]{2,0,1:T(8,128)(2,1)}) %all-gather.5.cloned.1.call-update) | async-done | bytes 1179664 | tf_op jit(solution)/shard_map/all_gather | solution.py:58
  55.5 63.5 %all-gather.9.cloned.1.call-done = bf16[3072,3,384]{2,0,1:T(8,128)(2,1)} async-done(((bf16[192,3,384]{2,0,1:T(8,128)(2,1)}), bf16[3072,3,384]{2,0,1:T(8,128)(2,1)}) %all-gather.9.cloned.1.call-update) | async-done | bytes 7077904 | tf_op jit(solution)/shard_map/all_gather | solution.py:73
  119.0 10.1 %copy.57 = bf16[3072,3,384]{0,2,1:T(8,128)(2,1)} copy(bf16[3072,3,384]{2,0,1:T(8,128)(2,1)} %all-gather.9.cloned.1.call-done) | data formatting | bytes 14155776 | tf_op jit(solution)/shard_map/all_gather | solution.py:73
  129.1 20.3 %all-gather.7.cloned.1.call-done = bf16[2,225,3072]{2,1,0:T(8,128)(2,1)} async-done(((bf16[2,225,384]{2,1,0:T(8,128)(2,1)}), bf16[2,225,3072]{2,1,0:T(8,128)(2,1)}) %all-gather.7.cloned.1.call-update) | async-done | bytes 2764816 | tf_op jit(solution)/shard_map/all_gather | solution.py:69
  149.3 7.1 %fusion.6 = f32[2,225,3,6,64]{1,4,3,2,0:T(8,128)S(1)} fusion(bf16[3,6,64,3072,1]{3,2,1,0,4:T(8,128)(2,1)} %bitcast.90, bf16[2,225,3072]{2,1,0:T(8,128)(2,1)} %all-gather.7.cloned.1.call-done), kind=kOutput, calls=%fused_computation.8 | convolution fusion | flops 3185049600 | bytes 11916288 | tf_op jit(solution)/shard_map/dot_general | solution.py:36
  161.3 5.4 %collective-permute-start.2 = (bf16[2,2,225,384]{3,1,2,0:T(2,128)(2,1)}, bf16[2,2,225,384]{3,1,2,0:T(2,128)(2,1)}, u32[]{:S(2)}, u32[]{:S(2)}) collective-permute-start(bf16[2,2,225,384]{3,1,2,0:T(2,128)(2,1)} %copy.58), channel_id=1, source_target_pairs={{8,0},{16,8},{24,16},{32,24},{40,32},{48,40},{56,48},{64,56},{72,6... | collective-permute-start | bytes 2073608 | tf_op jit(solution)/shard_map/ppermute | solution.py:17
  166.8 13.9 %collective-permute-done = bf16[2,2,225,384]{3,1,2,0:T(2,128)(2,1)} collective-permute-done((bf16[2,2,225,384]{3,1,2,0:T(2,128)(2,1)}, bf16[2,2,225,384]{3,1,2,0:T(2,128)(2,1)}, u32[]{:S(2)}, u32[]{:S(2)}) %collective-permute-start) | collective-permute-done | bytes 691232 | tf_op jit(solution)/shard_map/ppermute | solution.py:17
  189.8 5.4 %collective-permute-start.3 = (bf16[2,2,225,384]{3,1,2,0:T(2,128)(2,1)}, bf16[2,2,225,384]{3,1,2,0:T(2,128)(2,1)}, u32[]{:S(2)}, u32[]{:S(2)}) collective-permute-start(bf16[2,2,225,384]{3,1,2,0:T(2,128)(2,1)} %collective-permute-done.2), channel_id=1, source_target_pairs={{8,0},{16,8},{24,16},{32,24},{40,32},{48,40},{56,48},{64,56},{72,6... | collective-permute-start | bytes 2073608 | tf_op jit(solution)/shard_map/ppermute | solution.py:17
  195.4 3.0 copy.61
  200.7 3.0 copy.60
  213.1 2.5 fusion.43
  215.6 2.9 copy.64
  218.5 5.9 %reshape_squeeze.6 = bf16[2250,6,64]{0,2,1:T(8,128)(2,1)} reshape(bf16[1,10,225,384]{2,1,3,0:T(8,128)(2,1)} %copy.64) | data formatting | bytes 3456000 | tf_op jit(solution)/shard_map/reshape;squeeze | solution.py:97
  224.4 2.9 copy.70
  227.3 4.9 %reshape_squeeze.7 = bf16[2250,6,64]{0,2,1:T(8,128)(2,1)S(1)} reshape(bf16[1,10,225,384]{2,1,3,0:T(8,128)(2,1)} %copy.70) | data formatting | bytes 3456000 | tf_op jit(solution)/shard_map/reshape;squeeze | solution.py:96
  232.2 11.9 %fusion = (f32[6,450]{1,0:T(8,128)S(1)}, f32[6,450,2250]{2,1,0:T(8,128)}) fusion(pred[450,2250]{1,0:T(8,128)(4,1)S(1)} %copy.66, bf16[2250,6,64]{0,2,1:T(8,128)(2,1)S(1)} %reshape_squeeze.7, f32[450,6,64]{0,2,1:T(8,128)} %squeeze.16, f32[64]{0:T(128)S(1)} %copy-done.4, f32[450,6]{0,1:T(8,128)S(1)} %rsqrt.26, f32[450,6]{0,1:T(8,128)S(1)} %div.54), kind=kOutput, calls=%fused_computation.2 | convolution fusion | flops 796513536 | bytes 27764356 | tf_op jit(solution)/shard_map/qhd,khd->hqk/dot_general | solution.py:98
  244.1 12.1 %fusion.1 = f32[6,450]{1,0:T(8,128)S(1)} fusion(f32[6,450,2250]{2,1,0:T(8,128)} %get-tuple-element.29, f32[6,450]{1,0:T(8,128)S(1)} %get-tuple-element.28, pred[450,2250]{1,0:T(8,128)(4,1)S(1)} %copy.66), kind=kLoop, calls=%fused_computation.3 | loop fusion | flops 24297300 | bytes 25334100 | tf_op jit(solution)/shard_map/reduce_sum | solution.py:116
  256.2 12.4 %fusion.16 = bf16[450,6,64]{0,2,1:T(8,128)(2,1)} fusion(bf16[2250,6,64]{0,2,1:T(8,128)(2,1)S(1)} %copy-done.1, f32[6,450,2250]{2,1,0:T(8,128)} %get-tuple-element.29, f32[6,450]{1,0:T(8,128)S(1)} %get-tuple-element.28, pred[450,2250]{1,0:T(8,128)(4,1)S(1)} %copy.66, f32[450,6]{0,1:T(8,128)S(1)} %bitcast.95), kind=kOutput, calls=%fused_computation.18 | convolution fusion | flops 802245632 | bytes 27407700 | tf_op jit(solution)/shard_map/hqk,khd->qhd/dot_general | solution.py:118
  268.7 3.5 %convolution_convert_fusion = bf16[450,3072]{1,0:T(8,128)(2,1)S(1)} fusion(bf16[450,384]{0,1:T(8,128)(2,1)} %bitcast.96, bf16[384,3072]{0,1:T(8,128)(2,1)} %all-gather.11.cloned.1.call-done), kind=kOutput, calls=%fused_computation.7 | convolution fusion | flops 1063065600 | bytes 5469696 | tf_op jit(solution)/shard_map/dot_general | solution.py:121
  272.1 2.8 copy.73
  275.0 43.5 %reduce-scatter.4.cloned.1.call-done = bf16[384,450]{1,0:T(8,128)(2,1)} async-done(((bf16[3072,450]{1,0:T(8,128)(2,1)}), bf16[384,450]{1,0:T(8,128)(2,1)}) %reduce-scatter.4.cloned.1.call-update) | async-done | bytes 345616
  319.9 2.7 collective-permute-start.4
  322.7 3.0 collective-permute-done.4
  (79 shorter events, 34.7 us)
Async XLA Ops:
  6.5 47.8 %copy-start = (bf16[2,225,384]{2,0,1:T(2,128)(2,1)S(1)}, bf16[2,225,384]{2,0,1:T(2,128)(2,1)}, u32[]{:S(2)}) copy-start(bf16[2,225,384]{2,0,1:T(2,128)(2,1)} %param.9) | copy-start | bytes 1036804
  6.5 48.8 %copy-start.5 = (f32[64]{0:T(128)S(1)}, f32[64]{0:T(128)}, u32[]{:S(2)}) copy-start(f32[64]{0:T(128)} %param.15) | copy-start | bytes 772
  6.5 45.8 %all-gather.5.cloned.1.call-start = ((), (), s32[]{:S(2)}) async-start(), calls=%async_computation.1 | async-start | bytes 1253376 | tf_op jit(solution)/shard_map/all_gather | solution.py:58
  7.3 111.7 %all-gather.9.cloned.1.call-start = ((), (), s32[]{:S(2)}) async-start(), calls=%async_computation.3 | async-start | bytes 7520256 | tf_op jit(solution)/shard_map/all_gather | solution.py:73
  8.0 141.3 %all-gather.7.cloned.1.call-start = ((), (), s32[]{:S(2)}) async-start(), calls=%async_computation.2 | async-start | bytes 3207168 | tf_op jit(solution)/shard_map/all_gather | solution.py:69
  55.3 213.3 %all-gather.11.cloned.1.call-start = ((), (), s32[]{:S(2)}) async-start(), calls=%async_computation.4 | async-start | bytes 2506752 | tf_op jit(solution)/shard_map/all_gather | solution.py:123
  156.5 25.4 %copy-start.3 = (s32[2,2]{1,0:T(2,128)S(1)}, s32[2,2]{1,0:T(2,128)}, u32[]{:S(2)}) copy-start(s32[2,2]{1,0:T(2,128)} %param.11) | copy-start | bytes 52
  160.0 20.6 %collective-permute-start = (bf16[2,2,225,384]{3,1,2,0:T(2,128)(2,1)}, bf16[2,2,225,384]{3,1,2,0:T(2,128)(2,1)}, u32[]{:S(2)}, u32[]{:S(2)}) collective-permute-start(bf16[2,2,225,384]{3,1,2,0:T(2,128)(2,1)} %copy.58), channel_id=1, source_target_pairs={{0,8},{8,16},{16,24},{24,32},{32,40},{40,48},{48,56},{56,64},{64,7... | collective-permute-start | bytes 2073608 | tf_op jit(solution)/shard_map/ppermute | solution.py:17
  161.3 28.5 %collective-permute-start.2 = (bf16[2,2,225,384]{3,1,2,0:T(2,128)(2,1)}, bf16[2,2,225,384]{3,1,2,0:T(2,128)(2,1)}, u32[]{:S(2)}, u32[]{:S(2)}) collective-permute-start(bf16[2,2,225,384]{3,1,2,0:T(2,128)(2,1)} %copy.58), channel_id=1, source_target_pairs={{8,0},{16,8},{24,16},{32,24},{40,32},{48,40},{56,48},{64,56},{72,6... | collective-permute-start | bytes 2073608 | tf_op jit(solution)/shard_map/ppermute | solution.py:17
  166.7 151.8 %reduce-scatter.4.cloned.1.call-start = ((), (), s32[]{:S(2)}) async-start(), calls=%async_computation.5 | async-start | bytes 3538944
  180.6 20.0 %collective-permute-start.1 = (bf16[2,2,225,384]{3,1,2,0:T(2,128)(2,1)}, bf16[2,2,225,384]{3,1,2,0:T(2,128)(2,1)}, u32[]{:S(2)}, u32[]{:S(2)}) collective-permute-start(bf16[2,2,225,384]{3,1,2,0:T(2,128)(2,1)} %collective-permute-done), channel_id=1, source_target_pairs={{0,8},{8,16},{16,24},{24,32},{32,40},{40,48},{48,56},{56,64},{64,7... | collective-permute-start | bytes 2073608 | tf_op jit(solution)/shard_map/ppermute | solution.py:17
  189.8 20.1 %collective-permute-start.3 = (bf16[2,2,225,384]{3,1,2,0:T(2,128)(2,1)}, bf16[2,2,225,384]{3,1,2,0:T(2,128)(2,1)}, u32[]{:S(2)}, u32[]{:S(2)}) collective-permute-start(bf16[2,2,225,384]{3,1,2,0:T(2,128)(2,1)} %collective-permute-done.2), channel_id=1, source_target_pairs={{8,0},{16,8},{24,16},{32,24},{40,32},{48,40},{56,48},{64,56},{72,6... | collective-permute-start | bytes 2073608 | tf_op jit(solution)/shard_map/ppermute | solution.py:17
  224.4 7.8 %copy-start.4 = (f32[64]{0:T(128)S(1)}, f32[64]{0:T(128)}, u32[]{:S(2)}) copy-start(f32[64]{0:T(128)} %param.14) | copy-start | bytes 772
  244.1 12.1 %copy-start.1 = (bf16[2250,6,64]{0,2,1:T(8,128)(2,1)S(1)}, bf16[2250,6,64]{0,2,1:T(8,128)(2,1)}, u32[]{:S(2)}) copy-start(bf16[2250,6,64]{0,2,1:T(8,128)(2,1)} %reshape_squeeze.6) | copy-start | bytes 5184004
  274.9 50.7 %copy-start.2 = (bf16[225,384]{1,0:T(8,128)(2,1)S(1)}, bf16[225,384]{1,0:T(8,128)(2,1)}, u32[]{:S(2)}) copy-start(bf16[225,384]{1,0:T(8,128)(2,1)} %param.17) | copy-start | bytes 518404
  319.9 5.7 %collective-permute-start.4 = (bf16[225,384]{1,0:T(8,128)(2,1)S(1)}, bf16[225,384]{1,0:T(8,128)(2,1)S(1)}, u32[]{:S(2)}, u32[]{:S(2)}) collective-permute-start(bf16[225,384]{1,0:T(8,128)(2,1)S(1)} %get-tuple-element.20), channel_id=1, source_target_pairs={{8,0},{16,8},{24,16},{32,24},{40,32},{48,40},{56,48},{64,56},{72,6... | collective-permute-start | bytes 518408 | tf_op jit(solution)/shard_map/ppermute | solution.py:17
Sparse Core Ops, SparseCore 0:
  9.5 42.7 all-gather.4
  54.5 64.4 all-gather.8
  120.7 28.6 all-gather.6
  166.8 57.5 all-gather.10
  275.1 43.3 reduce-scatter.3
where the time goes:
time: 338 us; the launch traced here: 333 us
  waiting for transfers between devices  172 us (51%)
  local copies, waits for them, and re-layouts  62.2 us (18%)
  matrix products  35.4 us (10%)
  other arithmetic  18.1 us (5%)
  starting transfers between devices  16.3 us (5%)
  blocking collectives  15.9 us (5%)
  between operations  13.5 us (4%)
    all_gather x1, waiting for transfers between devices, per_device(): lax.all_gather(qkv_weight, 'frame', axis=0, tiled=True)  63.5 us
    unnamed x6, waiting for transfers between devices  45 us
    all_gather x1, waiting for transfers between devices, per_device(): lax.all_gather(mod_weight, 'frame', axis=0, tiled=True)  26.4 us
    all_gather x1, waiting for transfers between devices, per_device(): whole = lax.all_gather(modulated, 'row', axis=2, tiled=True)  20.3 us
    ppermute x5, waiting for transfers between devices, shifted(): return lax.ppermute(array, axis, pairs)  16.8 us
    ppermute x5, starting transfers between devices, shifted(): return lax.ppermute(array, axis, pairs)  16.1 us
    psum x1, blocking collectives, per_device(): lax.psum((jnp.sum(states, axis=2), jnp.sum(states * states, axis=2)), 'row')  15.9 us
    dot_general x1, matrix products, per_device(): jnp.einsum('hqk,khd->qhd', weights, value_blk, preferred_element_type=jnp...  12.4 us
  transfers between devices with their start and end apart: 10, of which 6 were waited for; matrix products, arithmetic and copies ran while one was open for 29% of the time, Pallas kernels for 0%

commit v1 on v0

v1 whole, which is shorter than its diff:
```python
import math

import jax
import jax.numpy as jnp
from jax import lax
from jax.experimental import pallas as pl
from jax.experimental.pallas import tpu as pltpu
from jax.sharding import PartitionSpec as P

HEAD = 64
D = 3072
TEMB = 512
REACH = 4
SIDE = 4
PADDED = 240
KEYS = 256
PAIR = 2 * HEAD
ORIGIN = (0, -1, 1, 2)


def frame_step(array, over_x, over_y):
    pairs = [
        (x * SIDE + y, (x + over_x) % SIDE * SIDE + (y + over_y) % SIDE)
        for x in range(SIDE)
        for y in range(SIDE)
    ]
    return lax.ppermute(array, "frame", pairs)


def along_x(array, by):
    return frame_step(array, by, 0)


def along_y(array, by):
    return frame_step(array, 0, by)


def along_z(array, by):
    pairs = [(z * 2 + c, (z + by) % SIDE * 2 + c) for z in range(SIDE) for c in range(2)]
    return lax.ppermute(array, "row", pairs)


def other_core(array):
    pairs = [(z * 2 + c, z * 2 + 1 - c) for z in range(SIDE) for c in range(2)]
    return lax.ppermute(array, "row", pairs)


def next_frame(array, by):
    peers = lax.axis_size("frame")
    return lax.ppermute(array, "frame", [(i, (i + by) % peers) for i in range(peers)])


def ring_direct(array, step):
    return [array, step(array, 1), step(array, -1), step(array, 2)]


def ring_relay(array, step):
    below = step(array, 1)
    above = step(array, -1)
    half = array.shape[0] // 2
    return [array, below, above, step(below[:half], 1), step(above[half:], -1)]


def level_embedding(levels):
    half = TEMB // 2
    freqs = jnp.exp(-math.log(10000.0) * jnp.arange(half).astype(jnp.float32) / half)
    angles = levels.astype(jnp.float32)[:, None] * freqs[None, :]
    waves = jnp.concatenate([jnp.cos(angles), jnp.sin(angles)], axis=1)
    return jax.nn.silu(waves).astype(jnp.bfloat16)


def wrap(value, by):
    return lax.rem(value + (by + SIDE), SIDE)


def piece_views(refs):
    views = []
    for hop in range(3):
        views.append([(refs[hop], i) for i in range(SIDE)])
    if len(refs) == SIDE:
        views.append([(refs[3], i) for i in range(SIDE)])
    else:
        views.append([(refs[3], 0), (refs[3], 1), (refs[4], 0), (refs[4], 1)])
    return views


def load_pieces(refs, pos_ref, y_first, rows, source, target, sems, first_sem):
    copies = []
    x = pos_ref[0]
    y = pos_ref[1]
    for outer, line in enumerate(piece_views(refs)):
        for inner, (ref, index) in enumerate(line):
            if y_first:
                over_x, over_y = ORIGIN[outer], ORIGIN[inner]
            else:
                over_x, over_y = ORIGIN[inner], ORIGIN[outer]
            owner = wrap(x, over_x) * SIDE + wrap(y, over_y)
            start = pl.multiple_of(owner * rows, rows)
            copy = pltpu.make_async_copy(
                ref.at[index, source],
                target.at[pl.ds(start, rows)],
                sems.at[first_sem + len(copies)],
            )
            copy.start()
            copies.append(copy)
    return copies


def head_norm_pair(values, gain):
    lane = lax.broadcasted_iota(jnp.int32, values.shape, 1)
    low = lane < HEAD

    def mean_of(array):
        first = jnp.sum(jnp.where(low, array, 0.0), axis=1, keepdims=True)
        second = jnp.sum(jnp.where(low, 0.0, array), axis=1, keepdims=True)
        return jnp.where(low, first, second) * (1.0 / HEAD)

    centered = values - mean_of(values)
    spread = mean_of(centered * centered)
    return (centered * lax.rsqrt(spread + 1e-06) * gain).astype(jnp.bfloat16)


def modulation_kernel(pos_ref, emb_ref, *refs):
    pieces, (out_ref, weight, sems) = refs[:-3], refs[-3:]
    copies = load_pieces(pieces, pos_ref, True, 32, slice(None), weight, sems, 0)
    for copy in copies:
        copy.wait()
    both = jnp.dot(emb_ref[...], weight[...], preferred_element_type=jnp.float32)
    out_ref[0:2] = both[:, :384]
    out_ref[2:4] = both[:, 384:]


def modulate_kernel(pos_ref, own_ref, other_ref, own_mod, other_mod, out_ref):
    tokens = own_ref.shape[2]
    width = own_ref.shape[3]
    z = pos_ref[2]
    core = pos_ref[3]
    for slot in range(2):
        total = jnp.zeros((tokens, width), jnp.float32)
        square = jnp.zeros((tokens, width), jnp.float32)
        for ref in (own_ref, other_ref):
            for hop in range(SIDE):
                part = ref[hop, slot].astype(jnp.float32)
                total += part
                square += part * part
        mean = jnp.sum(total, axis=1, keepdims=True) * (1.0 / D)
        meansq = jnp.sum(square, axis=1, keepdims=True) * (1.0 / D)
        inverse = lax.rsqrt(meansq - mean * mean + 1e-05)
        for ref, mod, at_core in ((own_ref, own_mod, core), (other_ref, other_mod, 1 - core)):
            for hop in range(SIDE):
                part = ref[hop, slot].astype(jnp.float32)
                normed = (part - mean) * inverse
                shift = mod[hop, slot][None]
                scale = mod[hop, 2 + slot][None]
                owner = wrap(z, ORIGIN[hop]) * 2 + at_core
                columns = pl.ds(pl.multiple_of(owner * width, width), width)
                out_ref[slot, 0:tokens, columns] = (normed * (1.0 + scale) + shift).astype(jnp.bfloat16)
        out_ref[slot, tokens:, :] = jnp.zeros((PADDED - tokens, D), jnp.bfloat16)


def key_value_kernel(tokens, count, pos_ref, x_ref, gain_ref, *refs):
    key_refs = refs[:count]
    value_refs = refs[count:-3]
    out_ref, weight, sems = refs[-3:]
    copies = load_pieces(key_refs, pos_ref, True, 192, slice(None), weight.at[:, 0:384], sems, 0)
    copies += load_pieces(value_refs, pos_ref, False, 192, slice(None), weight.at[:, 384:768], sems, 16)
    for copy in copies:
        copy.wait()
    x = x_ref[...].reshape(2 * PADDED, D)
    for block in range(3):
        both = jnp.dot(
            x, weight[:, block * 2 * PAIR : (block + 1) * 2 * PAIR], preferred_element_type=jnp.float32
        )
        for side in range(2):
            group = 2 * block + side
            part = both[:, side * PAIR : (side + 1) * PAIR]
            columns = slice(group % 3 * PAIR, (group % 3 + 1) * PAIR)
            if group < 3:
                part = head_norm_pair(part, gain_ref[...])
                for slot in range(2):
                    rows = part[slot * PADDED : (slot + 1) * PADDED]
                    out_ref[slot, :, columns] = rows
                    out_ref[slot, tokens:, columns] = jnp.broadcast_to(rows[0:1], (PADDED - tokens, PAIR))
            else:
                part = part.astype(jnp.bfloat16)
                for slot in range(2):
                    out_ref[2 + slot, :, columns] = part[slot * PADDED : (slot + 1) * PADDED]


def query_kernel(pos_ref, x_ref, gain_ref, *refs):
    pieces, (out_ref, weight, sems) = refs[:-3], refs[-3:]
    copies = load_pieces(pieces, pos_ref, True, 192, slice(None), weight, sems, 0)
    for copy in copies:
        copy.wait()
    x = x_ref[...].reshape(2 * PADDED, D)
    whole = jnp.dot(x, weight[...], preferred_element_type=jnp.float32)
    for pair in range(3):
        part = head_norm_pair(whole[:, pair * PAIR : (pair + 1) * PAIR], gain_ref[...])
        part = part * jnp.asarray(1.0 / math.sqrt(HEAD), jnp.bfloat16)
        for slot in range(2):
            out_ref[slot, :, pair * PAIR : (pair + 1) * PAIR] = part[slot * PADDED : (slot + 1) * PADDED]


def attention_kernel(tokens, seen_ref, q_ref, m2, m1, own, p1, p2, out_ref, keys, values, scores, top, mix):
    @pl.when(pl.program_id(0) == 0)
    def _():
        row = lax.broadcasted_iota(jnp.int32, (KEYS, PAIR), 0)
        ones = jnp.where(row < tokens, 1.0, 0.0).astype(jnp.bfloat16)
        for slot in range(10):
            values[slot, :, PAIR:] = ones
            values[slot, PADDED:, 0:PAIR] = jnp.zeros((KEYS - PADDED, PAIR), jnp.bfloat16)

    for index, ref in enumerate((m2, m1, own, p1, p2)):
        for half in range(2):
            slot = 2 * index + half
            keys[slot, 0:PADDED, :] = ref[half]
            keys[slot, PADDED:, :] = ref[half, 0 : KEYS - PADDED, :]
            values[slot, 0:PADDED, 0:PAIR] = ref[2 + half]
    lane = lax.broadcasted_iota(jnp.int32, (PADDED, PAIR), 1)
    low = lane < HEAD
    for slot in range(2):
        query = q_ref[slot]
        nothing = jnp.zeros_like(query)
        both = jnp.concatenate([jnp.where(low, query, nothing), jnp.where(low, nothing, query)], axis=0)
        first = seen_ref[2 * slot]
        last = seen_ref[2 * slot + 1]
        top[...] = jnp.full(top.shape, -jnp.inf, jnp.float32)
        mix[...] = jnp.zeros(mix.shape, jnp.float32)

        def score(at, _):
            part = lax.dot_general(
                both, keys[at], (((1,), (1,)), ((), ())), preferred_element_type=jnp.float32
            )
            scores[at] = part
            top[...] = jnp.maximum(top[...], jnp.maximum(part[:, :PAIR], part[:, PAIR:]))
            return 0

        lax.fori_loop(first, last + 1, score, 0)
        peak = jnp.max(top[...], axis=1, keepdims=True)

        def blend(at, _):
            expo = jnp.exp(scores[at] - peak).astype(jnp.bfloat16)
            mix[...] += jnp.dot(expo, values[at], preferred_element_type=jnp.float32)
            return 0

        lax.fori_loop(first, last + 1, blend, 0)
        shares = mix[:, :PAIR] / mix[:, PAIR:]
        out_ref[slot] = jnp.where(low, shares[:PADDED], shares[PADDED:]).astype(jnp.bfloat16)


def out_kernel(tokens, pos_ref, x_ref, *refs):
    pieces, (keep_ref, send_ref, weight, sems) = refs[:-4], refs[-4:]
    copies = load_pieces(pieces, pos_ref, True, 192, slice(0, 192), weight, sems, 0)
    for copy in copies:
        copy.wait()
    x = x_ref[...].reshape(2 * PADDED, 384)
    z = pos_ref[2]
    core = pos_ref[3]
    for ref, at_core in ((send_ref, 1 - core), (keep_ref, core)):
        for hop in range(SIDE):
            owner = lax.rem(z + hop, SIDE) * 2 + at_core
            rows = pl.ds(pl.multiple_of(owner * 384, 384), 384)
            part = lax.dot_general(
                x, weight[rows, :], (((1,), (1,)), ((), ())), preferred_element_type=jnp.float32
            ).astype(jnp.bfloat16)
            for slot in range(2):
                ref[hop, slot] = part[slot * PADDED : slot * PADDED + tokens]


def gate_kernel(pos_ref, emb_ref, *refs):
    pieces, (out_ref, weight, sems) = refs[:-3], refs[-3:]
    copies = load_pieces(pieces, pos_ref, True, 32, slice(192, 224), weight, sems, 0)
    for copy in copies:
        copy.wait()
    out_ref[...] = jnp.dot(emb_ref[...], weight[...], preferred_element_type=jnp.float32)


SMEM = pl.BlockSpec(memory_space=pltpu.SMEM)
VMEM = pl.BlockSpec(memory_space=pltpu.VMEM)
ANY = pl.BlockSpec(memory_space=pl.ANY)


def call(kernel, out_shape, in_specs, scratch, name, flops, moved):
    out_specs = [VMEM] * len(out_shape) if isinstance(out_shape, list) else VMEM
    return pl.pallas_call(
        kernel,
        out_shape=out_shape,
        in_specs=in_specs,
        out_specs=out_specs,
        scratch_shapes=scratch,
        name=name,
        compiler_params=pltpu.CompilerParams(vmem_limit_bytes=48 << 20),
        cost_estimate=pl.CostEstimate(flops=flops, bytes_accessed=moved, transcendentals=0),
    )


def struct(shape, dtype=jnp.bfloat16):
    return jax.ShapeDtypeStruct(shape, dtype)


def per_device(
    hidden_states,
    timestep_index,
    window_offsets,
    mod_weight,
    qkv_weight,
    query_gain,
    key_gain,
    out_weight,
    fresh_frame,
):
    tokens = hidden_states.shape[1]
    width = hidden_states.shape[2]
    place = lax.axis_index("frame")
    row = lax.axis_index("row")
    slots = 2 * lax.axis_size("frame")
    pos = jnp.stack([place // SIDE, place % SIDE, row // 2, row % 2]).astype(jnp.int32)

    head = next_frame(hidden_states[0], -1)
    plan = jnp.concatenate([timestep_index[0:1], window_offsets[0]])
    next_plan = next_frame(plan, -1)
    states = jnp.stack([hidden_states[1], head])
    levels = jnp.stack([timestep_index[1], next_plan[0]])
    back = jnp.stack([window_offsets[1, 0], next_plan[1]])
    ahead = jnp.stack([window_offsets[1, 1], next_plan[2]])

    mod_line = jnp.stack(ring_direct(mod_weight[:, :2].reshape(32, 2 * width), along_y))
    mod_pieces = ring_direct(mod_line, along_x)

    own_states = jnp.stack(ring_direct(states, along_z))
    other_states = other_core(own_states)

    key_line = jnp.stack(ring_direct(qkv_weight[:, 1], along_y))
    value_line = jnp.stack(ring_direct(qkv_weight[:, 2], along_x))
    key_pieces = ring_relay(key_line, along_x)
    value_pieces = ring_relay(value_line, along_y)

    embedded = level_embedding(levels)
    mods = call(
        modulation_kernel,
        struct((4, width), jnp.float32),
        [SMEM, VMEM] + [ANY] * len(mod_pieces),
        [pltpu.VMEM((TEMB, 2 * width), jnp.bfloat16), pltpu.SemaphoreType.DMA((16,))],
        "modulation",
        4 * TEMB * width * 2,
        TEMB * width * 4,
    )(pos, embedded, *mod_pieces)
    own_mods = jnp.stack(ring_direct(mods, along_z))
    other_mods = other_core(own_mods)
    modulated = call(
        modulate_kernel,
        struct((2, PADDED, D)),
        [SMEM] + [VMEM] * 4,
        [],
        "modulate",
        20 * 2 * PADDED * D,
        8 * PADDED * D,
    )(pos, own_states, other_states, own_mods, other_mods)

    key_gains = jnp.tile(key_gain, 2)[None]
    query_gains = jnp.tile(query_gain, 2)[None]
    kv = call(
        lambda *refs: key_value_kernel(tokens, len(key_pieces), *refs),
        struct((4, PADDED, width)),
        [SMEM, VMEM, VMEM] + [ANY] * (len(key_pieces) + len(value_pieces)),
        [pltpu.VMEM((D, 2 * width), jnp.bfloat16), pltpu.SemaphoreType.DMA((32,))],
        "keys_values",
        4 * PADDED * D * 2 * width,
        D * width * 4 + PADDED * D * 4,
    )(pos, modulated, key_gains, *key_pieces, *value_pieces)

    from_m1 = next_frame(kv, 1)
    from_p1 = next_frame(kv, -1)
    from_m2 = next_frame(from_m1, 1)
    from_p2 = next_frame(from_p1, -1)

    query_line = jnp.stack(ring_direct(qkv_weight[:, 0], along_y))
    query_pieces = ring_relay(query_line, along_x)
    out_line = jnp.stack(
        ring_direct(jnp.concatenate([out_weight.T, mod_weight[:, 2]], axis=0), along_y)
    )
    out_pieces = ring_relay(out_line, along_x)

    queries = call(
        query_kernel,
        struct((2, PADDED, width)),
        [SMEM, VMEM, VMEM] + [ANY] * len(query_pieces),
        [pltpu.VMEM((D, width), jnp.bfloat16), pltpu.SemaphoreType.DMA((16,))],
        "queries",
        4 * PADDED * D * width,
        D * width * 2 + PADDED * D * 4,
    )(pos, modulated, query_gains, *query_pieces)

    first_slot = 2 * place + 1
    here = jnp.arange(2, dtype=jnp.int32)
    low = jnp.maximum(here - back, -first_slot) + REACH
    high = jnp.minimum(here + ahead, slots - 1 - first_slot) + REACH
    seen = jnp.stack([low, high], axis=1).reshape(4).astype(jnp.int32)
    kv_block = pl.BlockSpec((4, PADDED, PAIR), lambda pair: (0, 0, pair))
    q_block = pl.BlockSpec((2, PADDED, PAIR), lambda pair: (0, 0, pair))
    mixed = pl.pallas_call(
        lambda *refs: attention_kernel(tokens, *refs),
        out_shape=struct((2, PADDED, width)),
        grid=(3,),
        in_specs=[SMEM, q_block] + [kv_block] * 5,
        out_specs=q_block,
        scratch_shapes=[
            pltpu.VMEM((10, KEYS, PAIR), jnp.bfloat16),
            pltpu.VMEM((10, KEYS, 2 * PAIR), jnp.bfloat16),
            pltpu.VMEM((10, 2 * PADDED, KEYS), jnp.float32),
            pltpu.VMEM((2 * PADDED, PAIR), jnp.float32),
            pltpu.VMEM((2 * PADDED, 2 * PAIR), jnp.float32),
        ],
        name="attention",
        compiler_params=pltpu.CompilerParams(vmem_limit_bytes=48 << 20),
        cost_estimate=pl.CostEstimate(
            flops=6 * 9 * 4 * 480 * 256 * 256, bytes_accessed=6 << 20, transcendentals=54 * 480 * 256
        ),
    )(seen, queries, from_m2, from_m1, kv, from_p1, from_p2)

    keep, send = call(
        lambda *refs: out_kernel(tokens, *refs),
        [struct((SIDE, 2, tokens, width))] * 2,
        [SMEM, VMEM] + [ANY] * len(out_pieces),
        [pltpu.VMEM((D, width), jnp.bfloat16), pltpu.SemaphoreType.DMA((16,))],
        "out_projection",
        4 * PADDED * D * width,
        D * width * 2 + PADDED * D * 4,
    )(pos, mixed, *out_pieces)
    gate = call(
        gate_kernel,
        struct((2, width), jnp.float32),
        [SMEM, VMEM] + [ANY] * len(out_pieces),
        [pltpu.VMEM((TEMB, width), jnp.bfloat16), pltpu.SemaphoreType.DMA((16,))],
        "gate",
        4 * TEMB * width,
        TEMB * width * 4,
    )(pos, embedded, *out_pieces)

    swapped = other_core(send)
    chip = [keep[hop].astype(jnp.float32) + swapped[hop].astype(jnp.float32) for hop in range(SIDE)]
    arrived = [along_z(chip[hop].astype(jnp.bfloat16), hop) for hop in range(1, SIDE)]
    attended = chip[0]
    for part in arrived:
        attended = attended + part.astype(jnp.float32)
    updated = (states.astype(jnp.float32) + gate[:, None, :] * attended).astype(jnp.bfloat16)
    tail = jnp.where(place == lax.axis_size("frame") - 1, fresh_frame, updated[1])
    return jnp.stack([updated[0], tail])


def solution(mesh):
    return jax.shard_map(
        per_device,
        mesh=mesh,
        in_specs=(
            P("frame", None, "row"),
            P("frame"),
            P("frame", None),
            P("frame", None, "row"),
            P("frame", None, "row"),
            P(),
            P(),
            P("row", "frame"),
            P(None, "row"),
        ),
        out_specs=P("frame", None, "row"),
        check_vma=False,
    )
```

time: 338 us -> 247 us (0.73)
  the two profiles are of different devices: /device:TPU:30 before, /device:TPU:7 now
where the time goes in v1:
time: 247 us; the launch traced here: 245 us
  starting transfers between devices  87.2 us (35%)
  waiting for transfers between devices  74 us (30%)
  Pallas kernels  43.5 us (18%)
  local copies, waits for them, and re-layouts  28.3 us (11%)
  other arithmetic  11.2 us (5%)
    ppermute x34, starting transfers between devices, frame_step(): return lax.ppermute(array, 'frame', pairs)  43.2 us
    ppermute x34, waiting for transfers between devices, frame_step(): return lax.ppermute(array, 'frame', pairs)  40.5 us
    ppermute x9, waiting for transfers between devices, along_z(): return lax.ppermute(array, 'row', pairs)  23.8 us
    pallas_call x1, Pallas kernels, per_device(): pl.pallas_call(lambda *refs: attention_kernel(tokens, *refs), out_shape=s...  20 us
    ppermute x6, starting transfers between devices, next_frame(): lax.ppermute(array, 'frame', [(i, (i + by) % peers) for i in range(peers)])  16.1 us
    ppermute x3, starting transfers between devices, other_core(): return lax.ppermute(array, 'row', pairs)  15.5 us
    ppermute x9, starting transfers between devices, along_z(): return lax.ppermute(array, 'row', pairs)  12.3 us
    slice x8, local copies, waits for them, and re-layouts, ring_relay(): return [array, below, above, step(below[:half], 1), step(above[half:], -1)]  8.46 us
  transfers between devices with their start and end apart: 52, of which 11 were waited for; matrix products, arithmetic and copies ran while one was open for 11% of the time, Pallas kernels for 16%

profile of v1, /device:TPU:7, one launch (start us, length us, event | category | flops | bytes accessed | tf_op | source)
XLA Modules:
  0.0 244.8 jit_solution(5224537017135875532)
XLA Ops:
  0.9 3.0 %collective-permute-start.15 = (bf16[32,768]{1,0:T(8,128)(2,1)S(1)}, bf16[32,768]{1,0:T(8,128)(2,1)S(1)}, u32[]{:S(2)}, u32[]{:S(2)}) collective-permute-start(bf16[32,768]{1,0:T(8,128)(2,1)S(1)} %bitcast.104), channel_id=1, source_target_pairs={{0,16},{8,24},{16,0},{24,8},{32,48},{40,56},{48,32},{56,40},{64,80... | collective-permute-start | bytes 147464 | tf_op jit(solution)/shard_map/ppermute | solution.py:27
  7.7 3.5 %collective-permute-done = bf16[225,384]{1,0:T(8,128)(2,1)S(1)} collective-permute-done((bf16[225,384]{1,0:T(8,128)(2,1)S(1)}, bf16[225,384]{1,0:T(8,128)(2,1)S(1)}, u32[]{:S(2)}, u32[]{:S(2)}) %collective-permute-start) | collective-permute-done | bytes 172832 | tf_op jit(solution)/shard_map/ppermute | solution.py:50
  11.9 3.6 %collective-permute-start.11 = (bf16[2,225,384]{2,1,0:T(8,128)(2,1)S(1)}, bf16[2,225,384]{2,1,0:T(8,128)(2,1)S(1)}, u32[]{:S(2)}, u32[]{:S(2)}) collective-permute-start(bf16[2,225,384]{2,1,0:T(8,128)(2,1)S(1)} %get-tuple-element.23), channel_id=1, source_target_pairs={{0,4},{1,5},{2,6},{3,7},{4,0},{5,1},{6,2},{7,3},{8,12},{9,13},{10,... | collective-permute-start | bytes 1036808 | tf_op jit(solution)/shard_map/ppermute | solution.py:40
  19.1 4.2 %collective-permute-start.32 = (bf16[192,384]{1,0:T(8,128)(2,1)}, bf16[192,384]{1,0:T(8,128)(2,1)S(1)}, u32[]{:S(2)}, u32[]{:S(2)}) collective-permute-start(bf16[192,384]{1,0:T(8,128)(2,1)} %get-tuple-element.18), channel_id=1, source_target_pairs={{0,16},{8,24},{16,0},{24,8},{32,48},{40,56},{48,32},{56,40},{64,80... | collective-permute-start | bytes 442376 | tf_op jit(solution)/shard_map/ppermute | solution.py:27
  24.8 6.8 %collective-permute-done.10 = bf16[2,225,384]{2,1,0:T(8,128)(2,1)S(1)} collective-permute-done((bf16[2,225,384]{2,1,0:T(8,128)(2,1)S(1)}, bf16[2,225,384]{2,1,0:T(8,128)(2,1)S(1)}, u32[]{:S(2)}, u32[]{:S(2)}) %collective-permute-start.10) | collective-permute-done | bytes 345632 | tf_op jit(solution)/shard_map/ppermute | solution.py:40
  42.7 3.3 %collective-permute-start.1 = (s32[3]{0:T(128)S(1)}, s32[3]{0:T(128)S(1)}, u32[]{:S(2)}, u32[]{:S(2)}) collective-permute-start(s32[3]{0:T(128)S(1)} %pad_add_fusion.2), channel_id=1, source_target_pairs={{0,120},{8,0},{16,8},{24,16},{32,24},{40,32},{48,40},{56,48},{64,5... | collective-permute-start | bytes 44 | tf_op jit(solution)/shard_map/ppermute | solution.py:50
  46.0 3.5 %collective-permute-done.1 = s32[3]{0:T(128)S(1)} collective-permute-done((s32[3]{0:T(128)S(1)}, s32[3]{0:T(128)S(1)}, u32[]{:S(2)}, u32[]{:S(2)}) %collective-permute-start.1) | collective-permute-done | bytes 44 | tf_op jit(solution)/shard_map/ppermute | solution.py:50
  51.0 4.3 %collective-permute-start.41 = (bf16[4,192,384]{2,1,0:T(8,128)(2,1)S(1)}, bf16[4,192,384]{2,1,0:T(8,128)(2,1)S(1)}, u32[]{:S(2)}, u32[]{:S(2)}) collective-permute-start(bf16[4,192,384]{2,1,0:T(8,128)(2,1)S(1)} %pad_maximum_fusion.4.refs_8_), channel_id=1, source_target_pairs={{0,24},{8,0},{16,8},{24,16},{32,56},{40,32},{48,40},{56,48},{64,88... | collective-permute-start | bytes 1769480 | tf_op jit(solution)/shard_map/ppermute | solution.py:27
  59.5 3.7 %collective-permute-done.33.refs_4_ = bf16[4,192,384]{2,1,0:T(8,128)(2,1)S(1)} collective-permute-done((bf16[4,192,384]{2,1,0:T(8,128)(2,1)S(1)}, bf16[4,192,384]{2,1,0:T(8,128)(2,1)S(1)}, u32[]{:S(2)}, u32[]{:S(2)}) %collective-permute-start.33) | collective-permute-done | bytes 589856 | tf_op jit(solution)/shard_map/ppermute | solution.py:27
  73.0 3.2 %collective-permute-start.43 = (bf16[2,192,384]{2,1,0:T(8,128)(2,1)}, bf16[2,192,384]{2,1,0:T(8,128)(2,1)}, u32[]{:S(2)}, u32[]{:S(2)}) collective-permute-start(bf16[2,192,384]{2,1,0:T(8,128)(2,1)} %slice.139), channel_id=1, source_target_pairs={{0,24},{8,0},{16,8},{24,16},{32,56},{40,32},{48,40},{56,48},{64,88... | collective-permute-start | bytes 884744 | tf_op jit(solution)/shard_map/ppermute | solution.py:27
  76.9 3.8 %collective-permute-start.22 = (f32[4,4,384]{2,1,0:T(4,128)S(1)}, f32[4,4,384]{2,1,0:T(4,128)S(1)}, u32[]{:S(2)}, u32[]{:S(2)}) collective-permute-start(f32[4,4,384]{2,1,0:T(4,128)S(1)} %pad_maximum_fusion.9.own_mod), channel_id=1, source_target_pairs={{0,1},{1,0},{2,3},{3,2},{4,5},{5,4},{6,7},{7,6},{8,9},{9,8},{10,11... | collective-permute-start | bytes 73736 | tf_op jit(solution)/shard_map/ppermute | solution.py:45
  95.3 6.5 %keys_values.1.refs_4_ = bf16[4,240,384]{2,1,0:T(8,128)(2,1)S(1)} custom-call(s32[4]{0:T(128)S(1)} %pad_add_fusion.1.pos_ref.refs_0_, bf16[2,240,3072]{2,1,0:T(8,128)(2,1)} %copy-done, f32[1,128]{1,0:T(1,128)S(1)} %broadcast_in_dim_tile.7.refs_2_, bf16[4,192,384]{2,1,0:T(8,128)(2,1)S(1)} %pad_maximum_fusion.3.refs_3_, ...), custom_call_target="tpu_custom_call" | custom-call | flops 2264924160 | bytes 7667712 | tf_op jit(solution)/shard_map/keys_values/pallas_call | solution.py:362
  102.2 3.4 %collective-permute-start.46 = (bf16[4,240,384]{2,1,0:T(8,128)(2,1)S(1)}, bf16[4,240,384]{2,1,0:T(8,128)(2,1)}, u32[]{:S(2)}, u32[]{:S(2)}) collective-permute-start(bf16[4,240,384]{2,1,0:T(8,128)(2,1)S(1)} %keys_values.1.refs_4_), channel_id=1, source_target_pairs={{0,120},{8,0},{16,8},{24,16},{32,24},{40,32},{48,40},{56,48},{64,5... | collective-permute-start | bytes 2211848 | tf_op jit(solution)/shard_map/ppermute | solution.py:50
  105.7 3.4 %collective-permute-start.26 = (bf16[4,192,384]{2,1,0:T(8,128)(2,1)S(1)}, bf16[4,192,384]{2,1,0:T(8,128)(2,1)S(1)}, u32[]{:S(2)}, u32[]{:S(2)}) collective-permute-start(bf16[4,192,384]{2,1,0:T(8,128)(2,1)S(1)} %pad_maximum_fusion.2.refs_0_), channel_id=1, source_target_pairs={{0,32},{8,40},{16,48},{24,56},{32,64},{40,72},{48,80},{56,88},{64,... | collective-permute-start | bytes 1769480 | tf_op jit(solution)/shard_map/ppermute | solution.py:27
  109.1 14.5 %collective-permute-done.2 = bf16[224,384]{1,0:T(8,128)(2,1)S(1)} collective-permute-done((bf16[224,384]{1,0:T(8,128)(2,1)S(1)}, bf16[224,384]{1,0:T(8,128)(2,1)S(1)}, u32[]{:S(2)}, u32[]{:S(2)}) %collective-permute-start.2) | collective-permute-done | bytes 172064 | tf_op jit(solution)/shard_map/ppermute | solution.py:27
  127.2 8.9 %collective-permute-start.47 = (bf16[4,240,384]{2,1,0:T(8,128)(2,1)}, bf16[4,240,384]{2,1,0:T(8,128)(2,1)}, u32[]{:S(2)}, u32[]{:S(2)}) collective-permute-start(bf16[4,240,384]{2,1,0:T(8,128)(2,1)} %collective-permute-done.46.refs_5_), channel_id=1, source_target_pairs={{0,120},{8,0},{16,8},{24,16},{32,24},{40,32},{48,40},{56,48},{64,5... | collective-permute-start | bytes 2211848 | tf_op jit(solution)/shard_map/ppermute | solution.py:50
  154.2 18.8 %collective-permute-done.29.refs_4_ = bf16[2,192,384]{2,1,0:T(8,128)(2,1)} collective-permute-done((bf16[2,192,384]{2,1,0:T(8,128)(2,1)}, bf16[2,192,384]{2,1,0:T(8,128)(2,1)}, u32[]{:S(2)}, u32[]{:S(2)}) %collective-permute-start.29) | collective-permute-done | bytes 294944 | tf_op jit(solution)/shard_map/ppermute | solution.py:27
  173.0 6.0 %queries.1.refs_1_ = bf16[2,240,384]{2,1,0:T(8,128)(2,1)S(1)} custom-call(s32[4]{0:T(128)S(1)} %pad_add_fusion.1.pos_ref.refs_0_, bf16[2,240,3072]{2,1,0:T(8,128)(2,1)S(1)} %copy-done.1, f32[1,128]{1,0:T(1,128)S(1)} %broadcast_in_dim_tile.6.gain_ref, bf16[4,192,384]{2,1,0:T(8,128)(2,1)S(1)} %pad_maximum_fusion.2.refs_0_, bf16[4,192,384]{2,1,0:T(8,128)(2,1)S(1)} %copy-done.9, ...), custom_call_target="tpu_custom_call" | custom-call | flops 1132462080 | bytes 5308416 | tf_op jit(solution)/shard_map/queries/pallas_call | solution.py:384
  179.1 20.0 %attention.1.refs_1_ = bf16[2,240,384]{2,1,0:T(8,128)(2,1)S(1)} custom-call(s32[4]{0:T(128)S(1)} %reshape.119.refs_0_, bf16[2,240,384]{2,1,0:T(8,128)(2,1)S(1)} %queries.1.refs_1_, bf16[4,240,384]{2,1,0:T(8,128)(2,1)} %collective-permute-done.45.refs_2_, bf16[4,240,384]{2,1,0:T(8,128)(2,1)} %collective-permute-done.44.refs_3_, ...), custom_call_target="tpu_custom_call" | custom-call | flops 6794772480 | bytes 6291456 | tf_op jit(solution)/shard_map/attention/pallas_call | solution.py:401
  199.1 4.2 %out_projection.1 = (bf16[4,2,225,384]{3,2,1,0:T(8,128)(2,1)S(1)}, bf16[4,2,225,384]{3,2,1,0:T(8,128)(2,1)S(1)}) custom-call(s32[4]{0:T(128)S(1)} %pad_add_fusion.1.pos_ref.refs_0_, bf16[2,240,384]{2,1,0:T(8,128)(2,1)S(1)} %attention.1.refs_1_, bf16[4,224,384]{2,1,0:T(8,128)(2,1)} %pad_maximum_fusion.1.refs_0_.refs_2_, ...), custom_call_target="tpu_custom_call" | custom-call | flops 1132462080 | bytes 5308416 | tf_op jit(solution)/shard_map/out_projection/pallas_call | solution.py:421
  203.9 9.3 %collective-permute-start.48 = (bf16[4,2,225,384]{3,0,2,1:T(4,128)(2,1)S(1)}, bf16[4,2,225,384]{3,0,2,1:T(4,128)(2,1)S(1)}, u32[]{:S(2)}, u32[]{:S(2)}) collective-permute-start(bf16[4,2,225,384]{3,0,2,1:T(4,128)(2,1)S(1)} %copy.21), channel_id=1, source_target_pairs={{0,1},{1,0},{2,3},{3,2},{4,5},{5,4},{6,7},{7,6},{8,9},{9,8},{10,11... | collective-permute-start | bytes 4147208 | tf_op jit(solution)/shard_map/ppermute | solution.py:45
  219.8 2.9 %collective-permute-start.51 = (bf16[2,225,384]{2,1,0:T(8,128)(2,1)}, bf16[2,225,384]{2,1,0:T(8,128)(2,1)S(1)}, u32[]{:S(2)}, u32[]{:S(2)}) collective-permute-start(bf16[2,225,384]{2,1,0:T(8,128)(2,1)} %get-tuple-element.10), channel_id=1, source_target_pairs={{0,6},{1,7},{2,0},{3,1},{4,2},{5,3},{6,4},{7,5},{8,14},{9,15},{10,... | collective-permute-start | bytes 1036808 | tf_op jit(solution)/shard_map/ppermute | solution.py:40
  225.2 12.7 %collective-permute-done.51 = bf16[2,225,384]{2,1,0:T(8,128)(2,1)S(1)} collective-permute-done((bf16[2,225,384]{2,1,0:T(8,128)(2,1)}, bf16[2,225,384]{2,1,0:T(8,128)(2,1)S(1)}, u32[]{:S(2)}, u32[]{:S(2)}) %collective-permute-start.51) | collective-permute-done | bytes 345632 | tf_op jit(solution)/shard_map/ppermute | solution.py:40
  237.9 4.4 %collective-permute-done.49 = bf16[2,225,384]{2,1,0:T(8,128)(2,1)} collective-permute-done((bf16[2,225,384]{2,1,0:T(8,128)(2,1)}, bf16[2,225,384]{2,1,0:T(8,128)(2,1)}, u32[]{:S(2)}, u32[]{:S(2)}) %collective-permute-start.49) | collective-permute-done | bytes 345632 | tf_op jit(solution)/shard_map/ppermute | solution.py:40
  (206 shorter events, 86.6 us)
Async XLA Ops:
  0.9 16.7 %collective-permute-start.15 = (bf16[32,768]{1,0:T(8,128)(2,1)S(1)}, bf16[32,768]{1,0:T(8,128)(2,1)S(1)}, u32[]{:S(2)}, u32[]{:S(2)}) collective-permute-start(bf16[32,768]{1,0:T(8,128)(2,1)S(1)} %bitcast.104), channel_id=1, source_target_pairs={{0,16},{8,24},{16,0},{24,8},{32,48},{40,56},{48,32},{56,40},{64,80... | collective-permute-start | bytes 147464 | tf_op jit(solution)/shard_map/ppermute | solution.py:27
  15.5 16.1 %collective-permute-start.10 = (bf16[2,225,384]{2,1,0:T(8,128)(2,1)S(1)}, bf16[2,225,384]{2,1,0:T(8,128)(2,1)S(1)}, u32[]{:S(2)}, u32[]{:S(2)}) collective-permute-start(bf16[2,225,384]{2,1,0:T(8,128)(2,1)S(1)} %get-tuple-element.23), channel_id=1, source_target_pairs={{0,6},{1,7},{2,0},{3,1},{4,2},{5,3},{6,4},{7,5},{8,14},{9,15},{10,... | collective-permute-start | bytes 1036808 | tf_op jit(solution)/shard_map/ppermute | solution.py:40
  15.9 16.8 %collective-permute-start.9 = (bf16[2,225,384]{2,1,0:T(8,128)(2,1)S(1)}, bf16[2,225,384]{2,1,0:T(8,128)(2,1)}, u32[]{:S(2)}, u32[]{:S(2)}) collective-permute-start(bf16[2,225,384]{2,1,0:T(8,128)(2,1)S(1)} %get-tuple-element.23), channel_id=1, source_target_pairs={{0,2},{1,3},{2,4},{3,5},{4,6},{5,7},{6,0},{7,1},{8,10},{9,11},{10,... | collective-permute-start | bytes 1036808 | tf_op jit(solution)/shard_map/ppermute | solution.py:40
  37.2 39.7 %collective-permute-start.12 = (bf16[4,2,225,384]{3,0,2,1:T(4,128)(2,1)S(1)}, bf16[4,2,225,384]{3,0,2,1:T(4,128)(2,1)S(1)}, u32[]{:S(2)}, u32[]{:S(2)}) collective-permute-start(bf16[4,2,225,384]{3,0,2,1:T(4,128)(2,1)S(1)} %copy.17), channel_id=1, source_target_pairs={{0,1},{1,0},{2,3},{3,2},{4,5},{5,4},{6,7},{7,6},{8,9},{9,8},{10,11... | collective-permute-start | bytes 4147208 | tf_op jit(solution)/shard_map/ppermute | solution.py:45
  51.0 15.6 %collective-permute-start.40 = (bf16[4,192,384]{2,1,0:T(8,128)(2,1)S(1)}, bf16[4,192,384]{2,1,0:T(8,128)(2,1)S(1)}, u32[]{:S(2)}, u32[]{:S(2)}) collective-permute-start(bf16[4,192,384]{2,1,0:T(8,128)(2,1)S(1)} %pad_maximum_fusion.4.refs_8_), channel_id=1, source_target_pairs={{0,8},{8,16},{16,24},{24,0},{32,40},{40,48},{48,56},{56,32},{64,72... | collective-permute-start | bytes 1769480 | tf_op jit(solution)/shard_map/ppermute | solution.py:27
  51.0 18.9 %collective-permute-start.41 = (bf16[4,192,384]{2,1,0:T(8,128)(2,1)S(1)}, bf16[4,192,384]{2,1,0:T(8,128)(2,1)S(1)}, u32[]{:S(2)}, u32[]{:S(2)}) collective-permute-start(bf16[4,192,384]{2,1,0:T(8,128)(2,1)S(1)} %pad_maximum_fusion.4.refs_8_), channel_id=1, source_target_pairs={{0,24},{8,0},{16,8},{24,16},{32,56},{40,32},{48,40},{56,48},{64,88... | collective-permute-start | bytes 1769480 | tf_op jit(solution)/shard_map/ppermute | solution.py:27
  69.9 20.3 %collective-permute-start.35 = (bf16[2,192,384]{2,1,0:T(8,128)(2,1)}, bf16[2,192,384]{2,1,0:T(8,128)(2,1)S(1)}, u32[]{:S(2)}, u32[]{:S(2)}) collective-permute-start(bf16[2,192,384]{2,1,0:T(8,128)(2,1)} %slice.136), channel_id=1, source_target_pairs={{0,32},{8,40},{16,48},{24,56},{32,64},{40,72},{48,80},{56,88},{64,... | collective-permute-start | bytes 884744 | tf_op jit(solution)/shard_map/ppermute | solution.py:27
  72.2 18.5 %collective-permute-start.36 = (bf16[2,192,384]{2,1,0:T(8,128)(2,1)}, bf16[2,192,384]{2,1,0:T(8,128)(2,1)}, u32[]{:S(2)}, u32[]{:S(2)}) collective-permute-start(bf16[2,192,384]{2,1,0:T(8,128)(2,1)} %slice.137), channel_id=1, source_target_pairs={{0,96},{8,104},{16,112},{24,120},{32,0},{40,8},{48,16},{56,24},{64... | collective-permute-start | bytes 884744 | tf_op jit(solution)/shard_map/ppermute | solution.py:27
  72.9 18.7 %collective-permute-start.42 = (bf16[2,192,384]{2,1,0:T(8,128)(2,1)}, bf16[2,192,384]{2,1,0:T(8,128)(2,1)}, u32[]{:S(2)}, u32[]{:S(2)}) collective-permute-start(bf16[2,192,384]{2,1,0:T(8,128)(2,1)} %slice.138), channel_id=1, source_target_pairs={{0,8},{8,16},{16,24},{24,0},{32,40},{40,48},{48,56},{56,32},{64,72... | collective-permute-start | bytes 884744 | tf_op jit(solution)/shard_map/ppermute | solution.py:27
  73.0 20.6 %collective-permute-start.43 = (bf16[2,192,384]{2,1,0:T(8,128)(2,1)}, bf16[2,192,384]{2,1,0:T(8,128)(2,1)}, u32[]{:S(2)}, u32[]{:S(2)}) collective-permute-start(bf16[2,192,384]{2,1,0:T(8,128)(2,1)} %slice.139), channel_id=1, source_target_pairs={{0,24},{8,0},{16,8},{24,16},{32,56},{40,32},{48,40},{56,48},{64,88... | collective-permute-start | bytes 884744 | tf_op jit(solution)/shard_map/ppermute | solution.py:27
  84.5 17.3 %collective-permute-start.25 = (bf16[192,384]{1,0:T(8,128)(2,1)S(1)}, bf16[192,384]{1,0:T(8,128)(2,1)S(1)}, u32[]{:S(2)}, u32[]{:S(2)}) collective-permute-start(bf16[192,384]{1,0:T(8,128)(2,1)S(1)} %copy-done.28), channel_id=1, source_target_pairs={{0,16},{8,24},{16,0},{24,8},{32,48},{40,56},{48,32},{56,40},{64,80... | collective-permute-start | bytes 442376 | tf_op jit(solution)/shard_map/ppermute | solution.py:27
  101.8 21.7 %collective-permute-start.2 = (bf16[224,384]{1,0:T(8,128)(2,1)S(1)}, bf16[224,384]{1,0:T(8,128)(2,1)S(1)}, u32[]{:S(2)}, u32[]{:S(2)}) collective-permute-start(bf16[224,384]{1,0:T(8,128)(2,1)S(1)} %copy-done.26), channel_id=1, source_target_pairs={{0,8},{8,16},{16,24},{24,0},{32,40},{40,48},{48,56},{56,32},{64,72... | collective-permute-start | bytes 516104 | tf_op jit(solution)/shard_map/ppermute | solution.py:27
  101.9 25.2 %collective-permute-start.44 = (bf16[4,240,384]{2,1,0:T(8,128)(2,1)S(1)}, bf16[4,240,384]{2,1,0:T(8,128)(2,1)}, u32[]{:S(2)}, u32[]{:S(2)}) collective-permute-start(bf16[4,240,384]{2,1,0:T(8,128)(2,1)S(1)} %keys_values.1.refs_4_), channel_id=1, source_target_pairs={{0,8},{8,16},{16,24},{24,32},{32,40},{40,48},{48,56},{56,64},{64,7... | collective-permute-start | bytes 2211848 | tf_op jit(solution)/shard_map/ppermute | solution.py:50
  102.2 24.9 %collective-permute-start.46 = (bf16[4,240,384]{2,1,0:T(8,128)(2,1)S(1)}, bf16[4,240,384]{2,1,0:T(8,128)(2,1)}, u32[]{:S(2)}, u32[]{:S(2)}) collective-permute-start(bf16[4,240,384]{2,1,0:T(8,128)(2,1)S(1)} %keys_values.1.refs_4_), channel_id=1, source_target_pairs={{0,120},{8,0},{16,8},{24,16},{32,24},{40,32},{48,40},{56,48},{64,5... | collective-permute-start | bytes 2211848 | tf_op jit(solution)/shard_map/ppermute | solution.py:50
  105.7 20.4 %collective-permute-start.26 = (bf16[4,192,384]{2,1,0:T(8,128)(2,1)S(1)}, bf16[4,192,384]{2,1,0:T(8,128)(2,1)S(1)}, u32[]{:S(2)}, u32[]{:S(2)}) collective-permute-start(bf16[4,192,384]{2,1,0:T(8,128)(2,1)S(1)} %pad_maximum_fusion.2.refs_0_), channel_id=1, source_target_pairs={{0,32},{8,40},{16,48},{24,56},{32,64},{40,72},{48,80},{56,88},{64,... | collective-permute-start | bytes 1769480 | tf_op jit(solution)/shard_map/ppermute | solution.py:27
  124.6 17.4 %collective-permute-start.5 = (bf16[4,224,384]{2,1,0:T(8,128)(2,1)}, bf16[4,224,384]{2,1,0:T(8,128)(2,1)}, u32[]{:S(2)}, u32[]{:S(2)}) collective-permute-start(bf16[4,224,384]{2,1,0:T(8,128)(2,1)} %pad_maximum_fusion.1.refs_0_.refs_2_), channel_id=1, source_target_pairs={{0,32},{8,40},{16,48},{24,56},{32,64},{40,72},{48,80},{56,88},{64,... | collective-permute-start | bytes 2064392 | tf_op jit(solution)/shard_map/ppermute | solution.py:27
  126.9 24.2 %collective-permute-start.6 = (bf16[4,224,384]{2,1,0:T(8,128)(2,1)}, bf16[4,224,384]{2,1,0:T(8,128)(2,1)}, u32[]{:S(2)}, u32[]{:S(2)}) collective-permute-start(bf16[4,224,384]{2,1,0:T(8,128)(2,1)} %pad_maximum_fusion.1.refs_0_.refs_2_), channel_id=1, source_target_pairs={{0,96},{8,104},{16,112},{24,120},{32,0},{40,8},{48,16},{56,24},{64... | collective-permute-start | bytes 2064392 | tf_op jit(solution)/shard_map/ppermute | solution.py:27
  127.1 51.9 %collective-permute-start.45 = (bf16[4,240,384]{2,1,0:T(8,128)(2,1)}, bf16[4,240,384]{2,1,0:T(8,128)(2,1)}, u32[]{:S(2)}, u32[]{:S(2)}) collective-permute-start(bf16[4,240,384]{2,1,0:T(8,128)(2,1)} %collective-permute-done.44.refs_3_), channel_id=1, source_target_pairs={{0,8},{8,16},{16,24},{24,32},{32,40},{40,48},{48,56},{56,64},{64,7... | collective-permute-start | bytes 2211848 | tf_op jit(solution)/shard_map/ppermute | solution.py:50
  127.2 51.9 %collective-permute-start.47 = (bf16[4,240,384]{2,1,0:T(8,128)(2,1)}, bf16[4,240,384]{2,1,0:T(8,128)(2,1)}, u32[]{:S(2)}, u32[]{:S(2)}) collective-permute-start(bf16[4,240,384]{2,1,0:T(8,128)(2,1)} %collective-permute-done.46.refs_5_), channel_id=1, source_target_pairs={{0,120},{8,0},{16,8},{24,16},{32,24},{40,32},{48,40},{56,48},{64,5... | collective-permute-start | bytes 2211848 | tf_op jit(solution)/shard_map/ppermute | solution.py:50
  142.0 31.0 %collective-permute-start.29 = (bf16[2,192,384]{2,1,0:T(8,128)(2,1)}, bf16[2,192,384]{2,1,0:T(8,128)(2,1)}, u32[]{:S(2)}, u32[]{:S(2)}) collective-permute-start(bf16[2,192,384]{2,1,0:T(8,128)(2,1)} %slice.135), channel_id=1, source_target_pairs={{0,96},{8,104},{16,112},{24,120},{32,0},{40,8},{48,16},{56,24},{64... | collective-permute-start | bytes 884744 | tf_op jit(solution)/shard_map/ppermute | solution.py:27
  151.1 48.0 %collective-permute-start.7 = (bf16[2,224,384]{2,1,0:T(8,128)(2,1)S(1)}, bf16[2,224,384]{2,1,0:T(8,128)(2,1)S(1)}, u32[]{:S(2)}, u32[]{:S(2)}) collective-permute-start(bf16[2,224,384]{2,1,0:T(8,128)(2,1)S(1)} %slice.132), channel_id=1, source_target_pairs={{0,32},{8,40},{16,48},{24,56},{32,64},{40,72},{48,80},{56,88},{64,... | collective-permute-start | bytes 1032200 | tf_op jit(solution)/shard_map/ppermute | solution.py:27
  152.9 46.2 %collective-permute-start.8 = (bf16[2,224,384]{2,1,0:T(8,128)(2,1)S(1)}, bf16[2,224,384]{2,1,0:T(8,128)(2,1)S(1)}, u32[]{:S(2)}, u32[]{:S(2)}) collective-permute-start(bf16[2,224,384]{2,1,0:T(8,128)(2,1)S(1)} %slice.133), channel_id=1, source_target_pairs={{0,96},{8,104},{16,112},{24,120},{32,0},{40,8},{48,16},{56,24},{64... | collective-permute-start | bytes 1032200 | tf_op jit(solution)/shard_map/ppermute | solution.py:27
  219.8 18.1 %collective-permute-start.51 = (bf16[2,225,384]{2,1,0:T(8,128)(2,1)}, bf16[2,225,384]{2,1,0:T(8,128)(2,1)S(1)}, u32[]{:S(2)}, u32[]{:S(2)}) collective-permute-start(bf16[2,225,384]{2,1,0:T(8,128)(2,1)} %get-tuple-element.10), channel_id=1, source_target_pairs={{0,6},{1,7},{2,0},{3,1},{4,2},{5,3},{6,4},{7,5},{8,14},{9,15},{10,... | collective-permute-start | bytes 1036808 | tf_op jit(solution)/shard_map/ppermute | solution.py:40
  222.9 19.3 %collective-permute-start.49 = (bf16[2,225,384]{2,1,0:T(8,128)(2,1)}, bf16[2,225,384]{2,1,0:T(8,128)(2,1)}, u32[]{:S(2)}, u32[]{:S(2)}) collective-permute-start(bf16[2,225,384]{2,1,0:T(8,128)(2,1)} %get-tuple-element.9), channel_id=1, source_target_pairs={{0,2},{1,3},{2,4},{3,5},{4,6},{5,7},{6,0},{7,1},{8,10},{9,11},{10,... | collective-permute-start | bytes 1036808 | tf_op jit(solution)/shard_map/ppermute | solution.py:40
  (61 other events, 764.0 us)

commit v2 on v0

v2 whole, which is shorter than its diff:
```python
import math

import jax
import jax.numpy as jnp
from jax import lax
from jax.experimental import pallas as pl
from jax.experimental.pallas import tpu as pltpu
from jax.sharding import PartitionSpec as P

HEAD = 64
D = 3072
TEMB = 512
REACH = 4
SIDE = 4
PADDED = 240
KEYS = 256
PAIR = 2 * HEAD
ORIGIN = (0, -1, 1, 2)


def torus_step(array, move):
    pairs = []
    for x in range(SIDE):
        for y in range(SIDE):
            for z in range(SIDE):
                for core in range(2):
                    to_x, to_y, to_z = (part % SIDE for part in move(x, y, z, core))
                    pairs.append((device_at(x, y, z, core), device_at(to_x, to_y, to_z, core)))
    return lax.ppermute(array, ("frame", "row"), pairs)


def device_at(x, y, z, core):
    return (x * SIDE + y) * 2 * SIDE + z * 2 + core


def first_step(array, by):
    return torus_step(array, lambda x, y, z, core: (x + by * core, y + by * (1 - core), z))


def second_step(array, by):
    return torus_step(array, lambda x, y, z, core: (x + by * (1 - core), y + by * core, z))


def z_step(array, by):
    return torus_step(array, lambda x, y, z, core: (x, y, z + by * (1 - 2 * core)))


def other_core(array):
    pairs = [(z * 2 + c, z * 2 + 1 - c) for z in range(SIDE) for c in range(2)]
    return lax.ppermute(array, "row", pairs)


def next_frame(array, by):
    peers = lax.axis_size("frame")
    return lax.ppermute(array, "frame", [(i, (i + by) % peers) for i in range(peers)])


def together(*values):
    return lax.optimization_barrier(values)


def level_waves(levels, place):
    half = TEMB // 2
    rows = TEMB // lax.axis_size("frame")
    entry = place * rows + jnp.arange(rows)
    freqs = jnp.exp(-math.log(10000.0) * (entry % half).astype(jnp.float32) / half)
    angles = levels.astype(jnp.float32)[:, None] * freqs[None, :]
    waves = jnp.where(entry[None, :] < half, jnp.cos(angles), jnp.sin(angles))
    return jax.nn.silu(waves).astype(jnp.bfloat16)


def spread(array, axis):
    copies = jnp.broadcast_to(array[None], (lax.axis_size(axis),) + array.shape)
    return lax.all_to_all(copies, axis, 0, 0, tiled=True)


def wrap(value, by):
    return lax.rem(value + by + SIDE, SIDE)


def shard_copies(places, inner_at, outer_at, inner_stride, outer_stride, target, sems):
    copies = []
    for outer in range(SIDE):
        for inner in range(SIDE):
            owner = wrap(outer_at, ORIGIN[outer]) * outer_stride + wrap(inner_at, ORIGIN[inner]) * inner_stride
            copies.append(
                pltpu.make_async_copy(places[outer][inner], target.at[owner], sems.at[len(copies)])
            )
    return copies


def head_norm_pair(values, gain_ref):
    low = lax.broadcasted_iota(jnp.int32, values.shape, 1) < HEAD

    def mean_of(array):
        first = jnp.sum(jnp.where(low, array, 0.0), axis=1, keepdims=True)
        second = jnp.sum(jnp.where(low, 0.0, array), axis=1, keepdims=True)
        return jnp.where(low, first, second) * (1.0 / HEAD)

    gain = jnp.concatenate([gain_ref[...], gain_ref[...]], axis=1)
    centered = values - mean_of(values)
    spread = mean_of(centered * centered)
    return (centered * lax.rsqrt(spread + 1e-06) * gain).astype(jnp.bfloat16)


def modulate(pos_ref, mod_ref, own_refs, other_refs, out_ref):
    tokens = own_refs[0].shape[1]
    width = own_refs[0].shape[2]
    z = pos_ref[4]
    core = pos_ref[5]
    way = pos_ref[6]
    for slot in range(2):
        total = jnp.zeros((tokens, width), jnp.float32)
        square = jnp.zeros((tokens, width), jnp.float32)
        for ref in (*own_refs, *other_refs):
            part = ref[slot].astype(jnp.float32)
            total += part
            square += part * part
        mean = jnp.sum(total, axis=1, keepdims=True) * (1.0 / D)
        meansq = jnp.sum(square, axis=1, keepdims=True) * (1.0 / D)
        inverse = lax.rsqrt(meansq - mean * mean + 1e-05)
        for refs_of, at_core, along in ((own_refs, core, way), (other_refs, 1 - core, -way)):
            for hop in range(SIDE):
                part = refs_of[hop][slot].astype(jnp.float32)
                normed = (part - mean) * inverse
                owner = wrap(z, ORIGIN[hop] * along) * 2 + at_core
                shift = mod_ref[owner, slot : slot + 1, 0:width]
                scale = mod_ref[owner, slot : slot + 1, width : 2 * width]
                columns = pl.ds(pl.multiple_of(owner * width, width), width)
                out_ref[slot, 0:tokens, columns] = (normed * (1.0 + scale) + shift).astype(jnp.bfloat16)
        out_ref[slot, tokens:, :] = jnp.zeros((PADDED - tokens, D), jnp.bfloat16)


def project_kernel(pos_ref, mod_ref, q_gain_ref, k_gain_ref, *refs):
    states, shards, (q_ref, k_ref, v_ref, modulated, weight, sems) = refs[:8], refs[8:24], refs[24:]
    places = [
        [shards[SIDE * outer + inner].at[pl.ds(0, 576)] for inner in range(SIDE)] for outer in range(SIDE)
    ]
    copies = shard_copies(places, pos_ref[0], pos_ref[1], pos_ref[2], pos_ref[3], weight, sems)
    for copy in copies:
        copy.start()
    modulate(pos_ref, mod_ref, states[:SIDE], states[SIDE:], modulated)
    for copy in copies:
        copy.wait()
    x = modulated[...].reshape(2 * PADDED, D)
    for part, target in enumerate((k_ref, v_ref, q_ref)):
        whole = jnp.dot(
            x,
            weight[:, part * 192 : part * 192 + 192, :].reshape(D, 384),
            preferred_element_type=jnp.float32,
        )
        for pair in range(3):
            columns = slice(pair * PAIR, (pair + 1) * PAIR)
            piece = whole[:, columns]
            if part == 0:
                piece = head_norm_pair(piece, k_gain_ref)
            elif part == 1:
                piece = piece.astype(jnp.bfloat16)
            else:
                piece = head_norm_pair(piece, q_gain_ref) * jnp.asarray(1.0 / math.sqrt(HEAD), jnp.bfloat16)
            for slot in range(2):
                target[slot, :, columns] = piece[slot * PADDED : (slot + 1) * PADDED]


def fill_window(pairs, keys, values):
    for index, (key_ref, value_ref) in enumerate(pairs):
        for half in range(2):
            slot = 2 * index + half
            keys[slot, 0:PADDED, :] = key_ref[half]
            keys[slot, PADDED:, :] = jnp.zeros((KEYS - PADDED, PAIR), jnp.bfloat16)
            values[slot, 0:PADDED, 0:PAIR] = value_ref[half]
            values[slot, PADDED:, 0:PAIR] = jnp.zeros((KEYS - PADDED, PAIR), jnp.bfloat16)
            values[slot, :, PAIR:] = jnp.ones((KEYS, PAIR), jnp.bfloat16)


def seen_bias(plan_ref, pos_ref, slot, window, tokens):
    first = 2 * pos_ref[9] + 1
    at = lax.rem(first + slot, plan_ref.shape[0])
    lowest = jnp.maximum(slot - plan_ref[at, 1], -first)
    highest = jnp.minimum(slot + plan_ref[at, 2], plan_ref.shape[0] - 1 - first)
    column = lax.broadcasted_iota(jnp.int32, (1, KEYS), 1)
    parts = []
    for relative in window:
        known = jnp.logical_and(relative >= lowest, relative <= highest)
        count = jnp.where(known, tokens, 0)
        parts.append(jnp.where(column < count, 0.0, -jnp.inf))
    return jnp.concatenate(parts, axis=1)


def near_kernel(tokens, plan_ref, pos_ref, q_ref, km, vm, ko, vo, kp, vp, mix_ref, total_ref, top_ref, keys, values):
    fill_window(((km, vm), (ko, vo), (kp, vp)), keys, values)
    low = lax.broadcasted_iota(jnp.int32, (PADDED, PAIR), 1) < HEAD
    key_win = keys[...].reshape(6 * KEYS, PAIR)
    value_win = values[...].reshape(6 * KEYS, 2 * PAIR)
    for slot in range(2):
        query = q_ref[slot]
        bias = seen_bias(plan_ref, pos_ref, slot, range(-2, 4), tokens)
        nothing = jnp.zeros_like(query)
        mixes = []
        peaks = []
        for one in (jnp.where(low, query, nothing), jnp.where(low, nothing, query)):
            scores = lax.dot_general(
                one, key_win, (((1,), (1,)), ((), ())), preferred_element_type=jnp.float32
            )
            scores = scores + bias
            peak = jnp.max(scores, axis=1, keepdims=True)
            expo = jnp.exp(scores - peak).astype(jnp.bfloat16)
            mixes.append(jnp.dot(expo, value_win, preferred_element_type=jnp.float32))
            peaks.append(jnp.broadcast_to(peak, (PADDED, PAIR)))
        mix_ref[slot] = jnp.where(low, mixes[0][:, :PAIR], mixes[1][:, :PAIR])
        total_ref[slot] = jnp.where(low, mixes[0][:, PAIR:], mixes[1][:, PAIR:])
        top_ref[slot] = jnp.where(low, peaks[0], peaks[1])


def far_kernel(tokens, plan_ref, pos_ref, q_ref, km, vm, kp, vp, mix_ref, total_ref, top_ref, out_ref, keys, values):
    fill_window(((km, vm), (kp, vp)), keys, values)
    low = lax.broadcasted_iota(jnp.int32, (PADDED, PAIR), 1) < HEAD
    window = (-4, -3, 4, 5)
    for slot in range(2):
        query = q_ref[slot]
        bias = seen_bias(plan_ref, pos_ref, slot, window[slot : slot + 3], tokens)
        nothing = jnp.zeros_like(query)
        key_win = keys[slot : slot + 3].reshape(3 * KEYS, PAIR)
        value_win = values[slot : slot + 3].reshape(3 * KEYS, 2 * PAIR)
        near_top = top_ref[slot]
        mixes = []
        peaks = []
        for head, one in enumerate((jnp.where(low, query, nothing), jnp.where(low, nothing, query))):
            scores = lax.dot_general(
                one, key_win, (((1,), (1,)), ((), ())), preferred_element_type=jnp.float32
            )
            scores = scores + bias
            peak = jnp.maximum(
                jnp.max(scores, axis=1, keepdims=True), near_top[:, head * HEAD : head * HEAD + 1]
            )
            expo = jnp.exp(scores - peak).astype(jnp.bfloat16)
            mixes.append(jnp.dot(expo, value_win, preferred_element_type=jnp.float32))
            peaks.append(jnp.broadcast_to(peak, (PADDED, PAIR)))
        fade = jnp.exp(near_top - jnp.where(low, peaks[0], peaks[1]))
        mix = jnp.where(low, mixes[0][:, :PAIR], mixes[1][:, :PAIR]) + mix_ref[slot] * fade
        total = jnp.where(low, mixes[0][:, PAIR:], mixes[1][:, PAIR:]) + total_ref[slot] * fade
        out_ref[slot] = (mix / total).astype(jnp.bfloat16)


def out_kernel(tokens, pos_ref, x_ref, *refs):
    shards, (keep_ref, send_ref, weight, sems) = refs[:16], refs[16:]
    places = [
        [shards[SIDE * outer + inner].at[pl.ds(576, 192)] for inner in range(SIDE)] for outer in range(SIDE)
    ]
    copies = shard_copies(places, pos_ref[0], pos_ref[1], pos_ref[2], pos_ref[3], weight, sems)
    for copy in copies:
        copy.start()
    for copy in copies:
        copy.wait()
    x = x_ref[...].reshape(2 * PADDED, 384)
    z = pos_ref[4]
    core = pos_ref[5]
    way = pos_ref[6]
    for ref, at_core, along in ((send_ref, 1 - core, -way), (keep_ref, core, way)):
        for hop in range(SIDE):
            owner = wrap(z, hop * along) * 2 + at_core
            rows = weight[pl.ds(owner * 2, 2)].reshape(384, 384)
            part = lax.dot_general(
                x, rows, (((1,), (1,)), ((), ())), preferred_element_type=jnp.float32
            ).astype(jnp.bfloat16)
            for slot in range(2):
                ref[2 * hop + slot] = part[slot * PADDED : slot * PADDED + tokens]


SMEM = pl.BlockSpec(memory_space=pltpu.SMEM)
VMEM = pl.BlockSpec(memory_space=pltpu.VMEM)
ANY = pl.BlockSpec(memory_space=pl.ANY)


def call(kernel, out_shape, in_specs, scratch, name, flops, moved, vmem=48):
    out_specs = [VMEM] * len(out_shape) if isinstance(out_shape, list) else VMEM
    return pl.pallas_call(
        kernel,
        out_shape=out_shape,
        in_specs=in_specs,
        out_specs=out_specs,
        scratch_shapes=scratch,
        name=name,
        compiler_params=pltpu.CompilerParams(vmem_limit_bytes=vmem << 20),
        cost_estimate=pl.CostEstimate(flops=flops, bytes_accessed=moved, transcendentals=0),
    )


def struct(shape, dtype=jnp.bfloat16):
    return jax.ShapeDtypeStruct(shape, dtype)


def per_device(
    hidden_states,
    timestep_index,
    window_offsets,
    mod_weight,
    qkv_weight,
    query_gain,
    key_gain,
    out_weight,
    fresh_frame,
):
    tokens = hidden_states.shape[1]
    width = hidden_states.shape[2]
    place = lax.axis_index("frame")
    row = lax.axis_index("row")
    slots = 2 * lax.axis_size("frame")
    first_slot = 2 * place + 1
    x, y, z, core = place // SIDE, place % SIDE, row // 2, row % 2
    pos = jnp.where(core == 0, jnp.stack([y, x, 1, SIDE]), jnp.stack([x, y, SIDE, 1]))
    pos = jnp.concatenate([pos, jnp.stack([z, core, 1 - 2 * core, x, y, place])]).astype(jnp.int32)

    shard = jnp.concatenate(
        [qkv_weight[:, 1], qkv_weight[:, 2], qkv_weight[:, 0], out_weight.T], axis=0
    )

    plan = jnp.concatenate([timestep_index[:, None], window_offsets], axis=1)
    below = first_step(shard, 1)
    above = first_step(shard, -1)
    head = next_frame(hidden_states[0], -1)
    plan = spread(plan, "frame").reshape(slots, 3)
    shard, plan = together(shard, plan)
    own_b = second_step(shard, 1)
    own_a = second_step(shard, -1)
    waves = level_waves(jnp.roll(plan[:, 0], -1), place)
    sums = jnp.dot(waves, mod_weight.reshape(-1, 3 * width), preferred_element_type=jnp.float32)
    states = jnp.stack([hidden_states[1], head])
    sums = lax.all_to_all(sums.reshape(slots // 2, 2, 3 * width), "frame", 0, 0, tiled=True)
    below, above, states, sums = together(below, above, states, sums)
    far = first_step(below, 1)
    below_b = second_step(below, 1)
    below_a = second_step(below, -1)
    above_b = second_step(above, 1)
    above_a = second_step(above, -1)
    z_b = z_step(states, 1)
    z_a = z_step(states, -1)
    far, z_b, z_a = together(far, z_b, z_a)
    far_b = second_step(far, 1)
    far_a = second_step(far, -1)
    own_f = second_step(own_b, 1)
    z_f = z_step(z_b, 1)
    below_f = second_step(below_b, 1)
    above_f = second_step(above_a, -1)
    far_f = second_step(far_a, -1)
    own_states = [states, z_b, z_a, z_f]
    other_states = [other_core(part) for part in own_states]
    mods = jnp.sum(sums, axis=0)
    all_mods = spread(mods, "row")
    shards = [
        shard, below, above, far,
        own_b, below_b, above_b, far_b,
        own_a, below_a, above_a, far_a,
        own_f, below_f, above_f, far_f,
    ]
    queries, keys, values = call(
        project_kernel,
        [struct((2, PADDED, width))] * 3,
        [SMEM] + [VMEM] * 11 + [ANY] * len(shards),
        [
            pltpu.VMEM((2, PADDED, D), jnp.bfloat16),
            pltpu.VMEM((16, 3 * 192, width), jnp.bfloat16),
            pltpu.SemaphoreType.DMA((16,)),
        ],
        "projections",
        4 * PADDED * D * 3 * width,
        D * width * 6 + PADDED * D * 4,
        vmem=60,
    )(pos, all_mods, query_gain[None], key_gain[None], *own_states, *other_states, *shards)

    near = [next_frame(part, by) for part in (keys, values) for by in (1, -1)]
    far_kv = [next_frame(part, by) for part, by in zip(near, (1, -1, 1, -1))]

    block = pl.BlockSpec((2, PADDED, PAIR), lambda pair: (0, 0, pair))
    params = pltpu.CompilerParams(vmem_limit_bytes=48 << 20)
    mix, total, top = pl.pallas_call(
        lambda *refs: near_kernel(tokens, *refs),
        out_shape=[struct((2, PADDED, width), jnp.float32)] * 3,
        grid=(3,),
        in_specs=[SMEM, SMEM] + [block] * 7,
        out_specs=[block] * 3,
        scratch_shapes=[
            pltpu.VMEM((6, KEYS, PAIR), jnp.bfloat16),
            pltpu.VMEM((6, KEYS, 2 * PAIR), jnp.bfloat16),
        ],
        name="attention_near",
        compiler_params=params,
        cost_estimate=pl.CostEstimate(
            flops=6 * 6 * 4 * 480 * 256 * 256, bytes_accessed=6 << 20, transcendentals=36 * 480 * 256
        ),
    )(plan, pos, queries, near[0], near[2], keys, values, near[1], near[3])
    mixed = pl.pallas_call(
        lambda *refs: far_kernel(tokens, *refs),
        out_shape=struct((2, PADDED, width)),
        grid=(3,),
        in_specs=[SMEM, SMEM] + [block] * 8,
        out_specs=block,
        scratch_shapes=[
            pltpu.VMEM((4, KEYS, PAIR), jnp.bfloat16),
            pltpu.VMEM((4, KEYS, 2 * PAIR), jnp.bfloat16),
        ],
        name="attention_far",
        compiler_params=params,
        cost_estimate=pl.CostEstimate(
            flops=6 * 3 * 4 * 480 * 256 * 256, bytes_accessed=6 << 20, transcendentals=18 * 480 * 256
        ),
    )(plan, pos, queries, far_kv[0], far_kv[2], far_kv[1], far_kv[3], mix, total, top)
    keep, send = call(
        lambda *refs: out_kernel(tokens, *refs),
        [struct((2 * SIDE, tokens, width))] * 2,
        [SMEM, VMEM] + [ANY] * len(shards),
        [pltpu.VMEM((16, 192, width), jnp.bfloat16), pltpu.SemaphoreType.DMA((16,))],
        "out_projection",
        4 * PADDED * D * width,
        D * width * 2 + PADDED * D * 4,
    )(pos, mixed, *shards)

    swapped = other_core(send)
    chip = [
        keep[2 * hop : 2 * hop + 2].astype(jnp.float32) + swapped[2 * hop : 2 * hop + 2].astype(jnp.float32)
        for hop in range(SIDE)
    ]
    onward = z_step(chip[2].astype(jnp.bfloat16), 1)
    back = z_step(chip[3].astype(jnp.bfloat16), -1)
    forth = z_step((chip[1] + onward.astype(jnp.float32)).astype(jnp.bfloat16), 1)
    attended = chip[0] + back.astype(jnp.float32) + forth.astype(jnp.float32)
    gate = mods[:, None, 2 * width :]
    updated = (states.astype(jnp.float32) + gate * attended).astype(jnp.bfloat16)
    spare = (first_slot + jnp.arange(2) == slots)[:, None, None]
    return jnp.where(spare, fresh_frame[None], updated)


def solution(mesh):
    return jax.shard_map(
        per_device,
        mesh=mesh,
        in_specs=(
            P("frame", None, "row"),
            P("frame"),
            P("frame", None),
            P("frame", None, "row"),
            P("frame", None, "row"),
            P(),
            P(),
            P("row", "frame"),
            P(None, "row"),
        ),
        out_specs=P("frame", None, "row"),
        check_vma=False,
    )
```

time: 338 us -> 186 us (0.55); the launches traced: 333 us -> 185 us
  waiting for transfers between devices: 172 us -> 65 us
  local copies, waits for them, and re-layouts: 62.2 us -> 14.2 us
  starting transfers between devices: 16.3 us -> 63.9 us
  matrix products: 35.4 us -> 0.28 us
  Pallas kernels: 0 us -> 34.7 us
  blocking collectives: 15.9 us -> 0 us
  between operations: 13.5 us -> 0.49 us
  other arithmetic: 18.1 us -> 6.86 us
    all_gather x4 -> x0, waiting for transfers between devices: 110 us -> none  [the longest x1 63.5 us: per_device(): lax.all_gather(qkv_weight, 'frame', axis=0, tiled=True)]
    unnamed x6 -> x0, waiting for transfers between devices: 45 us -> none
    ppermute x5 -> x35, waiting for transfers between devices: 16.8 us -> 55.6 us  [the longest x21 36.3 us: torus_step(): return lax.ppermute(array, ('frame', 'row'), pairs)]
    dot_general x5 -> x1, matrix products: 35.4 us -> 0.28 us  [per_device(): jnp.dot(waves, mod_weight.reshape(-1, 3 * width), preferred_element_type=...]
    pallas_call x0 -> x4, Pallas kernels: none -> 34.7 us  [the longest x1 13.4 us: per_device(): call(project_kernel, [struct((2, PADDED, width))] * 3, [SMEM] + [VMEM] *...]
    ppermute x5 -> x35, starting transfers between devices: 16.1 us -> 44 us  [the longest x21 27 us: torus_step(): return lax.ppermute(array, ('frame', 'row'), pairs)]
    all_to_all x0 -> x3, starting transfers between devices: none -> 19.9 us  [the longest x2 11.2 us: spread(): return lax.all_to_all(copies, axis, 0, 0, tiled=True)]
    psum x1 -> x0, blocking collectives: 15.9 us -> none  [per_device(): lax.psum((jnp.sum(states, axis=2), jnp.sum(states * states, axis=2)), 'row')]
  transfers between devices with their start and end apart: 10 -> 38, of which waited for: 6 -> 17; matrix products, arithmetic and copies ran while one was open for 29% -> 6% of each run, Pallas kernels for 0% -> 5%
where the time goes in v2:
time: 186 us; the launch traced here: 185 us
  waiting for transfers between devices  65 us (35%)
  starting transfers between devices  63.9 us (34%)
  Pallas kernels  34.7 us (19%)
  local copies, waits for them, and re-layouts  14.2 us (8%)
  other arithmetic  6.86 us (4%)
    ppermute x21, waiting for transfers between devices, torus_step(): return lax.ppermute(array, ('frame', 'row'), pairs)  36.3 us
    ppermute x21, starting transfers between devices, torus_step(): return lax.ppermute(array, ('frame', 'row'), pairs)  27 us
    ppermute x9, starting transfers between devices, next_frame(): lax.ppermute(array, 'frame', [(i, (i + by) % peers) for i in range(peers)])  16.5 us
    ppermute x9, waiting for transfers between devices, next_frame(): lax.ppermute(array, 'frame', [(i, (i + by) % peers) for i in range(peers)])  16.2 us
    pallas_call x1, Pallas kernels, per_device(): call(project_kernel, [struct((2, PADDED, width))] * 3, [SMEM] + [VMEM] *...  13.4 us
    all_to_all x2, starting transfers between devices, spread(): return lax.all_to_all(copies, axis, 0, 0, tiled=True)  11.2 us
    all_to_all x1, starting transfers between devices, per_device(): lax.all_to_all(sums.reshape(slots // 2, 2, 3 * width), 'frame', 0, 0, til...  8.69 us
    pallas_call x1, Pallas kernels, per_device(): pl.pallas_call(lambda *refs: near_kernel(tokens, *refs), out_shape=[struc...  8.62 us
  transfers between devices with their start and end apart: 38, of which 17 were waited for; matrix products, arithmetic and copies ran while one was open for 6% of the time, Pallas kernels for 5%

profile of v2, /device:TPU:30, one launch (start us, length us, event | category | flops | bytes accessed | tf_op | source)
XLA Modules:
  0.0 185.4 jit_solution(7133933100550011303)
XLA Ops:
  5.1 7.1 %all-to-all-start = ((s32[16,2,3]{2,1,0:T(2,128)}), s32[16,2,3]{2,1,0:T(2,128)S(1)}, u32[]{:S(2)}, u32[]{:S(2)}) async-start(s32[16,2,3]{2,1,0:T(2,128)} %broadcast_in_dim.55), calls=%async_computation | async-start | bytes 32768 | tf_op jit(solution)/shard_map/all_to_all | solution.py:74
  21.2 8.7 %all-to-all-start.1 = ((f32[16,2,1152]{2,1,0:T(2,128)}), f32[16,2,1152]{2,1,0:T(2,128)}, u32[]{:S(2)}, u32[]{:S(2)}) async-start(f32[16,2,1152]{2,1,0:T(2,128)} %copy.33), calls=%async_computation.1 | async-start | bytes 294912 | tf_op jit(solution)/shard_map/all_to_all | solution.py:329
  31.6 2.6 %all-to-all-done.1 = f32[16,2,1152]{2,1,0:T(2,128)} async-done(((f32[16,2,1152]{2,1,0:T(2,128)}), f32[16,2,1152]{2,1,0:T(2,128)}, u32[]{:S(2)}, u32[]{:S(2)}) %all-to-all-start.1) | async-done | bytes 147488 | tf_op jit(solution)/shard_map/all_to_all | solution.py:329
  42.7 3.4 %collective-permute-done.4.refs_1_ = bf16[2,225,384]{2,1,0:T(8,128)(2,1)S(1)} collective-permute-done((bf16[2,225,384]{2,1,0:T(8,128)(2,1)}, bf16[2,225,384]{2,1,0:T(8,128)(2,1)S(1)}, u32[]{:S(2)}, u32[]{:S(2)}) %collective-permute-start.4) | collective-permute-done | bytes 345632 | tf_op jit(solution)/shard_map/ppermute | solution.py:29
  50.1 4.6 %collective-permute-done.3.refs_11_.refs_5_ = bf16[768,384]{1,0:T(8,128)(2,1)S(1)} collective-permute-done((bf16[768,384]{1,0:T(8,128)(2,1)S(1)}, bf16[768,384]{1,0:T(8,128)(2,1)S(1)}, u32[]{:S(2)}, u32[]{:S(2)}) %collective-permute-start.3) | collective-permute-done | bytes 589856 | tf_op jit(solution)/shard_map/ppermute | solution.py:29
  57.3 6.2 %collective-permute-done.16.refs_17_.refs_11_ = bf16[768,384]{1,0:T(8,128)(2,1)S(1)} collective-permute-done((bf16[768,384]{1,0:T(8,128)(2,1)S(1)}, bf16[768,384]{1,0:T(8,128)(2,1)S(1)}, u32[]{:S(2)}, u32[]{:S(2)}) %collective-permute-start.16) | collective-permute-done | bytes 589856 | tf_op jit(solution)/shard_map/ppermute | solution.py:29
  64.5 2.9 %collective-permute-start.14 = (bf16[768,384]{1,0:T(8,128)(2,1)S(1)}, bf16[768,384]{1,0:T(8,128)(2,1)}, u32[]{:S(2)}, u32[]{:S(2)}) collective-permute-start(bf16[768,384]{1,0:T(8,128)(2,1)S(1)} %collective-permute-done.3.refs_11_.refs_5_), channel_id=1, source_target_pairs={{0,32},{1,9},{2,34},{3,11},{4,36},{5,13},{6,38},{7,15},{8,40},{9,1... | collective-permute-start | bytes 1769480 | tf_op jit(solution)/shard_map/ppermute | solution.py:29
  72.3 4.2 %all-to-all-start.2 = ((f32[8,2,1152]{2,1,0:T(2,128)}), f32[8,2,1152]{2,1,0:T(2,128)}, u32[]{:S(2)}, u32[]{:S(2)}) async-start(f32[8,2,1152]{2,1,0:T(2,128)} %broadcast_in_dim.56), calls=%async_computation.2 | async-start | bytes 147456 | tf_op jit(solution)/shard_map/all_to_all | solution.py:74
  77.2 4.7 %all-to-all-done.2.mod_ref = f32[8,2,1152]{2,1,0:T(2,128)} async-done(((f32[8,2,1152]{2,1,0:T(2,128)}), f32[8,2,1152]{2,1,0:T(2,128)}, u32[]{:S(2)}, u32[]{:S(2)}) %all-to-all-start.2) | async-done | bytes 73760 | tf_op jit(solution)/shard_map/all_to_all | solution.py:74
  82.0 3.3 %collective-permute-done.22.refs_23_.refs_17_ = bf16[768,384]{1,0:T(8,128)(2,1)} collective-permute-done((bf16[768,384]{1,0:T(8,128)(2,1)}, bf16[768,384]{1,0:T(8,128)(2,1)}, u32[]{:S(2)}, u32[]{:S(2)}) %collective-permute-start.22) | collective-permute-done | bytes 589856 | tf_op jit(solution)/shard_map/ppermute | solution.py:29
  85.4 13.4 %projections.1 = (bf16[2,240,384]{2,1,0:T(8,128)(2,1)}, bf16[2,240,384]{2,1,0:T(8,128)(2,1)}, bf16[2,240,384]{2,1,0:T(8,128)(2,1)}) custom-call(s32[10]{0:T(128)} %concatenate.19.pos_ref.refs_1_.refs_0_, f32[8,2,1152]{2,1,0:T(2,128)} %all-to-all-done.2.mod_ref, f32[1,64]{1,0:T(1,128)} %bitcast.25, f32[1,64]{1,0:T(1,128)} %bitcast.26, ...), custom_call_target="tpu_custom_call" | custom-call | flops 3397386240 | bytes 10027008 | tf_op jit(solution)/shard_map/projections/pallas_call | solution.py:356
  103.8 6.7 %collective-permute-done.23.refs_3_ = bf16[2,240,384]{2,1,0:T(8,128)(2,1)S(1)} collective-permute-done((bf16[2,240,384]{2,1,0:T(8,128)(2,1)}, bf16[2,240,384]{2,1,0:T(8,128)(2,1)S(1)}, u32[]{:S(2)}, u32[]{:S(2)}) %collective-permute-start.23) | collective-permute-done | bytes 368672 | tf_op jit(solution)/shard_map/ppermute | solution.py:55
  110.6 5.5 %collective-permute-start.24 = (bf16[2,240,384]{2,1,0:T(8,128)(2,1)S(1)}, bf16[2,240,384]{2,1,0:T(8,128)(2,1)S(1)}, u32[]{:S(2)}, u32[]{:S(2)}) collective-permute-start(bf16[2,240,384]{2,1,0:T(8,128)(2,1)S(1)} %collective-permute-done.23.refs_3_), channel_id=1, source_target_pairs={{0,8},{8,16},{16,24},{24,32},{32,40},{40,48},{48,56},{56,64},{64,7... | collective-permute-start | bytes 1105928 | tf_op jit(solution)/shard_map/ppermute | solution.py:55
  116.1 2.4 %collective-permute-done.25.refs_4_ = bf16[2,240,384]{2,1,0:T(8,128)(2,1)S(1)} collective-permute-done((bf16[2,240,384]{2,1,0:T(8,128)(2,1)}, bf16[2,240,384]{2,1,0:T(8,128)(2,1)S(1)}, u32[]{:S(2)}, u32[]{:S(2)}) %collective-permute-start.25) | collective-permute-done | bytes 368672 | tf_op jit(solution)/shard_map/ppermute | solution.py:55
  118.5 5.5 %collective-permute-start.26 = (bf16[2,240,384]{2,1,0:T(8,128)(2,1)S(1)}, bf16[2,240,384]{2,1,0:T(8,128)(2,1)S(1)}, u32[]{:S(2)}, u32[]{:S(2)}) collective-permute-start(bf16[2,240,384]{2,1,0:T(8,128)(2,1)S(1)} %collective-permute-done.25.refs_4_), channel_id=1, source_target_pairs={{0,8},{8,16},{16,24},{24,32},{32,40},{40,48},{48,56},{56,64},{64,7... | collective-permute-start | bytes 1105928 | tf_op jit(solution)/shard_map/ppermute | solution.py:55
  127.2 8.6 %attention_near.1 = (f32[2,240,384]{2,1,0:T(8,128)S(1)}, f32[2,240,384]{2,1,0:T(8,128)S(1)}, f32[2,240,384]{2,1,0:T(8,128)S(1)}) custom-call(s32[32,3]{1,0:T(8,128)S(1)} %copy.35.refs_0_, s32[10]{0:T(128)S(1)} %copy-done.14, bf16[2,240,384]{2,1,0:T(8,128)(2,1)S(1)} %copy-done.17, bf16[2,240,384]{2,1,0:T(8,128)(2,1)S(1)} %collective-permute-done.23.refs_3_, ...), custom_call_target="tpu_custom_call" | custom-call | flops 4529848320 | bytes 6291456 | tf_op jit(solution)/shard_map/attention_near/pallas_call | solution.py:376
  135.9 2.9 %collective-permute-done.28.refs_5_ = bf16[2,240,384]{2,1,0:T(8,128)(2,1)S(1)} collective-permute-done((bf16[2,240,384]{2,1,0:T(8,128)(2,1)S(1)}, bf16[2,240,384]{2,1,0:T(8,128)(2,1)S(1)}, u32[]{:S(2)}, u32[]{:S(2)}) %collective-permute-start.28) | collective-permute-done | bytes 368672 | tf_op jit(solution)/shard_map/ppermute | solution.py:55
  138.8 4.1 %collective-permute-done.30.refs_6_ = bf16[2,240,384]{2,1,0:T(8,128)(2,1)S(1)} collective-permute-done((bf16[2,240,384]{2,1,0:T(8,128)(2,1)S(1)}, bf16[2,240,384]{2,1,0:T(8,128)(2,1)S(1)}, u32[]{:S(2)}, u32[]{:S(2)}) %collective-permute-start.30) | collective-permute-done | bytes 368672 | tf_op jit(solution)/shard_map/ppermute | solution.py:55
  143.0 5.9 %attention_far.1.refs_1_ = bf16[2,240,384]{2,1,0:T(8,128)(2,1)S(1)} custom-call(s32[32,3]{1,0:T(8,128)S(1)} %copy.35.refs_0_, s32[10]{0:T(128)S(1)} %copy-done.14, bf16[2,240,384]{2,1,0:T(8,128)(2,1)S(1)} %copy-done.17, bf16[2,240,384]{2,1,0:T(8,128)(2,1)S(1)} %collective-permute-done.24.refs_3_, bf16[2,240,384]{2,1,0:T(8,128)(2,1)S(1)} %collective-permute-done.26.refs_4_, ...), custom_call_target="tpu_custom_call" | custom-call | flops 2264924160 | bytes 6291456 | tf_op jit(solution)/shard_map/attention_far/pallas_call | solution.py:392
  149.0 6.8 %out_projection.1 = (bf16[8,225,384]{2,1,0:T(8,128)(2,1)}, bf16[8,225,384]{2,1,0:T(8,128)(2,1)}) custom-call(s32[10]{0:T(128)S(1)} %copy-done.14, bf16[2,240,384]{2,1,0:T(8,128)(2,1)S(1)} %attention_far.1.refs_1_, bf16[768,384]{1,0:T(8,128)(2,1)S(1)} %copy-done.1, bf16[768,384]{1,0:T(8,128)(2,1)S(1)} %copy-done.3, bf16[768,384]{1,0:T(8,128)(2,1)S(1)} %copy-done.5, ...), custom_call_target="tpu_custom_call" | custom-call | flops 1132462080 | bytes 5308416 | tf_op jit(solution)/shard_map/out_projection/pallas_call | solution.py:408
  157.4 3.1 %collective-permute-done.31 = bf16[8,225,384]{2,0,1:T(8,128)(2,1)S(1)} collective-permute-done((bf16[8,225,384]{2,0,1:T(8,128)(2,1)S(1)}, bf16[8,225,384]{2,0,1:T(8,128)(2,1)S(1)}, u32[]{:S(2)}, u32[]{:S(2)}) %collective-permute-start.31) | collective-permute-done | bytes 1382432 | tf_op jit(solution)/shard_map/ppermute | solution.py:50
  162.4 2.7 %collective-permute-start.32 = (bf16[2,225,384]{2,1,0:T(8,128)(2,1)S(1)}, bf16[2,225,384]{2,1,0:T(8,128)(2,1)S(1)}, u32[]{:S(2)}, u32[]{:S(2)}) collective-permute-start(bf16[2,225,384]{2,1,0:T(8,128)(2,1)S(1)} %get-tuple-element.39), channel_id=1, source_target_pairs={{0,6},{1,3},{2,0},{3,5},{4,2},{5,7},{6,4},{7,1},{8,14},{9,11},{10,... | collective-permute-start | bytes 1036808 | tf_op jit(solution)/shard_map/ppermute | solution.py:29
  165.0 8.4 %collective-permute-done.33 = bf16[2,225,384]{2,1,0:T(8,128)(2,1)S(1)} collective-permute-done((bf16[2,225,384]{2,1,0:T(8,128)(2,1)S(1)}, bf16[2,225,384]{2,1,0:T(8,128)(2,1)S(1)}, u32[]{:S(2)}, u32[]{:S(2)}) %collective-permute-start.33) | collective-permute-done | bytes 345632 | tf_op jit(solution)/shard_map/ppermute | solution.py:29
  174.4 8.8 %collective-permute-done.34 = bf16[2,225,384]{2,1,0:T(8,128)(2,1)S(1)} collective-permute-done((bf16[2,225,384]{2,1,0:T(8,128)(2,1)}, bf16[2,225,384]{2,1,0:T(8,128)(2,1)S(1)}, u32[]{:S(2)}, u32[]{:S(2)}) %collective-permute-start.34) | collective-permute-done | bytes 345632 | tf_op jit(solution)/shard_map/ppermute | solution.py:29
  (154 shorter events, 52.4 us)
Async XLA Ops:
  2.2 32.0 %collective-permute-start = (bf16[768,384]{1,0:T(8,128)(2,1)S(1)}, bf16[768,384]{1,0:T(8,128)(2,1)S(1)}, u32[]{:S(2)}, u32[]{:S(2)}) collective-permute-start(bf16[768,384]{1,0:T(8,128)(2,1)S(1)} %pad_maximum_fusion.refs_8_.refs_2_), channel_id=1, source_target_pairs={{0,8},{1,33},{2,10},{3,35},{4,12},{5,37},{6,14},{7,39},{8,16},{9,4... | collective-permute-start | bytes 1769480 | tf_op jit(solution)/shard_map/ppermute | solution.py:29
  2.5 31.7 %collective-permute-start.1 = (bf16[768,384]{1,0:T(8,128)(2,1)S(1)}, bf16[768,384]{1,0:T(8,128)(2,1)S(1)}, u32[]{:S(2)}, u32[]{:S(2)}) collective-permute-start(bf16[768,384]{1,0:T(8,128)(2,1)S(1)} %pad_maximum_fusion.refs_8_.refs_2_), channel_id=1, source_target_pairs={{0,24},{1,97},{2,26},{3,99},{4,28},{5,101},{6,30},{7,103},{8,0},{9... | collective-permute-start | bytes 1769480 | tf_op jit(solution)/shard_map/ppermute | solution.py:29
  13.3 16.5 %collective-permute-start.2 = (bf16[225,384]{1,0:T(8,128)(2,1)}, bf16[225,384]{1,0:T(8,128)(2,1)}, u32[]{:S(2)}, u32[]{:S(2)}) collective-permute-start(bf16[225,384]{1,0:T(8,128)(2,1)} %bitcast.21), channel_id=1, source_target_pairs={{0,120},{8,0},{16,8},{24,16},{32,24},{40,32},{48,40},{56,48},{64,5... | collective-permute-start | bytes 518408 | tf_op jit(solution)/shard_map/ppermute | solution.py:55
  16.3 24.2 %collective-permute-start.11 = (bf16[768,384]{1,0:T(8,128)(2,1)S(1)}, bf16[768,384]{1,0:T(8,128)(2,1)S(1)}, u32[]{:S(2)}, u32[]{:S(2)}) collective-permute-start(bf16[768,384]{1,0:T(8,128)(2,1)S(1)} %pad_maximum_fusion.refs_8_.refs_2_), channel_id=1, source_target_pairs={{0,32},{1,9},{2,34},{3,11},{4,36},{5,13},{6,38},{7,15},{8,40},{9,1... | collective-permute-start | bytes 1769480 | tf_op jit(solution)/shard_map/ppermute | solution.py:29
  19.2 23.4 %collective-permute-start.15 = (bf16[768,384]{1,0:T(8,128)(2,1)S(1)}, bf16[768,384]{1,0:T(8,128)(2,1)S(1)}, u32[]{:S(2)}, u32[]{:S(2)}) collective-permute-start(bf16[768,384]{1,0:T(8,128)(2,1)S(1)} %pad_maximum_fusion.refs_8_.refs_2_), channel_id=1, source_target_pairs={{0,96},{1,25},{2,98},{3,27},{4,100},{5,29},{6,102},{7,31},{8,104},... | collective-permute-start | bytes 1769480 | tf_op jit(solution)/shard_map/ppermute | solution.py:29
  21.2 13.0 %all-to-all-start.1 = ((f32[16,2,1152]{2,1,0:T(2,128)}), f32[16,2,1152]{2,1,0:T(2,128)}, u32[]{:S(2)}, u32[]{:S(2)}) async-start(f32[16,2,1152]{2,1,0:T(2,128)} %copy.33), calls=%async_computation.1 | async-start | bytes 294912 | tf_op jit(solution)/shard_map/all_to_all | solution.py:329
  34.2 11.9 %collective-permute-start.4 = (bf16[2,225,384]{2,1,0:T(8,128)(2,1)}, bf16[2,225,384]{2,1,0:T(8,128)(2,1)S(1)}, u32[]{:S(2)}, u32[]{:S(2)}) collective-permute-start(bf16[2,225,384]{2,1,0:T(8,128)(2,1)} %pad_maximum_fusion.1.refs_0_), channel_id=1, source_target_pairs={{0,2},{1,7},{2,4},{3,1},{4,6},{5,3},{6,0},{7,5},{8,10},{9,15},{10,... | collective-permute-start | bytes 1036808 | tf_op jit(solution)/shard_map/ppermute | solution.py:29
  38.4 16.3 %collective-permute-start.3 = (bf16[768,384]{1,0:T(8,128)(2,1)S(1)}, bf16[768,384]{1,0:T(8,128)(2,1)S(1)}, u32[]{:S(2)}, u32[]{:S(2)}) collective-permute-start(bf16[768,384]{1,0:T(8,128)(2,1)S(1)} %collective-permute-done.refs_9_.refs_3_), channel_id=1, source_target_pairs={{0,8},{1,33},{2,10},{3,35},{4,12},{5,37},{6,14},{7,39},{8,16},{9,4... | collective-permute-start | bytes 1769480 | tf_op jit(solution)/shard_map/ppermute | solution.py:29
  40.6 14.1 %collective-permute-start.12 = (bf16[768,384]{1,0:T(8,128)(2,1)S(1)}, bf16[768,384]{1,0:T(8,128)(2,1)}, u32[]{:S(2)}, u32[]{:S(2)}) collective-permute-start(bf16[768,384]{1,0:T(8,128)(2,1)S(1)} %collective-permute-done.refs_9_.refs_3_), channel_id=1, source_target_pairs={{0,32},{1,9},{2,34},{3,11},{4,36},{5,13},{6,38},{7,15},{8,40},{9,1... | collective-permute-start | bytes 1769480 | tf_op jit(solution)/shard_map/ppermute | solution.py:29
  46.8 16.7 %collective-permute-start.16 = (bf16[768,384]{1,0:T(8,128)(2,1)S(1)}, bf16[768,384]{1,0:T(8,128)(2,1)S(1)}, u32[]{:S(2)}, u32[]{:S(2)}) collective-permute-start(bf16[768,384]{1,0:T(8,128)(2,1)S(1)} %collective-permute-done.refs_9_.refs_3_), channel_id=1, source_target_pairs={{0,96},{1,25},{2,98},{3,27},{4,100},{5,29},{6,102},{7,31},{8,104},... | collective-permute-start | bytes 1769480 | tf_op jit(solution)/shard_map/ppermute | solution.py:29
  48.1 15.4 %collective-permute-start.13 = (bf16[768,384]{1,0:T(8,128)(2,1)S(1)}, bf16[768,384]{1,0:T(8,128)(2,1)S(1)}, u32[]{:S(2)}, u32[]{:S(2)}) collective-permute-start(bf16[768,384]{1,0:T(8,128)(2,1)S(1)} %collective-permute-done.1.refs_10_.refs_4_), channel_id=1, source_target_pairs={{0,32},{1,9},{2,34},{3,11},{4,36},{5,13},{6,38},{7,15},{8,40},{9,1... | collective-permute-start | bytes 1769480 | tf_op jit(solution)/shard_map/ppermute | solution.py:29
  54.7 15.3 %collective-permute-start.18 = (bf16[768,384]{1,0:T(8,128)(2,1)S(1)}, bf16[768,384]{1,0:T(8,128)(2,1)}, u32[]{:S(2)}, u32[]{:S(2)}) collective-permute-start(bf16[768,384]{1,0:T(8,128)(2,1)S(1)} %collective-permute-done.3.refs_11_.refs_5_), channel_id=1, source_target_pairs={{0,96},{1,25},{2,98},{3,27},{4,100},{5,29},{6,102},{7,31},{8,104},... | collective-permute-start | bytes 1769480 | tf_op jit(solution)/shard_map/ppermute | solution.py:29
  64.5 17.4 %collective-permute-start.14 = (bf16[768,384]{1,0:T(8,128)(2,1)S(1)}, bf16[768,384]{1,0:T(8,128)(2,1)}, u32[]{:S(2)}, u32[]{:S(2)}) collective-permute-start(bf16[768,384]{1,0:T(8,128)(2,1)S(1)} %collective-permute-done.3.refs_11_.refs_5_), channel_id=1, source_target_pairs={{0,32},{1,9},{2,34},{3,11},{4,36},{5,13},{6,38},{7,15},{8,40},{9,1... | collective-permute-start | bytes 1769480 | tf_op jit(solution)/shard_map/ppermute | solution.py:29
  67.5 14.5 %collective-permute-start.20 = (bf16[768,384]{1,0:T(8,128)(2,1)}, bf16[768,384]{1,0:T(8,128)(2,1)}, u32[]{:S(2)}, u32[]{:S(2)}) collective-permute-start(bf16[768,384]{1,0:T(8,128)(2,1)} %collective-permute-done.12.refs_13_.refs_7_), channel_id=1, source_target_pairs={{0,32},{1,9},{2,34},{3,11},{4,36},{5,13},{6,38},{7,15},{8,40},{9,1... | collective-permute-start | bytes 1769480 | tf_op jit(solution)/shard_map/ppermute | solution.py:29
  67.6 14.4 %collective-permute-start.21 = (bf16[768,384]{1,0:T(8,128)(2,1)}, bf16[768,384]{1,0:T(8,128)(2,1)}, u32[]{:S(2)}, u32[]{:S(2)}) collective-permute-start(bf16[768,384]{1,0:T(8,128)(2,1)} %collective-permute-done.17.refs_18_.refs_12_), channel_id=1, source_target_pairs={{0,96},{1,25},{2,98},{3,27},{4,100},{5,29},{6,102},{7,31},{8,104},... | collective-permute-start | bytes 1769480 | tf_op jit(solution)/shard_map/ppermute | solution.py:29
  69.9 15.4 %collective-permute-start.22 = (bf16[768,384]{1,0:T(8,128)(2,1)}, bf16[768,384]{1,0:T(8,128)(2,1)}, u32[]{:S(2)}, u32[]{:S(2)}) collective-permute-start(bf16[768,384]{1,0:T(8,128)(2,1)} %collective-permute-done.18.refs_19_.refs_13_), channel_id=1, source_target_pairs={{0,96},{1,25},{2,98},{3,27},{4,100},{5,29},{6,102},{7,31},{8,104},... | collective-permute-start | bytes 1769480 | tf_op jit(solution)/shard_map/ppermute | solution.py:29
  101.0 17.4 %collective-permute-start.25 = (bf16[2,240,384]{2,1,0:T(8,128)(2,1)}, bf16[2,240,384]{2,1,0:T(8,128)(2,1)S(1)}, u32[]{:S(2)}, u32[]{:S(2)}) collective-permute-start(bf16[2,240,384]{2,1,0:T(8,128)(2,1)} %get-tuple-element.33.refs_6_), channel_id=1, source_target_pairs={{0,8},{8,16},{16,24},{24,32},{32,40},{40,48},{48,56},{56,64},{64,7... | collective-permute-start | bytes 1105928 | tf_op jit(solution)/shard_map/ppermute | solution.py:55
  101.1 22.8 %collective-permute-start.27 = (bf16[2,240,384]{2,1,0:T(8,128)(2,1)}, bf16[2,240,384]{2,1,0:T(8,128)(2,1)S(1)}, u32[]{:S(2)}, u32[]{:S(2)}) collective-permute-start(bf16[2,240,384]{2,1,0:T(8,128)(2,1)} %get-tuple-element.32.refs_5_), channel_id=1, source_target_pairs={{0,120},{8,0},{16,8},{24,16},{32,24},{40,32},{48,40},{56,48},{64,5... | collective-permute-start | bytes 1105928 | tf_op jit(solution)/shard_map/ppermute | solution.py:55
  103.1 20.9 %collective-permute-start.29 = (bf16[2,240,384]{2,1,0:T(8,128)(2,1)}, bf16[2,240,384]{2,1,0:T(8,128)(2,1)S(1)}, u32[]{:S(2)}, u32[]{:S(2)}) collective-permute-start(bf16[2,240,384]{2,1,0:T(8,128)(2,1)} %get-tuple-element.33.refs_6_), channel_id=1, source_target_pairs={{0,120},{8,0},{16,8},{24,16},{32,24},{40,32},{48,40},{56,48},{64,5... | collective-permute-start | bytes 1105928 | tf_op jit(solution)/shard_map/ppermute | solution.py:55
  110.6 25.3 %collective-permute-start.24 = (bf16[2,240,384]{2,1,0:T(8,128)(2,1)S(1)}, bf16[2,240,384]{2,1,0:T(8,128)(2,1)S(1)}, u32[]{:S(2)}, u32[]{:S(2)}) collective-permute-start(bf16[2,240,384]{2,1,0:T(8,128)(2,1)S(1)} %collective-permute-done.23.refs_3_), channel_id=1, source_target_pairs={{0,8},{8,16},{16,24},{24,32},{32,40},{40,48},{48,56},{56,64},{64,7... | collective-permute-start | bytes 1105928 | tf_op jit(solution)/shard_map/ppermute | solution.py:55
  118.5 17.4 %collective-permute-start.26 = (bf16[2,240,384]{2,1,0:T(8,128)(2,1)S(1)}, bf16[2,240,384]{2,1,0:T(8,128)(2,1)S(1)}, u32[]{:S(2)}, u32[]{:S(2)}) collective-permute-start(bf16[2,240,384]{2,1,0:T(8,128)(2,1)S(1)} %collective-permute-done.25.refs_4_), channel_id=1, source_target_pairs={{0,8},{8,16},{16,24},{24,32},{32,40},{40,48},{48,56},{56,64},{64,7... | collective-permute-start | bytes 1105928 | tf_op jit(solution)/shard_map/ppermute | solution.py:55
  124.0 14.8 %collective-permute-start.28 = (bf16[2,240,384]{2,1,0:T(8,128)(2,1)S(1)}, bf16[2,240,384]{2,1,0:T(8,128)(2,1)S(1)}, u32[]{:S(2)}, u32[]{:S(2)}) collective-permute-start(bf16[2,240,384]{2,1,0:T(8,128)(2,1)S(1)} %collective-permute-done.27.refs_7_), channel_id=1, source_target_pairs={{0,120},{8,0},{16,8},{24,16},{32,24},{40,32},{48,40},{56,48},{64,5... | collective-permute-start | bytes 1105928 | tf_op jit(solution)/shard_map/ppermute | solution.py:55
  124.0 19.0 %collective-permute-start.30 = (bf16[2,240,384]{2,1,0:T(8,128)(2,1)S(1)}, bf16[2,240,384]{2,1,0:T(8,128)(2,1)S(1)}, u32[]{:S(2)}, u32[]{:S(2)}) collective-permute-start(bf16[2,240,384]{2,1,0:T(8,128)(2,1)S(1)} %collective-permute-done.29.refs_8_), channel_id=1, source_target_pairs={{0,120},{8,0},{16,8},{24,16},{32,24},{40,32},{48,40},{56,48},{64,5... | collective-permute-start | bytes 1105928 | tf_op jit(solution)/shard_map/ppermute | solution.py:55
  162.4 12.0 %collective-permute-start.32 = (bf16[2,225,384]{2,1,0:T(8,128)(2,1)S(1)}, bf16[2,225,384]{2,1,0:T(8,128)(2,1)S(1)}, u32[]{:S(2)}, u32[]{:S(2)}) collective-permute-start(bf16[2,225,384]{2,1,0:T(8,128)(2,1)S(1)} %get-tuple-element.39), channel_id=1, source_target_pairs={{0,6},{1,3},{2,0},{3,5},{4,2},{5,7},{6,4},{7,1},{8,14},{9,11},{10,... | collective-permute-start | bytes 1036808 | tf_op jit(solution)/shard_map/ppermute | solution.py:29
  (46 other events, 602.1 us)

commit v3 on v2

--- a/solution.py
+++ b/solution.py
@@ -78,13 +78,16 @@
     return lax.rem(value + by + SIDE, SIDE)
 
 
-def shard_copies(places, inner_at, outer_at, inner_stride, outer_stride, target, sems):
+def shard_copies(places, pos_ref, target, column, sems):
     copies = []
     for outer in range(SIDE):
         for inner in range(SIDE):
-            owner = wrap(outer_at, ORIGIN[outer]) * outer_stride + wrap(inner_at, ORIGIN[inner]) * inner_stride
+            owner = wrap(pos_ref[1], ORIGIN[outer]) * pos_ref[3] + wrap(pos_ref[0], ORIGIN[inner]) * pos_ref[2]
+            rows = pl.ds(pl.multiple_of(owner * 192, 192), 192)
             copies.append(
-                pltpu.make_async_copy(places[outer][inner], target.at[owner], sems.at[len(copies)])
+                pltpu.make_async_copy(
+                    places[outer][inner], target.at[rows, column : column + 384], sems.at[len(copies)]
+                )
             )
     return copies
 
@@ -131,35 +134,62 @@
         out_ref[slot, tokens:, :] = jnp.zeros((PADDED - tokens, D), jnp.bfloat16)
 
 
-def project_kernel(pos_ref, mod_ref, q_gain_ref, k_gain_ref, *refs):
-    states, shards, (q_ref, k_ref, v_ref, modulated, weight, sems) = refs[:8], refs[8:24], refs[24:]
-    places = [
-        [shards[SIDE * outer + inner].at[pl.ds(0, 576)] for inner in range(SIDE)] for outer in range(SIDE)
+def shard_places(shards, top):
+    return [[shards[SIDE * outer + inner].at[pl.ds(top, 192)] for inner in range(SIDE)] for outer in range(SIDE)]
+
+
+def key_value_kernel(pos_ref, mod_ref, gain_ref, *refs):
+    given, shards = refs[:8], refs[8:24]
+    k_ref, v_ref, x_ref, held, modulated, weight, held_sems, x_sem, sems = refs[24:]
+    states = [held.at[part] for part in range(8)]
+    arriving = [
+        pltpu.make_async_copy(given[part], states[part], held_sems.at[part]) for part in range(8)
     ]
-    copies = shard_copies(places, pos_ref[0], pos_ref[1], pos_ref[2], pos_ref[3], weight, sems)
+    for copy in arriving:
+        copy.start()
+    copies = [
+        shard_copies(shard_places(shards, part * 192), pos_ref, weight, part * 384, sems.at[part])
+        for part in range(2)
+    ]
+    for copy in sum(copies, []):
+        copy.start()
+    for copy in arriving:
+        copy.wait()
+    modulate(pos_ref, mod_ref, states[:SIDE], states[SIDE:], modulated)
+    x_copy = pltpu.make_async_copy(modulated, x_ref, x_sem)
+    x_copy.start()
+    x = modulated[...].reshape(2 * PADDED, D)
+    for group in range(6):
+        if group in (0, 2):
+            for copy in copies[group // 2]:
+                copy.wait()
+        if group % 2 == 0:
+            both = jnp.dot(
+                x, weight[:, group * PAIR : (group + 2) * PAIR], preferred_element_type=jnp.float32
+            )
+        piece = both[:, group % 2 * PAIR : (group % 2 + 1) * PAIR]
+        columns = slice(group % 3 * PAIR, (group % 3 + 1) * PAIR)
+        piece = head_norm_pair(piece, gain_ref) if group < 3 else piece.astype(jnp.bfloat16)
+        for slot in range(2):
+            (k_ref, v_ref)[group // 3][slot, :, columns] = piece[slot * PADDED : (slot + 1) * PADDED]
+    x_copy.wait()
+
+
+def query_kernel(pos_ref, x_ref, gain_ref, *refs):
+    shards, (q_ref, out_weight_ref, weight, sems) = refs[:16], refs[16:]
+    copies = shard_copies(shard_places(shards, 384), pos_ref, weight, 0, sems.at[0])
+    copies += shard_copies(shard_places(shards, 576), pos_ref, out_weight_ref, 0, sems.at[1])
     for copy in copies:
         copy.start()
-    modulate(pos_ref, mod_ref, states[:SIDE], states[SIDE:], modulated)
     for copy in copies:
         copy.wait()
-    x = modulated[...].reshape(2 * PADDED, D)
-    for part, target in enumerate((k_ref, v_ref, q_ref)):
-        whole = jnp.dot(
-            x,
-            weight[:, part * 192 : part * 192 + 192, :].reshape(D, 384),
-            preferred_element_type=jnp.float32,
-        )
-        for pair in range(3):
-            columns = slice(pair * PAIR, (pair + 1) * PAIR)
-            piece = whole[:, columns]
-            if part == 0:
-                piece = head_norm_pair(piece, k_gain_ref)
-            elif part == 1:
-                piece = piece.astype(jnp.bfloat16)
-            else:
-                piece = head_norm_pair(piece, q_gain_ref) * jnp.asarray(1.0 / math.sqrt(HEAD), jnp.bfloat16)
-            for slot in range(2):
-                target[slot, :, columns] = piece[slot * PADDED : (slot + 1) * PADDED]
+    x = x_ref[...].reshape(2 * PADDED, D)
+    whole = jnp.dot(x, weight[...], preferred_element_type=jnp.float32)
+    for pair in range(3):
+        columns = slice(pair * PAIR, (pair + 1) * PAIR)
+        piece = head_norm_pair(whole[:, columns], gain_ref) * jnp.asarray(1.0 / math.sqrt(HEAD), jnp.bfloat16)
+        for slot in range(2):
+            q_ref[slot, :, columns] = piece[slot * PADDED : (slot + 1) * PADDED]
 
 
 def fill_window(pairs, keys, values):
@@ -242,16 +272,7 @@
         out_ref[slot] = (mix / total).astype(jnp.bfloat16)
 
 
-def out_kernel(tokens, pos_ref, x_ref, *refs):
-    shards, (keep_ref, send_ref, weight, sems) = refs[:16], refs[16:]
-    places = [
-        [shards[SIDE * outer + inner].at[pl.ds(576, 192)] for inner in range(SIDE)] for outer in range(SIDE)
-    ]
-    copies = shard_copies(places, pos_ref[0], pos_ref[1], pos_ref[2], pos_ref[3], weight, sems)
-    for copy in copies:
-        copy.start()
-    for copy in copies:
-        copy.wait()
+def out_kernel(tokens, pos_ref, x_ref, weight, keep_ref, send_ref):
     x = x_ref[...].reshape(2 * PADDED, 384)
     z = pos_ref[4]
     core = pos_ref[5]
@@ -259,7 +280,7 @@
     for ref, at_core, along in ((send_ref, 1 - core, -way), (keep_ref, core, way)):
         for hop in range(SIDE):
             owner = wrap(z, hop * along) * 2 + at_core
-            rows = weight[pl.ds(owner * 2, 2)].reshape(384, 384)
+            rows = weight[pl.ds(pl.multiple_of(owner * 384, 384), 384), :]
             part = lax.dot_general(
                 x, rows, (((1,), (1,)), ((), ())), preferred_element_type=jnp.float32
             ).astype(jnp.bfloat16)
@@ -318,13 +339,14 @@
     plan = jnp.concatenate([timestep_index[:, None], window_offsets], axis=1)
     below = first_step(shard, 1)
     above = first_step(shard, -1)
-    head = next_frame(hidden_states[0], -1)
     plan = spread(plan, "frame").reshape(slots, 3)
     shard, plan = together(shard, plan)
     own_b = second_step(shard, 1)
     own_a = second_step(shard, -1)
     waves = level_waves(jnp.roll(plan[:, 0], -1), place)
     sums = jnp.dot(waves, mod_weight.reshape(-1, 3 * width), preferred_element_type=jnp.float32)
+    sums, first = together(sums, hidden_states[0])
+    head = next_frame(first, -1)
     states = jnp.stack([hidden_states[1], head])
     sums = lax.all_to_all(sums.reshape(slots // 2, 2, 3 * width), "frame", 0, 0, tiled=True)
     below, above, states, sums = together(below, above, states, sums)
@@ -341,32 +363,47 @@
     own_f = second_step(own_b, 1)
     z_f = z_step(z_b, 1)
     below_f = second_step(below_b, 1)
+    mods = jnp.sum(sums, axis=0)
+    all_mods = spread(mods, "row")
     above_f = second_step(above_a, -1)
     far_f = second_step(far_a, -1)
     own_states = [states, z_b, z_a, z_f]
     other_states = [other_core(part) for part in own_states]
-    mods = jnp.sum(sums, axis=0)
-    all_mods = spread(mods, "row")
     shards = [
         shard, below, above, far,
         own_b, below_b, above_b, far_b,
         own_a, below_a, above_a, far_a,
         own_f, below_f, above_f, far_f,
     ]
-    queries, keys, values = call(
-        project_kernel,
-        [struct((2, PADDED, width))] * 3,
-        [SMEM] + [VMEM] * 11 + [ANY] * len(shards),
-        [
+    keys, values, modulated = pl.pallas_call(
+        key_value_kernel,
+        out_shape=[struct((2, PADDED, width))] * 2 + [struct((2, PADDED, D))],
+        in_specs=[SMEM] + [VMEM] * 2 + [ANY] * (8 + len(shards)),
+        out_specs=[VMEM, VMEM, ANY],
+        scratch_shapes=[
+            pltpu.VMEM((8, 2, tokens, width), jnp.bfloat16),
             pltpu.VMEM((2, PADDED, D), jnp.bfloat16),
-            pltpu.VMEM((16, 3 * 192, width), jnp.bfloat16),
-            pltpu.SemaphoreType.DMA((16,)),
+            pltpu.VMEM((D, 2 * width), jnp.bfloat16),
+            pltpu.SemaphoreType.DMA((8,)),
+            pltpu.SemaphoreType.DMA,
+            pltpu.SemaphoreType.DMA((2, 16)),
         ],
-        "projections",
-        4 * PADDED * D * 3 * width,
-        D * width * 6 + PADDED * D * 4,
+        name="keys_values",
+        compiler_params=pltpu.CompilerParams(vmem_limit_bytes=60 << 20),
+        cost_estimate=pl.CostEstimate(
+            flops=4 * PADDED * D * 2 * width, bytes_accessed=D * width * 4 + PADDED * D * 4, transcendentals=0
+        ),
+    )(pos, all_mods, key_gain[None], *own_states, *other_states, *shards)
+    queries, out_whole = call(
+        query_kernel,
+        [struct((2, PADDED, width)), struct((D, width))],
+        [SMEM, VMEM, VMEM] + [ANY] * len(shards),
+        [pltpu.VMEM((D, width), jnp.bfloat16), pltpu.SemaphoreType.DMA((2, 16))],
+        "queries",
+        4 * PADDED * D * width,
+        D * width * 4 + PADDED * D * 4,
         vmem=60,
-    )(pos, all_mods, query_gain[None], key_gain[None], *own_states, *other_states, *shards)
+    )(pos, modulated, query_gain[None], *shards)
 
     near = [next_frame(part, by) for part in (keys, values) for by in (1, -1)]
     far_kv = [next_frame(part, by) for part, by in zip(near, (1, -1, 1, -1))]
@@ -408,12 +445,12 @@
     keep, send = call(
         lambda *refs: out_kernel(tokens, *refs),
         [struct((2 * SIDE, tokens, width))] * 2,
-        [SMEM, VMEM] + [ANY] * len(shards),
-        [pltpu.VMEM((16, 192, width), jnp.bfloat16), pltpu.SemaphoreType.DMA((16,))],
+        [SMEM, VMEM, VMEM],
+        [],
         "out_projection",
         4 * PADDED * D * width,
         D * width * 2 + PADDED * D * 4,
-    )(pos, mixed, *shards)
+    )(pos, mixed, out_whole)
 
     swapped = other_core(send)
     chip = [

time: 186 us -> 176 us (0.946)
  starting transfers between devices: 63.9 us -> 58.9 us
  local copies, waits for them, and re-layouts: 14.2 us -> 10.6 us
  other arithmetic: 6.86 us -> 4.25 us
    pallas_call x1 -> x2, Pallas kernels: 13.4 us -> 19 us  [the longest x1 11.2 us: per_device(): pl.pallas_call(key_value_kernel, out_shape=[struct((2, PADDED, width))] *...]
    pallas_call x1, Pallas kernels: 6.84 us -> 2.55 us  [per_device(): call(lambda *refs: out_kernel(tokens, *refs), [struct((2 * SIDE, tokens,...]
    ppermute x21, starting transfers between devices: 27 us -> 24 us  [torus_step(): return lax.ppermute(array, ('frame', 'row'), pairs)]
    all_to_all x1, waiting for transfers between devices: 2.59 us -> 0.01 us  [per_device(): lax.all_to_all(sums.reshape(slots // 2, 2, 3 * width), 'frame', 0, 0, til...]
    ppermute x9, starting transfers between devices: 16.5 us -> 14.3 us  [next_frame(): lax.ppermute(array, 'frame', [(i, (i + by) % peers) for i in range(peers)])]
    unnamed x67 -> x56, local copies, waits for them, and re-layouts: 4.58 us -> 2.54 us
  transfers between devices with their start and end apart: 38 -> 38, of which waited for: 17 -> 16; matrix products, arithmetic and copies ran while one was open for 6% -> 5% of each run, Pallas kernels for 5% -> 9%
where the time goes in v3:
time: 176 us
  waiting for transfers between devices  65.1 us (37%)
  starting transfers between devices  58.9 us (33%)
  Pallas kernels  36.1 us (21%)
  local copies, waits for them, and re-layouts  10.6 us (6%)
  other arithmetic  4.25 us (2%)
    ppermute x21, waiting for transfers between devices, torus_step(): return lax.ppermute(array, ('frame', 'row'), pairs)  37.9 us
    ppermute x21, starting transfers between devices, torus_step(): return lax.ppermute(array, ('frame', 'row'), pairs)  24 us
    ppermute x9, waiting for transfers between devices, next_frame(): lax.ppermute(array, 'frame', [(i, (i + by) % peers) for i in range(peers)])  17 us
    ppermute x9, starting transfers between devices, next_frame(): lax.ppermute(array, 'frame', [(i, (i + by) % peers) for i in range(peers)])  14.3 us
    all_to_all x2, starting transfers between devices, spread(): return lax.all_to_all(copies, axis, 0, 0, tiled=True)  11.8 us
    pallas_call x1, Pallas kernels, per_device(): pl.pallas_call(key_value_kernel, out_shape=[struct((2, PADDED, width))] *...  11.2 us
    pallas_call x1, Pallas kernels, per_device(): pl.pallas_call(lambda *refs: near_kernel(tokens, *refs), out_shape=[struc...  8.62 us
    all_to_all x1, starting transfers between devices, per_device(): lax.all_to_all(sums.reshape(slots // 2, 2, 3 * width), 'frame', 0, 0, til...  8.15 us
  transfers between devices with their start and end apart: 38, of which 16 were waited for; matrix products, arithmetic and copies ran while one was open for 5% of the time, Pallas kernels for 9%

profile of v3, /device:TPU:30, one launch (start us, length us, event | category | flops | bytes accessed | tf_op | source)
XLA Modules:
  0.0 175.6 jit_solution(2283339667057487388)
XLA Ops:
  5.1 7.1 %all-to-all-start = ((s32[16,2,3]{2,1,0:T(2,128)}), s32[16,2,3]{2,1,0:T(2,128)S(1)}, u32[]{:S(2)}, u32[]{:S(2)}) async-start(s32[16,2,3]{2,1,0:T(2,128)} %broadcast_in_dim.55), calls=%async_computation | async-start | bytes 32768 | tf_op jit(solution)/shard_map/all_to_all | solution.py:74
  21.5 8.1 %all-to-all-start.1 = ((f32[16,2,1152]{2,1,0:T(2,128)}), f32[16,2,1152]{2,1,0:T(2,128)S(1)}, u32[]{:S(2)}, u32[]{:S(2)}) async-start(f32[16,2,1152]{2,1,0:T(2,128)} %reshape.59), calls=%async_computation.1 | async-start | bytes 294912 | tf_op jit(solution)/shard_map/all_to_all | solution.py:351
  29.7 5.6 %collective-permute-done.2 = bf16[225,384]{1,0:T(8,128)(2,1)} collective-permute-done((bf16[225,384]{1,0:T(8,128)(2,1)}, bf16[225,384]{1,0:T(8,128)(2,1)}, u32[]{:S(2)}, u32[]{:S(2)}) %collective-permute-start.2) | collective-permute-done | bytes 172832 | tf_op jit(solution)/shard_map/ppermute | solution.py:55
  38.3 2.2 %collective-permute-start.5 = (bf16[2,225,384]{2,1,0:T(8,128)(2,1)S(1)}, bf16[2,225,384]{2,1,0:T(8,128)(2,1)S(1)}, u32[]{:S(2)}, u32[]{:S(2)}) collective-permute-start(bf16[2,225,384]{2,1,0:T(8,128)(2,1)S(1)} %pad_maximum_fusion.1.refs_0_), channel_id=1, source_target_pairs={{0,6},{1,3},{2,0},{3,5},{4,2},{5,7},{6,4},{7,1},{8,14},{9,11},{10,... | collective-permute-start | bytes 1036808 | tf_op jit(solution)/shard_map/ppermute | solution.py:29
  42.4 3.3 %collective-permute-done.4.refs_1_ = bf16[2,225,384]{2,1,0:T(8,128)(2,1)S(1)} collective-permute-done((bf16[2,225,384]{2,1,0:T(8,128)(2,1)S(1)}, bf16[2,225,384]{2,1,0:T(8,128)(2,1)S(1)}, u32[]{:S(2)}, u32[]{:S(2)}) %collective-permute-start.4) | collective-permute-done | bytes 345632 | tf_op jit(solution)/shard_map/ppermute | solution.py:29
  47.5 2.2 %collective-permute-start.13 = (bf16[768,384]{1,0:T(8,128)(2,1)S(1)}, bf16[768,384]{1,0:T(8,128)(2,1)S(1)}, u32[]{:S(2)}, u32[]{:S(2)}) collective-permute-start(bf16[768,384]{1,0:T(8,128)(2,1)S(1)} %collective-permute-done.1.refs_10_.refs_2_), channel_id=1, source_target_pairs={{0,32},{1,9},{2,34},{3,11},{4,36},{5,13},{6,38},{7,15},{8,40},{9,1... | collective-permute-start | bytes 1769480 | tf_op jit(solution)/shard_map/ppermute | solution.py:29
  49.7 5.6 %collective-permute-done.3.refs_11_.refs_3_ = bf16[768,384]{1,0:T(8,128)(2,1)} collective-permute-done((bf16[768,384]{1,0:T(8,128)(2,1)S(1)}, bf16[768,384]{1,0:T(8,128)(2,1)}, u32[]{:S(2)}, u32[]{:S(2)}) %collective-permute-start.3) | collective-permute-done | bytes 589856 | tf_op jit(solution)/shard_map/ppermute | solution.py:29
  57.3 5.9 %collective-permute-done.16.refs_17_.refs_9_ = bf16[768,384]{1,0:T(8,128)(2,1)S(1)} collective-permute-done((bf16[768,384]{1,0:T(8,128)(2,1)S(1)}, bf16[768,384]{1,0:T(8,128)(2,1)S(1)}, u32[]{:S(2)}, u32[]{:S(2)}) %collective-permute-start.16) | collective-permute-done | bytes 589856 | tf_op jit(solution)/shard_map/ppermute | solution.py:29
  71.1 4.7 %all-to-all-start.2 = ((f32[8,2,1152]{2,1,0:T(2,128)}), f32[8,2,1152]{2,1,0:T(2,128)S(1)}, u32[]{:S(2)}, u32[]{:S(2)}) async-start(f32[8,2,1152]{2,1,0:T(2,128)} %broadcast_in_dim.56), calls=%async_computation.2 | async-start | bytes 147456 | tf_op jit(solution)/shard_map/all_to_all | solution.py:74
  76.5 5.0 %all-to-all-done.2.mod_ref = f32[8,2,1152]{2,1,0:T(2,128)S(1)} async-done(((f32[8,2,1152]{2,1,0:T(2,128)}), f32[8,2,1152]{2,1,0:T(2,128)S(1)}, u32[]{:S(2)}, u32[]{:S(2)}) %all-to-all-start.2) | async-done | bytes 73760 | tf_op jit(solution)/shard_map/all_to_all | solution.py:74
  81.7 4.3 %collective-permute-done.22.refs_23_.refs_15_ = bf16[768,384]{1,0:T(8,128)(2,1)} collective-permute-done((bf16[768,384]{1,0:T(8,128)(2,1)}, bf16[768,384]{1,0:T(8,128)(2,1)}, u32[]{:S(2)}, u32[]{:S(2)}) %collective-permute-start.22) | collective-permute-done | bytes 589856 | tf_op jit(solution)/shard_map/ppermute | solution.py:29
  86.0 11.2 %keys_values.1 = (bf16[2,240,384]{2,1,0:T(8,128)(2,1)}, bf16[2,240,384]{2,1,0:T(8,128)(2,1)}, bf16[2,240,3072]{2,1,0:T(8,128)(2,1)}) custom-call(s32[10]{0:T(128)} %concatenate.26.pos_ref.refs_1_.refs_0_, f32[8,2,1152]{2,1,0:T(2,128)} %copy-done.22, f32[1,64]{1,0:T(1,128)} %bitcast.32, bf16[2,225,384]{2,1,0:T(8,128)(2,1)} %copy-done.6, ...), custom_call_target="tpu_custom_call" | custom-call | flops 2264924160 | bytes 7667712 | tf_op jit(solution)/shard_map/keys_values/pallas_call | solution.py:378
  101.4 7.8 %queries.1 = (bf16[2,240,384]{2,1,0:T(8,128)(2,1)}, bf16[3072,384]{1,0:T(8,128)(2,1)}) custom-call(s32[10]{0:T(128)} %concatenate.26.pos_ref.refs_1_.refs_0_, bf16[2,240,3072]{2,1,0:T(8,128)(2,1)} %get-tuple-element.37.x_ref, f32[1,64]{1,0:T(1,128)} %bitcast.33, bf16[768,384]{1,0:T(8,128)(2,1)} %copy-done.5, bf16[768,384]{1,0:T(8,128)(2,1)} %copy-done.8, ...), custom_call_target="tpu_custom_call" | custom-call | flops 1132462080 | bytes 7667712 | tf_op jit(solution)/shard_map/queries/pallas_call | solution.py:397
  109.2 4.7 %collective-permute-start.24 = (bf16[2,240,384]{2,1,0:T(8,128)(2,1)S(1)}, bf16[2,240,384]{2,1,0:T(8,128)(2,1)S(1)}, u32[]{:S(2)}, u32[]{:S(2)}) collective-permute-start(bf16[2,240,384]{2,1,0:T(8,128)(2,1)S(1)} %collective-permute-done.23.refs_3_), channel_id=1, source_target_pairs={{0,8},{8,16},{16,24},{24,32},{32,40},{40,48},{48,56},{56,64},{64,7... | collective-permute-start | bytes 1105928 | tf_op jit(solution)/shard_map/ppermute | solution.py:55
  113.9 3.0 %collective-permute-done.25.refs_4_ = bf16[2,240,384]{2,1,0:T(8,128)(2,1)S(1)} collective-permute-done((bf16[2,240,384]{2,1,0:T(8,128)(2,1)}, bf16[2,240,384]{2,1,0:T(8,128)(2,1)S(1)}, u32[]{:S(2)}, u32[]{:S(2)}) %collective-permute-start.25) | collective-permute-done | bytes 368672 | tf_op jit(solution)/shard_map/ppermute | solution.py:55
  116.9 4.6 %collective-permute-start.26 = (bf16[2,240,384]{2,1,0:T(8,128)(2,1)S(1)}, bf16[2,240,384]{2,1,0:T(8,128)(2,1)S(1)}, u32[]{:S(2)}, u32[]{:S(2)}) collective-permute-start(bf16[2,240,384]{2,1,0:T(8,128)(2,1)S(1)} %collective-permute-done.25.refs_4_), channel_id=1, source_target_pairs={{0,8},{8,16},{16,24},{24,32},{32,40},{40,48},{48,56},{56,64},{64,7... | collective-permute-start | bytes 1105928 | tf_op jit(solution)/shard_map/ppermute | solution.py:55
  122.8 8.6 %attention_near.1 = (f32[2,240,384]{2,1,0:T(8,128)S(1)}, f32[2,240,384]{2,1,0:T(8,128)S(1)}, f32[2,240,384]{2,1,0:T(8,128)S(1)}) custom-call(s32[32,3]{1,0:T(8,128)S(1)} %copy.31.refs_0_, s32[10]{0:T(128)S(1)} %copy-done, bf16[2,240,384]{2,1,0:T(8,128)(2,1)S(1)} %copy-done.4, bf16[2,240,384]{2,1,0:T(8,128)(2,1)S(1)} %collective-permute-done.23.refs_3_, ...), custom_call_target="tpu_custom_call" | custom-call | flops 4529848320 | bytes 6291456 | tf_op jit(solution)/shard_map/attention_near/pallas_call | solution.py:413
  131.5 4.4 %collective-permute-done.28.refs_5_ = bf16[2,240,384]{2,1,0:T(8,128)(2,1)S(1)} collective-permute-done((bf16[2,240,384]{2,1,0:T(8,128)(2,1)S(1)}, bf16[2,240,384]{2,1,0:T(8,128)(2,1)S(1)}, u32[]{:S(2)}, u32[]{:S(2)}) %collective-permute-start.28) | collective-permute-done | bytes 368672 | tf_op jit(solution)/shard_map/ppermute | solution.py:55
  135.9 3.9 %collective-permute-done.30.refs_6_ = bf16[2,240,384]{2,1,0:T(8,128)(2,1)S(1)} collective-permute-done((bf16[2,240,384]{2,1,0:T(8,128)(2,1)S(1)}, bf16[2,240,384]{2,1,0:T(8,128)(2,1)S(1)}, u32[]{:S(2)}, u32[]{:S(2)}) %collective-permute-start.30) | collective-permute-done | bytes 368672 | tf_op jit(solution)/shard_map/ppermute | solution.py:55
  139.9 5.9 %attention_far.1.refs_1_ = bf16[2,240,384]{2,1,0:T(8,128)(2,1)S(1)} custom-call(s32[32,3]{1,0:T(8,128)S(1)} %copy.31.refs_0_, s32[10]{0:T(128)S(1)} %copy-done, bf16[2,240,384]{2,1,0:T(8,128)(2,1)S(1)} %copy-done.4, bf16[2,240,384]{2,1,0:T(8,128)(2,1)S(1)} %collective-permute-done.24.refs_3_, bf16[2,240,384]{2,1,0:T(8,128)(2,1)S(1)} %collective-permute-done.26.refs_4_, ...), custom_call_target="tpu_custom_call" | custom-call | flops 2264924160 | bytes 6291456 | tf_op jit(solution)/shard_map/attention_far/pallas_call | solution.py:429
  145.8 2.5 %out_projection.1 = (bf16[8,225,384]{2,1,0:T(8,128)(2,1)S(1)}, bf16[8,225,384]{2,1,0:T(8,128)(2,1)S(1)}) custom-call(s32[10]{0:T(128)S(1)} %copy-done, bf16[2,240,384]{2,1,0:T(8,128)(2,1)S(1)} %attention_far.1.refs_1_, bf16[3072,384]{1,0:T(8,128)(2,1)S(1)} %copy-done.1), custom_call_target="tpu_custom_call" | custom-call | flops 1132462080 | bytes 5308416 | tf_op jit(solution)/shard_map/out_projection/pallas_call | solution.py:445
  148.6 3.1 %collective-permute-done.31 = bf16[8,225,384]{2,0,1:T(8,128)(2,1)S(1)} collective-permute-done((bf16[8,225,384]{2,0,1:T(8,128)(2,1)S(1)}, bf16[8,225,384]{2,0,1:T(8,128)(2,1)S(1)}, u32[]{:S(2)}, u32[]{:S(2)}) %collective-permute-start.31) | collective-permute-done | bytes 1382432 | tf_op jit(solution)/shard_map/ppermute | solution.py:50
  156.2 8.4 %collective-permute-done.33 = bf16[2,225,384]{2,1,0:T(8,128)(2,1)S(1)} collective-permute-done((bf16[2,225,384]{2,1,0:T(8,128)(2,1)S(1)}, bf16[2,225,384]{2,1,0:T(8,128)(2,1)S(1)}, u32[]{:S(2)}, u32[]{:S(2)}) %collective-permute-start.33) | collective-permute-done | bytes 345632 | tf_op jit(solution)/shard_map/ppermute | solution.py:29
  166.0 8.3 %collective-permute-done.34 = bf16[2,225,384]{2,1,0:T(8,128)(2,1)S(1)} collective-permute-done((bf16[2,225,384]{2,1,0:T(8,128)(2,1)}, bf16[2,225,384]{2,1,0:T(8,128)(2,1)S(1)}, u32[]{:S(2)}, u32[]{:S(2)}) %collective-permute-start.34) | collective-permute-done | bytes 345632 | tf_op jit(solution)/shard_map/ppermute | solution.py:29
  (142 shorter events, 44.7 us)
Async XLA Ops:
  2.2 34.0 %collective-permute-start = (bf16[768,384]{1,0:T(8,128)(2,1)S(1)}, bf16[768,384]{1,0:T(8,128)(2,1)S(1)}, u32[]{:S(2)}, u32[]{:S(2)}) collective-permute-start(bf16[768,384]{1,0:T(8,128)(2,1)S(1)} %pad_maximum_fusion.refs_8_.refs_0_), channel_id=1, source_target_pairs={{0,8},{1,33},{2,10},{3,35},{4,12},{5,37},{6,14},{7,39},{8,16},{9,4... | collective-permute-start | bytes 1769480 | tf_op jit(solution)/shard_map/ppermute | solution.py:29
  2.5 33.8 %collective-permute-start.1 = (bf16[768,384]{1,0:T(8,128)(2,1)S(1)}, bf16[768,384]{1,0:T(8,128)(2,1)S(1)}, u32[]{:S(2)}, u32[]{:S(2)}) collective-permute-start(bf16[768,384]{1,0:T(8,128)(2,1)S(1)} %pad_maximum_fusion.refs_8_.refs_0_), channel_id=1, source_target_pairs={{0,24},{1,97},{2,26},{3,99},{4,28},{5,101},{6,30},{7,103},{8,0},{9... | collective-permute-start | bytes 1769480 | tf_op jit(solution)/shard_map/ppermute | solution.py:29
  17.0 23.5 %collective-permute-start.11 = (bf16[768,384]{1,0:T(8,128)(2,1)S(1)}, bf16[768,384]{1,0:T(8,128)(2,1)S(1)}, u32[]{:S(2)}, u32[]{:S(2)}) collective-permute-start(bf16[768,384]{1,0:T(8,128)(2,1)S(1)} %pad_maximum_fusion.refs_8_.refs_0_), channel_id=1, source_target_pairs={{0,32},{1,9},{2,34},{3,11},{4,36},{5,13},{6,38},{7,15},{8,40},{9,1... | collective-permute-start | bytes 1769480 | tf_op jit(solution)/shard_map/ppermute | solution.py:29
  19.1 23.3 %collective-permute-start.15 = (bf16[768,384]{1,0:T(8,128)(2,1)S(1)}, bf16[768,384]{1,0:T(8,128)(2,1)S(1)}, u32[]{:S(2)}, u32[]{:S(2)}) collective-permute-start(bf16[768,384]{1,0:T(8,128)(2,1)S(1)} %pad_maximum_fusion.refs_8_.refs_0_), channel_id=1, source_target_pairs={{0,96},{1,25},{2,98},{3,27},{4,100},{5,29},{6,102},{7,31},{8,104},... | collective-permute-start | bytes 1769480 | tf_op jit(solution)/shard_map/ppermute | solution.py:29
  20.1 15.2 %collective-permute-start.2 = (bf16[225,384]{1,0:T(8,128)(2,1)}, bf16[225,384]{1,0:T(8,128)(2,1)}, u32[]{:S(2)}, u32[]{:S(2)}) collective-permute-start(bf16[225,384]{1,0:T(8,128)(2,1)} %bitcast.28), channel_id=1, source_target_pairs={{0,120},{8,0},{16,8},{24,16},{32,24},{40,32},{48,40},{56,48},{64,5... | collective-permute-start | bytes 518408 | tf_op jit(solution)/shard_map/ppermute | solution.py:55
  21.5 14.7 %all-to-all-start.1 = ((f32[16,2,1152]{2,1,0:T(2,128)}), f32[16,2,1152]{2,1,0:T(2,128)S(1)}, u32[]{:S(2)}, u32[]{:S(2)}) async-start(f32[16,2,1152]{2,1,0:T(2,128)} %reshape.59), calls=%async_computation.1 | async-start | bytes 294912 | tf_op jit(solution)/shard_map/all_to_all | solution.py:351
  40.5 14.8 %collective-permute-start.3 = (bf16[768,384]{1,0:T(8,128)(2,1)S(1)}, bf16[768,384]{1,0:T(8,128)(2,1)}, u32[]{:S(2)}, u32[]{:S(2)}) collective-permute-start(bf16[768,384]{1,0:T(8,128)(2,1)S(1)} %collective-permute-done.refs_9_.refs_1_), channel_id=1, source_target_pairs={{0,8},{1,33},{2,10},{3,35},{4,12},{5,37},{6,14},{7,39},{8,16},{9,4... | collective-permute-start | bytes 1769480 | tf_op jit(solution)/shard_map/ppermute | solution.py:29
  40.5 14.8 %collective-permute-start.12 = (bf16[768,384]{1,0:T(8,128)(2,1)S(1)}, bf16[768,384]{1,0:T(8,128)(2,1)}, u32[]{:S(2)}, u32[]{:S(2)}) collective-permute-start(bf16[768,384]{1,0:T(8,128)(2,1)S(1)} %collective-permute-done.refs_9_.refs_1_), channel_id=1, source_target_pairs={{0,32},{1,9},{2,34},{3,11},{4,36},{5,13},{6,38},{7,15},{8,40},{9,1... | collective-permute-start | bytes 1769480 | tf_op jit(solution)/shard_map/ppermute | solution.py:29
  46.4 16.7 %collective-permute-start.16 = (bf16[768,384]{1,0:T(8,128)(2,1)S(1)}, bf16[768,384]{1,0:T(8,128)(2,1)S(1)}, u32[]{:S(2)}, u32[]{:S(2)}) collective-permute-start(bf16[768,384]{1,0:T(8,128)(2,1)S(1)} %collective-permute-done.refs_9_.refs_1_), channel_id=1, source_target_pairs={{0,96},{1,25},{2,98},{3,27},{4,100},{5,29},{6,102},{7,31},{8,104},... | collective-permute-start | bytes 1769480 | tf_op jit(solution)/shard_map/ppermute | solution.py:29
  47.5 15.7 %collective-permute-start.13 = (bf16[768,384]{1,0:T(8,128)(2,1)S(1)}, bf16[768,384]{1,0:T(8,128)(2,1)S(1)}, u32[]{:S(2)}, u32[]{:S(2)}) collective-permute-start(bf16[768,384]{1,0:T(8,128)(2,1)S(1)} %collective-permute-done.1.refs_10_.refs_2_), channel_id=1, source_target_pairs={{0,32},{1,9},{2,34},{3,11},{4,36},{5,13},{6,38},{7,15},{8,40},{9,1... | collective-permute-start | bytes 1769480 | tf_op jit(solution)/shard_map/ppermute | solution.py:29
  55.3 14.3 %collective-permute-start.18 = (bf16[768,384]{1,0:T(8,128)(2,1)}, bf16[768,384]{1,0:T(8,128)(2,1)}, u32[]{:S(2)}, u32[]{:S(2)}) collective-permute-start(bf16[768,384]{1,0:T(8,128)(2,1)} %collective-permute-done.3.refs_11_.refs_3_), channel_id=1, source_target_pairs={{0,96},{1,25},{2,98},{3,27},{4,100},{5,29},{6,102},{7,31},{8,104},... | collective-permute-start | bytes 1769480 | tf_op jit(solution)/shard_map/ppermute | solution.py:29
  65.1 16.3 %collective-permute-start.14 = (bf16[768,384]{1,0:T(8,128)(2,1)}, bf16[768,384]{1,0:T(8,128)(2,1)}, u32[]{:S(2)}, u32[]{:S(2)}) collective-permute-start(bf16[768,384]{1,0:T(8,128)(2,1)} %collective-permute-done.3.refs_11_.refs_3_), channel_id=1, source_target_pairs={{0,32},{1,9},{2,34},{3,11},{4,36},{5,13},{6,38},{7,15},{8,40},{9,1... | collective-permute-start | bytes 1769480 | tf_op jit(solution)/shard_map/ppermute | solution.py:29
  67.1 14.6 %collective-permute-start.20 = (bf16[768,384]{1,0:T(8,128)(2,1)}, bf16[768,384]{1,0:T(8,128)(2,1)}, u32[]{:S(2)}, u32[]{:S(2)}) collective-permute-start(bf16[768,384]{1,0:T(8,128)(2,1)} %collective-permute-done.12.refs_13_.refs_5_), channel_id=1, source_target_pairs={{0,32},{1,9},{2,34},{3,11},{4,36},{5,13},{6,38},{7,15},{8,40},{9,1... | collective-permute-start | bytes 1769480 | tf_op jit(solution)/shard_map/ppermute | solution.py:29
  68.3 13.3 %collective-permute-start.21 = (bf16[768,384]{1,0:T(8,128)(2,1)S(1)}, bf16[768,384]{1,0:T(8,128)(2,1)}, u32[]{:S(2)}, u32[]{:S(2)}) collective-permute-start(bf16[768,384]{1,0:T(8,128)(2,1)S(1)} %collective-permute-done.17.refs_18_.refs_10_), channel_id=1, source_target_pairs={{0,96},{1,25},{2,98},{3,27},{4,100},{5,29},{6,102},{7,31},{8,104},... | collective-permute-start | bytes 1769480 | tf_op jit(solution)/shard_map/ppermute | solution.py:29
  69.6 16.3 %collective-permute-start.22 = (bf16[768,384]{1,0:T(8,128)(2,1)}, bf16[768,384]{1,0:T(8,128)(2,1)}, u32[]{:S(2)}, u32[]{:S(2)}) collective-permute-start(bf16[768,384]{1,0:T(8,128)(2,1)} %collective-permute-done.18.refs_19_.refs_11_), channel_id=1, source_target_pairs={{0,96},{1,25},{2,98},{3,27},{4,100},{5,29},{6,102},{7,31},{8,104},... | collective-permute-start | bytes 1769480 | tf_op jit(solution)/shard_map/ppermute | solution.py:29
  97.2 12.0 %collective-permute-start.23 = (bf16[2,240,384]{2,1,0:T(8,128)(2,1)}, bf16[2,240,384]{2,1,0:T(8,128)(2,1)S(1)}, u32[]{:S(2)}, u32[]{:S(2)}) collective-permute-start(bf16[2,240,384]{2,1,0:T(8,128)(2,1)} %get-tuple-element.39.refs_5_), channel_id=1, source_target_pairs={{0,8},{8,16},{16,24},{24,32},{32,40},{40,48},{48,56},{56,64},{64,7... | collective-permute-start | bytes 1105928 | tf_op jit(solution)/shard_map/ppermute | solution.py:55
  98.5 18.4 %collective-permute-start.25 = (bf16[2,240,384]{2,1,0:T(8,128)(2,1)}, bf16[2,240,384]{2,1,0:T(8,128)(2,1)S(1)}, u32[]{:S(2)}, u32[]{:S(2)}) collective-permute-start(bf16[2,240,384]{2,1,0:T(8,128)(2,1)} %get-tuple-element.40.refs_6_), channel_id=1, source_target_pairs={{0,8},{8,16},{16,24},{24,32},{32,40},{40,48},{48,56},{56,64},{64,7... | collective-permute-start | bytes 1105928 | tf_op jit(solution)/shard_map/ppermute | solution.py:55
  98.6 22.9 %collective-permute-start.27 = (bf16[2,240,384]{2,1,0:T(8,128)(2,1)}, bf16[2,240,384]{2,1,0:T(8,128)(2,1)S(1)}, u32[]{:S(2)}, u32[]{:S(2)}) collective-permute-start(bf16[2,240,384]{2,1,0:T(8,128)(2,1)} %get-tuple-element.39.refs_5_), channel_id=1, source_target_pairs={{0,120},{8,0},{16,8},{24,16},{32,24},{40,32},{48,40},{56,48},{64,5... | collective-permute-start | bytes 1105928 | tf_op jit(solution)/shard_map/ppermute | solution.py:55
  100.6 20.9 %collective-permute-start.29 = (bf16[2,240,384]{2,1,0:T(8,128)(2,1)}, bf16[2,240,384]{2,1,0:T(8,128)(2,1)S(1)}, u32[]{:S(2)}, u32[]{:S(2)}) collective-permute-start(bf16[2,240,384]{2,1,0:T(8,128)(2,1)} %get-tuple-element.40.refs_6_), channel_id=1, source_target_pairs={{0,120},{8,0},{16,8},{24,16},{32,24},{40,32},{48,40},{56,48},{64,5... | collective-permute-start | bytes 1105928 | tf_op jit(solution)/shard_map/ppermute | solution.py:55
  109.2 22.2 %collective-permute-start.24 = (bf16[2,240,384]{2,1,0:T(8,128)(2,1)S(1)}, bf16[2,240,384]{2,1,0:T(8,128)(2,1)S(1)}, u32[]{:S(2)}, u32[]{:S(2)}) collective-permute-start(bf16[2,240,384]{2,1,0:T(8,128)(2,1)S(1)} %collective-permute-done.23.refs_3_), channel_id=1, source_target_pairs={{0,8},{8,16},{16,24},{24,32},{32,40},{40,48},{48,56},{56,64},{64,7... | collective-permute-start | bytes 1105928 | tf_op jit(solution)/shard_map/ppermute | solution.py:55
  116.9 14.6 %collective-permute-start.26 = (bf16[2,240,384]{2,1,0:T(8,128)(2,1)S(1)}, bf16[2,240,384]{2,1,0:T(8,128)(2,1)S(1)}, u32[]{:S(2)}, u32[]{:S(2)}) collective-permute-start(bf16[2,240,384]{2,1,0:T(8,128)(2,1)S(1)} %collective-permute-done.25.refs_4_), channel_id=1, source_target_pairs={{0,8},{8,16},{16,24},{24,32},{32,40},{40,48},{48,56},{56,64},{64,7... | collective-permute-start | bytes 1105928 | tf_op jit(solution)/shard_map/ppermute | solution.py:55
  121.5 14.4 %collective-permute-start.28 = (bf16[2,240,384]{2,1,0:T(8,128)(2,1)S(1)}, bf16[2,240,384]{2,1,0:T(8,128)(2,1)S(1)}, u32[]{:S(2)}, u32[]{:S(2)}) collective-permute-start(bf16[2,240,384]{2,1,0:T(8,128)(2,1)S(1)} %collective-permute-done.27.refs_7_), channel_id=1, source_target_pairs={{0,120},{8,0},{16,8},{24,16},{32,24},{40,32},{48,40},{56,48},{64,5... | collective-permute-start | bytes 1105928 | tf_op jit(solution)/shard_map/ppermute | solution.py:55
  121.5 18.4 %collective-permute-start.30 = (bf16[2,240,384]{2,1,0:T(8,128)(2,1)S(1)}, bf16[2,240,384]{2,1,0:T(8,128)(2,1)S(1)}, u32[]{:S(2)}, u32[]{:S(2)}) collective-permute-start(bf16[2,240,384]{2,1,0:T(8,128)(2,1)S(1)} %collective-permute-done.29.refs_8_), channel_id=1, source_target_pairs={{0,120},{8,0},{16,8},{24,16},{32,24},{40,32},{48,40},{56,48},{64,5... | collective-permute-start | bytes 1105928 | tf_op jit(solution)/shard_map/ppermute | solution.py:55
  152.9 11.7 %collective-permute-start.33 = (bf16[2,225,384]{2,1,0:T(8,128)(2,1)S(1)}, bf16[2,225,384]{2,1,0:T(8,128)(2,1)S(1)}, u32[]{:S(2)}, u32[]{:S(2)}) collective-permute-start(bf16[2,225,384]{2,1,0:T(8,128)(2,1)S(1)} %get-tuple-element.48), channel_id=1, source_target_pairs={{0,2},{1,7},{2,4},{3,1},{4,6},{5,3},{6,0},{7,5},{8,10},{9,15},{10,... | collective-permute-start | bytes 1036808 | tf_op jit(solution)/shard_map/ppermute | solution.py:29
  (41 other events, 636.5 us)

commit v4 on v3

--- a/solution.py
+++ b/solution.py
@@ -106,8 +106,7 @@
     return (centered * lax.rsqrt(spread + 1e-06) * gain).astype(jnp.bfloat16)
 
 
-def modulate(pos_ref, mod_ref, own_refs, other_refs, out_ref):
-    tokens = own_refs[0].shape[1]
+def modulate(tokens, pos_ref, own_refs, other_refs, out_ref):
     width = own_refs[0].shape[2]
     z = pos_ref[4]
     core = pos_ref[5]
@@ -116,7 +115,7 @@
         total = jnp.zeros((tokens, width), jnp.float32)
         square = jnp.zeros((tokens, width), jnp.float32)
         for ref in (*own_refs, *other_refs):
-            part = ref[slot].astype(jnp.float32)
+            part = ref[slot, 0:tokens, :].astype(jnp.float32)
             total += part
             square += part * part
         mean = jnp.sum(total, axis=1, keepdims=True) * (1.0 / D)
@@ -124,11 +123,13 @@
         inverse = lax.rsqrt(meansq - mean * mean + 1e-05)
         for refs_of, at_core, along in ((own_refs, core, way), (other_refs, 1 - core, -way)):
             for hop in range(SIDE):
-                part = refs_of[hop][slot].astype(jnp.float32)
+                part = refs_of[hop][slot, 0:tokens, :].astype(jnp.float32)
+                last = refs_of[hop][slot, tokens // 16 * 16 : PADDED, :].astype(jnp.float32)
+                first = tokens % 16
                 normed = (part - mean) * inverse
                 owner = wrap(z, ORIGIN[hop] * along) * 2 + at_core
-                shift = mod_ref[owner, slot : slot + 1, 0:width]
-                scale = mod_ref[owner, slot : slot + 1, width : 2 * width]
+                shift = last[first : first + 1] + last[first + 1 : first + 2]
+                scale = last[first + 2 : first + 3] + last[first + 3 : first + 4]
                 columns = pl.ds(pl.multiple_of(owner * width, width), width)
                 out_ref[slot, 0:tokens, columns] = (normed * (1.0 + scale) + shift).astype(jnp.bfloat16)
         out_ref[slot, tokens:, :] = jnp.zeros((PADDED - tokens, D), jnp.bfloat16)
@@ -138,7 +139,7 @@
     return [[shards[SIDE * outer + inner].at[pl.ds(top, 192)] for inner in range(SIDE)] for outer in range(SIDE)]
 
 
-def key_value_kernel(pos_ref, mod_ref, gain_ref, *refs):
+def key_value_kernel(tokens, pos_ref, gain_ref, *refs):
     given, shards = refs[:8], refs[8:24]
     k_ref, v_ref, x_ref, held, modulated, weight, held_sems, x_sem, sems = refs[24:]
     states = [held.at[part] for part in range(8)]
@@ -155,7 +156,7 @@
         copy.start()
     for copy in arriving:
         copy.wait()
-    modulate(pos_ref, mod_ref, states[:SIDE], states[SIDE:], modulated)
+    modulate(tokens, pos_ref, states[:SIDE], states[SIDE:], modulated)
     x_copy = pltpu.make_async_copy(modulated, x_ref, x_sem)
     x_copy.start()
     x = modulated[...].reshape(2 * PADDED, D)
@@ -349,25 +350,30 @@
     head = next_frame(first, -1)
     states = jnp.stack([hidden_states[1], head])
     sums = lax.all_to_all(sums.reshape(slots // 2, 2, 3 * width), "frame", 0, 0, tiled=True)
-    below, above, states, sums = together(below, above, states, sums)
+    travelling = jnp.pad(states, ((0, 0), (0, PADDED - tokens), (0, 0)))
+    below, above, travelling, sums = together(below, above, travelling, sums)
+    mods = jnp.sum(sums, axis=0)
+    near_mods = lax.reduce_precision(mods, 8, 7)
+    pieces = [near_mods[:, :width], (mods - near_mods)[:, :width]]
+    pieces += [near_mods[:, width : 2 * width], (mods - near_mods)[:, width : 2 * width]]
+    pieces = jnp.stack(pieces, axis=1).astype(jnp.bfloat16)
+    travelling = lax.dynamic_update_slice(travelling, pieces, (0, tokens, 0))
     far = first_step(below, 1)
     below_b = second_step(below, 1)
     below_a = second_step(below, -1)
     above_b = second_step(above, 1)
     above_a = second_step(above, -1)
-    z_b = z_step(states, 1)
-    z_a = z_step(states, -1)
+    z_b = z_step(travelling, 1)
+    z_a = z_step(travelling, -1)
     far, z_b, z_a = together(far, z_b, z_a)
     far_b = second_step(far, 1)
     far_a = second_step(far, -1)
     own_f = second_step(own_b, 1)
     z_f = z_step(z_b, 1)
     below_f = second_step(below_b, 1)
-    mods = jnp.sum(sums, axis=0)
-    all_mods = spread(mods, "row")
     above_f = second_step(above_a, -1)
     far_f = second_step(far_a, -1)
-    own_states = [states, z_b, z_a, z_f]
+    own_states = [travelling, z_b, z_a, z_f]
     other_states = [other_core(part) for part in own_states]
     shards = [
         shard, below, above, far,
@@ -376,12 +382,12 @@
         own_f, below_f, above_f, far_f,
     ]
     keys, values, modulated = pl.pallas_call(
-        key_value_kernel,
+        lambda *refs: key_value_kernel(tokens, *refs),
         out_shape=[struct((2, PADDED, width))] * 2 + [struct((2, PADDED, D))],
-        in_specs=[SMEM] + [VMEM] * 2 + [ANY] * (8 + len(shards)),
+        in_specs=[SMEM, VMEM] + [ANY] * (8 + len(shards)),
         out_specs=[VMEM, VMEM, ANY],
         scratch_shapes=[
-            pltpu.VMEM((8, 2, tokens, width), jnp.bfloat16),
+            pltpu.VMEM((8, 2, PADDED, width), jnp.bfloat16),
             pltpu.VMEM((2, PADDED, D), jnp.bfloat16),
             pltpu.VMEM((D, 2 * width), jnp.bfloat16),
             pltpu.SemaphoreType.DMA((8,)),
@@ -393,7 +399,7 @@
         cost_estimate=pl.CostEstimate(
             flops=4 * PADDED * D * 2 * width, bytes_accessed=D * width * 4 + PADDED * D * 4, transcendentals=0
         ),
-    )(pos, all_mods, key_gain[None], *own_states, *other_states, *shards)
+    )(pos, key_gain[None], *own_states, *other_states, *shards)
     queries, out_whole = call(
         query_kernel,
         [struct((2, PADDED, width)), struct((D, width))],

time: 176 us -> 171 us (0.972)
  waiting for transfers between devices: 65.1 us -> 60.8 us
    ppermute x9, waiting for transfers between devices: 17 us -> 7.95 us  [next_frame(): lax.ppermute(array, 'frame', [(i, (i + by) % peers) for i in range(peers)])]
    ppermute x21, waiting for transfers between devices: 37.9 us -> 44.8 us  [torus_step(): return lax.ppermute(array, ('frame', 'row'), pairs)]
    ppermute x21, starting transfers between devices: 24 us -> 28.9 us  [torus_step(): return lax.ppermute(array, ('frame', 'row'), pairs)]
    all_to_all x2 -> x1, starting transfers between devices: 11.8 us -> 7.09 us  [spread(): return lax.all_to_all(copies, axis, 0, 0, tiled=True)]
    all_to_all x2 -> x1, waiting for transfers between devices: 7.13 us -> 3.52 us  [spread(): return lax.all_to_all(copies, axis, 0, 0, tiled=True)]
  transfers between devices with their start and end apart: 38 -> 37, of which waited for: 16 -> 18; matrix products, arithmetic and copies ran while one was open for 5% -> 4% of each run, Pallas kernels for 9% -> 10%
where the time goes in v4:
time: 171 us; the launch traced here: 170 us
  waiting for transfers between devices  60.8 us (36%)
  starting transfers between devices  59 us (35%)
  Pallas kernels  35.9 us (21%)
  local copies, waits for them, and re-layouts  9.37 us (5%)
  other arithmetic  4.45 us (3%)
    ppermute x21, waiting for transfers between devices, torus_step(): return lax.ppermute(array, ('frame', 'row'), pairs)  44.8 us
    ppermute x21, starting transfers between devices, torus_step(): return lax.ppermute(array, ('frame', 'row'), pairs)  28.9 us
    ppermute x9, starting transfers between devices, next_frame(): lax.ppermute(array, 'frame', [(i, (i + by) % peers) for i in range(peers)])  13.7 us
    pallas_call x1, Pallas kernels, per_device(): pl.pallas_call(lambda *refs: key_value_kernel(tokens, *refs), out_shape=[...  11 us
    all_to_all x1, starting transfers between devices, per_device(): lax.all_to_all(sums.reshape(slots // 2, 2, 3 * width), 'frame', 0, 0, til...  8.75 us
    pallas_call x1, Pallas kernels, per_device(): pl.pallas_call(lambda *refs: near_kernel(tokens, *refs), out_shape=[struc...  8.62 us
    ppermute x9, waiting for transfers between devices, next_frame(): lax.ppermute(array, 'frame', [(i, (i + by) % peers) for i in range(peers)])  7.95 us
    pallas_call x1, Pallas kernels, per_device(): call(query_kernel, [struct((2, PADDED, width)), struct((D, width))], [SME...  7.84 us
  transfers between devices with their start and end apart: 37, of which 18 were waited for; matrix products, arithmetic and copies ran while one was open for 4% of the time, Pallas kernels for 10%

profile of v4, /device:TPU:30, one launch (start us, length us, event | category | flops | bytes accessed | tf_op | source)
XLA Modules:
  0.0 170.3 jit_solution(6040727025083926011)
XLA Ops:
  5.1 7.1 %all-to-all-start = ((s32[16,2,3]{2,1,0:T(2,128)}), s32[16,2,3]{2,1,0:T(2,128)S(1)}, u32[]{:S(2)}, u32[]{:S(2)}) async-start(s32[16,2,3]{2,1,0:T(2,128)} %broadcast_in_dim.49), calls=%async_computation | async-start | bytes 32768 | tf_op jit(solution)/shard_map/all_to_all | solution.py:74
  12.8 3.5 %all-to-all-done = s32[16,2,3]{2,1,0:T(2,128)S(1)} async-done(((s32[16,2,3]{2,1,0:T(2,128)}), s32[16,2,3]{2,1,0:T(2,128)S(1)}, u32[]{:S(2)}, u32[]{:S(2)}) %all-to-all-start) | async-done | bytes 416 | tf_op jit(solution)/shard_map/all_to_all | solution.py:74
  19.4 8.7 %all-to-all-start.1 = ((f32[16,2,1152]{2,1,0:T(2,128)}), f32[16,2,1152]{2,1,0:T(2,128)}, u32[]{:S(2)}, u32[]{:S(2)}) async-start(f32[16,2,1152]{2,1,0:T(2,128)} %reshape.58), calls=%async_computation.1 | async-start | bytes 294912 | tf_op jit(solution)/shard_map/all_to_all | solution.py:352
  40.3 2.2 %collective-permute-start.12 = (bf16[768,384]{1,0:T(8,128)(2,1)S(1)}, bf16[768,384]{1,0:T(8,128)(2,1)}, u32[]{:S(2)}, u32[]{:S(2)}) collective-permute-start(bf16[768,384]{1,0:T(8,128)(2,1)S(1)} %collective-permute-done.1.refs_11_.refs_1_), channel_id=1, source_target_pairs={{0,32},{1,9},{2,34},{3,11},{4,36},{5,13},{6,38},{7,15},{8,40},{9,1... | collective-permute-start | bytes 1769480 | tf_op jit(solution)/shard_map/ppermute | solution.py:29
  42.5 3.3 %collective-permute-done.4.refs_3_ = bf16[2,240,384]{2,1,0:T(8,128)(2,1)S(1)} collective-permute-done((bf16[2,240,384]{2,1,0:T(8,128)(2,1)S(1)}, bf16[2,240,384]{2,1,0:T(8,128)(2,1)S(1)}, u32[]{:S(2)}, u32[]{:S(2)}) %collective-permute-start.4) | collective-permute-done | bytes 368672 | tf_op jit(solution)/shard_map/ppermute | solution.py:29
  49.9 4.6 %collective-permute-done.3.refs_13_.refs_3_ = bf16[768,384]{1,0:T(8,128)(2,1)} collective-permute-done((bf16[768,384]{1,0:T(8,128)(2,1)S(1)}, bf16[768,384]{1,0:T(8,128)(2,1)}, u32[]{:S(2)}, u32[]{:S(2)}) %collective-permute-start.3) | collective-permute-done | bytes 589856 | tf_op jit(solution)/shard_map/ppermute | solution.py:29
  56.9 6.3 %collective-permute-done.16.refs_19_.refs_9_ = bf16[768,384]{1,0:T(8,128)(2,1)S(1)} collective-permute-done((bf16[768,384]{1,0:T(8,128)(2,1)S(1)}, bf16[768,384]{1,0:T(8,128)(2,1)S(1)}, u32[]{:S(2)}, u32[]{:S(2)}) %collective-permute-start.16) | collective-permute-done | bytes 589856 | tf_op jit(solution)/shard_map/ppermute | solution.py:29
  64.4 2.9 %collective-permute-start.14 = (bf16[768,384]{1,0:T(8,128)(2,1)}, bf16[768,384]{1,0:T(8,128)(2,1)}, u32[]{:S(2)}, u32[]{:S(2)}) collective-permute-start(bf16[768,384]{1,0:T(8,128)(2,1)} %collective-permute-done.3.refs_13_.refs_3_), channel_id=1, source_target_pairs={{0,32},{1,9},{2,34},{3,11},{4,36},{5,13},{6,38},{7,15},{8,40},{9,1... | collective-permute-start | bytes 1769480 | tf_op jit(solution)/shard_map/ppermute | solution.py:29
  71.2 3.9 %collective-permute-done.14.refs_17_.refs_7_ = bf16[768,384]{1,0:T(8,128)(2,1)} collective-permute-done((bf16[768,384]{1,0:T(8,128)(2,1)}, bf16[768,384]{1,0:T(8,128)(2,1)}, u32[]{:S(2)}, u32[]{:S(2)}) %collective-permute-start.14) | collective-permute-done | bytes 589856 | tf_op jit(solution)/shard_map/ppermute | solution.py:29
  75.0 6.3 %collective-permute-done.20.refs_23_.refs_13_ = bf16[768,384]{1,0:T(8,128)(2,1)} collective-permute-done((bf16[768,384]{1,0:T(8,128)(2,1)}, bf16[768,384]{1,0:T(8,128)(2,1)}, u32[]{:S(2)}, u32[]{:S(2)}) %collective-permute-start.20) | collective-permute-done | bytes 589856 | tf_op jit(solution)/shard_map/ppermute | solution.py:29
  81.4 3.9 %collective-permute-done.22.refs_25_.refs_15_ = bf16[768,384]{1,0:T(8,128)(2,1)} collective-permute-done((bf16[768,384]{1,0:T(8,128)(2,1)}, bf16[768,384]{1,0:T(8,128)(2,1)}, u32[]{:S(2)}, u32[]{:S(2)}) %collective-permute-start.22) | collective-permute-done | bytes 589856 | tf_op jit(solution)/shard_map/ppermute | solution.py:29
  85.3 11.0 %keys_values.1 = (bf16[2,240,384]{2,1,0:T(8,128)(2,1)}, bf16[2,240,384]{2,1,0:T(8,128)(2,1)}, bf16[2,240,3072]{2,1,0:T(8,128)(2,1)}) custom-call(s32[10]{0:T(128)} %concatenate.26.refs_0_.pos_ref.refs_1_, f32[1,64]{1,0:T(1,128)} %bitcast.42, bf16[2,240,384]{2,1,0:T(8,128)(2,1)} %copy-done.14, bf16[2,240,384]{2,1,0:T(8,128)(2,1)} %copy-done.18, ...), custom_call_target="tpu_custom_call" | custom-call | flops 2264924160 | bytes 7667712 | tf_op jit(solution)/shard_map/keys_values/pallas_call | solution.py:384
  96.3 2.3 %collective-permute-start.23 = (bf16[2,240,384]{2,1,0:T(8,128)(2,1)}, bf16[2,240,384]{2,1,0:T(8,128)(2,1)S(1)}, u32[]{:S(2)}, u32[]{:S(2)}) collective-permute-start(bf16[2,240,384]{2,1,0:T(8,128)(2,1)} %get-tuple-element.39.refs_5_), channel_id=1, source_target_pairs={{0,8},{8,16},{16,24},{24,32},{32,40},{40,48},{48,56},{56,64},{64,7... | collective-permute-start | bytes 1105928 | tf_op jit(solution)/shard_map/ppermute | solution.py:55
  100.8 7.8 %queries.1 = (bf16[2,240,384]{2,1,0:T(8,128)(2,1)}, bf16[3072,384]{1,0:T(8,128)(2,1)}) custom-call(s32[10]{0:T(128)} %concatenate.26.refs_0_.pos_ref.refs_1_, bf16[2,240,3072]{2,1,0:T(8,128)(2,1)} %get-tuple-element.37.x_ref, f32[1,64]{1,0:T(1,128)} %bitcast.43, bf16[768,384]{1,0:T(8,128)(2,1)} %copy-done.5, bf16[768,384]{1,0:T(8,128)(2,1)} %copy-done.6, ...), custom_call_target="tpu_custom_call" | custom-call | flops 1132462080 | bytes 7667712 | tf_op jit(solution)/shard_map/queries/pallas_call | solution.py:403
  108.6 5.4 %collective-permute-start.24 = (bf16[2,240,384]{2,1,0:T(8,128)(2,1)S(1)}, bf16[2,240,384]{2,1,0:T(8,128)(2,1)S(1)}, u32[]{:S(2)}, u32[]{:S(2)}) collective-permute-start(bf16[2,240,384]{2,1,0:T(8,128)(2,1)S(1)} %collective-permute-done.23.refs_3_), channel_id=1, source_target_pairs={{0,8},{8,16},{16,24},{24,32},{32,40},{40,48},{48,56},{56,64},{64,7... | collective-permute-start | bytes 1105928 | tf_op jit(solution)/shard_map/ppermute | solution.py:55
  116.0 3.0 %collective-permute-start.26 = (bf16[2,240,384]{2,1,0:T(8,128)(2,1)S(1)}, bf16[2,240,384]{2,1,0:T(8,128)(2,1)S(1)}, u32[]{:S(2)}, u32[]{:S(2)}) collective-permute-start(bf16[2,240,384]{2,1,0:T(8,128)(2,1)S(1)} %collective-permute-done.25.refs_4_), channel_id=1, source_target_pairs={{0,8},{8,16},{16,24},{24,32},{32,40},{40,48},{48,56},{56,64},{64,7... | collective-permute-start | bytes 1105928 | tf_op jit(solution)/shard_map/ppermute | solution.py:55
  120.4 8.6 %attention_near.1 = (f32[2,240,384]{2,1,0:T(8,128)S(1)}, f32[2,240,384]{2,1,0:T(8,128)S(1)}, f32[2,240,384]{2,1,0:T(8,128)S(1)}) custom-call(s32[32,3]{1,0:T(8,128)S(1)} %copy.75.refs_0_, s32[10]{0:T(128)S(1)} %copy-done, bf16[2,240,384]{2,1,0:T(8,128)(2,1)S(1)} %copy-done.4, bf16[2,240,384]{2,1,0:T(8,128)(2,1)S(1)} %collective-permute-done.23.refs_3_, ...), custom_call_target="tpu_custom_call" | custom-call | flops 4529848320 | bytes 6291456 | tf_op jit(solution)/shard_map/attention_near/pallas_call | solution.py:419
  131.0 3.9 %collective-permute-done.30.refs_6_ = bf16[2,240,384]{2,1,0:T(8,128)(2,1)S(1)} collective-permute-done((bf16[2,240,384]{2,1,0:T(8,128)(2,1)S(1)}, bf16[2,240,384]{2,1,0:T(8,128)(2,1)S(1)}, u32[]{:S(2)}, u32[]{:S(2)}) %collective-permute-start.30) | collective-permute-done | bytes 368672 | tf_op jit(solution)/shard_map/ppermute | solution.py:55
  134.9 5.9 %attention_far.1.refs_1_ = bf16[2,240,384]{2,1,0:T(8,128)(2,1)S(1)} custom-call(s32[32,3]{1,0:T(8,128)S(1)} %copy.75.refs_0_, s32[10]{0:T(128)S(1)} %copy-done, bf16[2,240,384]{2,1,0:T(8,128)(2,1)S(1)} %copy-done.4, bf16[2,240,384]{2,1,0:T(8,128)(2,1)S(1)} %collective-permute-done.24.refs_3_, bf16[2,240,384]{2,1,0:T(8,128)(2,1)S(1)} %collective-permute-done.26.refs_4_, ...), custom_call_target="tpu_custom_call" | custom-call | flops 2264924160 | bytes 6291456 | tf_op jit(solution)/shard_map/attention_far/pallas_call | solution.py:435
  140.9 2.5 %out_projection.1 = (bf16[8,225,384]{2,1,0:T(8,128)(2,1)S(1)}, bf16[8,225,384]{2,1,0:T(8,128)(2,1)S(1)}) custom-call(s32[10]{0:T(128)S(1)} %copy-done, bf16[2,240,384]{2,1,0:T(8,128)(2,1)S(1)} %attention_far.1.refs_1_, bf16[3072,384]{1,0:T(8,128)(2,1)S(1)} %copy-done.1), custom_call_target="tpu_custom_call" | custom-call | flops 1132462080 | bytes 5308416 | tf_op jit(solution)/shard_map/out_projection/pallas_call | solution.py:451
  143.7 3.1 %collective-permute-done.31 = bf16[8,225,384]{2,0,1:T(8,128)(2,1)S(1)} collective-permute-done((bf16[8,225,384]{2,0,1:T(8,128)(2,1)S(1)}, bf16[8,225,384]{2,0,1:T(8,128)(2,1)S(1)}, u32[]{:S(2)}, u32[]{:S(2)}) %collective-permute-start.31) | collective-permute-done | bytes 1382432 | tf_op jit(solution)/shard_map/ppermute | solution.py:50
  150.0 2.2 %collective-permute-start.32 = (bf16[2,225,384]{2,1,0:T(8,128)(2,1)S(1)}, bf16[2,225,384]{2,1,0:T(8,128)(2,1)S(1)}, u32[]{:S(2)}, u32[]{:S(2)}) collective-permute-start(bf16[2,225,384]{2,1,0:T(8,128)(2,1)S(1)} %get-tuple-element.47), channel_id=1, source_target_pairs={{0,6},{1,3},{2,0},{3,5},{4,2},{5,7},{6,4},{7,1},{8,14},{9,11},{10,... | collective-permute-start | bytes 1036808 | tf_op jit(solution)/shard_map/ppermute | solution.py:29
  152.2 6.9 %collective-permute-done.33 = bf16[2,225,384]{2,1,0:T(8,128)(2,1)S(1)} collective-permute-done((bf16[2,225,384]{2,1,0:T(8,128)(2,1)S(1)}, bf16[2,225,384]{2,1,0:T(8,128)(2,1)S(1)}, u32[]{:S(2)}, u32[]{:S(2)}) %collective-permute-start.33) | collective-permute-done | bytes 345632 | tf_op jit(solution)/shard_map/ppermute | solution.py:29
  160.8 8.3 %collective-permute-done.34 = bf16[2,225,384]{2,1,0:T(8,128)(2,1)S(1)} collective-permute-done((bf16[2,225,384]{2,1,0:T(8,128)(2,1)}, bf16[2,225,384]{2,1,0:T(8,128)(2,1)S(1)}, u32[]{:S(2)}, u32[]{:S(2)}) %collective-permute-start.34) | collective-permute-done | bytes 345632 | tf_op jit(solution)/shard_map/ppermute | solution.py:29
  (146 shorter events, 46.0 us)
Async XLA Ops:
  2.2 30.3 %collective-permute-start.1 = (bf16[768,384]{1,0:T(8,128)(2,1)S(1)}, bf16[768,384]{1,0:T(8,128)(2,1)S(1)}, u32[]{:S(2)}, u32[]{:S(2)}) collective-permute-start(bf16[768,384]{1,0:T(8,128)(2,1)S(1)} %pad_maximum_fusion.refs_10_.refs_0_), channel_id=1, source_target_pairs={{0,8},{1,33},{2,10},{3,35},{4,12},{5,37},{6,14},{7,39},{8,16},{9,4... | collective-permute-start | bytes 1769480 | tf_op jit(solution)/shard_map/ppermute | solution.py:29
  2.5 30.0 %collective-permute-start.2 = (bf16[768,384]{1,0:T(8,128)(2,1)S(1)}, bf16[768,384]{1,0:T(8,128)(2,1)S(1)}, u32[]{:S(2)}, u32[]{:S(2)}) collective-permute-start(bf16[768,384]{1,0:T(8,128)(2,1)S(1)} %pad_maximum_fusion.refs_10_.refs_0_), channel_id=1, source_target_pairs={{0,24},{1,97},{2,26},{3,99},{4,28},{5,101},{6,30},{7,103},{8,0},{9... | collective-permute-start | bytes 1769480 | tf_op jit(solution)/shard_map/ppermute | solution.py:29
  5.1 11.2 %all-to-all-start = ((s32[16,2,3]{2,1,0:T(2,128)}), s32[16,2,3]{2,1,0:T(2,128)S(1)}, u32[]{:S(2)}, u32[]{:S(2)}) async-start(s32[16,2,3]{2,1,0:T(2,128)} %broadcast_in_dim.49), calls=%async_computation | async-start | bytes 32768 | tf_op jit(solution)/shard_map/all_to_all | solution.py:74
  17.9 12.3 %collective-permute-start = (bf16[225,384]{1,0:T(8,128)(2,1)S(1)}, bf16[225,384]{1,0:T(8,128)(2,1)S(1)}, u32[]{:S(2)}, u32[]{:S(2)}) collective-permute-start(bf16[225,384]{1,0:T(8,128)(2,1)S(1)} %bitcast.38), channel_id=1, source_target_pairs={{0,120},{8,0},{16,8},{24,16},{32,24},{40,32},{48,40},{56,48},{64,5... | collective-permute-start | bytes 518408 | tf_op jit(solution)/shard_map/ppermute | solution.py:55
  19.4 13.1 %all-to-all-start.1 = ((f32[16,2,1152]{2,1,0:T(2,128)}), f32[16,2,1152]{2,1,0:T(2,128)}, u32[]{:S(2)}, u32[]{:S(2)}) async-start(f32[16,2,1152]{2,1,0:T(2,128)} %reshape.58), calls=%async_computation.1 | async-start | bytes 294912 | tf_op jit(solution)/shard_map/all_to_all | solution.py:352
  28.2 12.1 %collective-permute-start.11 = (bf16[768,384]{1,0:T(8,128)(2,1)S(1)}, bf16[768,384]{1,0:T(8,128)(2,1)S(1)}, u32[]{:S(2)}, u32[]{:S(2)}) collective-permute-start(bf16[768,384]{1,0:T(8,128)(2,1)S(1)} %pad_maximum_fusion.refs_10_.refs_0_), channel_id=1, source_target_pairs={{0,32},{1,9},{2,34},{3,11},{4,36},{5,13},{6,38},{7,15},{8,40},{9,1... | collective-permute-start | bytes 1769480 | tf_op jit(solution)/shard_map/ppermute | solution.py:29
  28.7 13.8 %collective-permute-start.15 = (bf16[768,384]{1,0:T(8,128)(2,1)S(1)}, bf16[768,384]{1,0:T(8,128)(2,1)S(1)}, u32[]{:S(2)}, u32[]{:S(2)}) collective-permute-start(bf16[768,384]{1,0:T(8,128)(2,1)S(1)} %pad_maximum_fusion.refs_10_.refs_0_), channel_id=1, source_target_pairs={{0,96},{1,25},{2,98},{3,27},{4,100},{5,29},{6,102},{7,31},{8,104},... | collective-permute-start | bytes 1769480 | tf_op jit(solution)/shard_map/ppermute | solution.py:29
  33.9 11.9 %collective-permute-start.4 = (bf16[2,240,384]{2,1,0:T(8,128)(2,1)S(1)}, bf16[2,240,384]{2,1,0:T(8,128)(2,1)S(1)}, u32[]{:S(2)}, u32[]{:S(2)}) collective-permute-start(bf16[2,240,384]{2,1,0:T(8,128)(2,1)S(1)} %dynamic_update_slice.3.refs_2_), channel_id=1, source_target_pairs={{0,2},{1,7},{2,4},{3,1},{4,6},{5,3},{6,0},{7,5},{8,10},{9,15},{10,... | collective-permute-start | bytes 1105928 | tf_op jit(solution)/shard_map/ppermute | solution.py:29
  38.1 16.4 %collective-permute-start.3 = (bf16[768,384]{1,0:T(8,128)(2,1)S(1)}, bf16[768,384]{1,0:T(8,128)(2,1)}, u32[]{:S(2)}, u32[]{:S(2)}) collective-permute-start(bf16[768,384]{1,0:T(8,128)(2,1)S(1)} %collective-permute-done.1.refs_11_.refs_1_), channel_id=1, source_target_pairs={{0,8},{1,33},{2,10},{3,35},{4,12},{5,37},{6,14},{7,39},{8,16},{9,4... | collective-permute-start | bytes 1769480 | tf_op jit(solution)/shard_map/ppermute | solution.py:29
  40.3 14.2 %collective-permute-start.12 = (bf16[768,384]{1,0:T(8,128)(2,1)S(1)}, bf16[768,384]{1,0:T(8,128)(2,1)}, u32[]{:S(2)}, u32[]{:S(2)}) collective-permute-start(bf16[768,384]{1,0:T(8,128)(2,1)S(1)} %collective-permute-done.1.refs_11_.refs_1_), channel_id=1, source_target_pairs={{0,32},{1,9},{2,34},{3,11},{4,36},{5,13},{6,38},{7,15},{8,40},{9,1... | collective-permute-start | bytes 1769480 | tf_op jit(solution)/shard_map/ppermute | solution.py:29
  46.7 16.6 %collective-permute-start.16 = (bf16[768,384]{1,0:T(8,128)(2,1)S(1)}, bf16[768,384]{1,0:T(8,128)(2,1)S(1)}, u32[]{:S(2)}, u32[]{:S(2)}) collective-permute-start(bf16[768,384]{1,0:T(8,128)(2,1)S(1)} %collective-permute-done.1.refs_11_.refs_1_), channel_id=1, source_target_pairs={{0,96},{1,25},{2,98},{3,27},{4,100},{5,29},{6,102},{7,31},{8,104},... | collective-permute-start | bytes 1769480 | tf_op jit(solution)/shard_map/ppermute | solution.py:29
  48.1 15.1 %collective-permute-start.13 = (bf16[768,384]{1,0:T(8,128)(2,1)S(1)}, bf16[768,384]{1,0:T(8,128)(2,1)S(1)}, u32[]{:S(2)}, u32[]{:S(2)}) collective-permute-start(bf16[768,384]{1,0:T(8,128)(2,1)S(1)} %collective-permute-done.2.refs_12_.refs_2_), channel_id=1, source_target_pairs={{0,32},{1,9},{2,34},{3,11},{4,36},{5,13},{6,38},{7,15},{8,40},{9,1... | collective-permute-start | bytes 1769480 | tf_op jit(solution)/shard_map/ppermute | solution.py:29
  54.5 15.2 %collective-permute-start.18 = (bf16[768,384]{1,0:T(8,128)(2,1)}, bf16[768,384]{1,0:T(8,128)(2,1)}, u32[]{:S(2)}, u32[]{:S(2)}) collective-permute-start(bf16[768,384]{1,0:T(8,128)(2,1)} %collective-permute-done.3.refs_13_.refs_3_), channel_id=1, source_target_pairs={{0,96},{1,25},{2,98},{3,27},{4,100},{5,29},{6,102},{7,31},{8,104},... | collective-permute-start | bytes 1769480 | tf_op jit(solution)/shard_map/ppermute | solution.py:29
  67.3 14.0 %collective-permute-start.20 = (bf16[768,384]{1,0:T(8,128)(2,1)}, bf16[768,384]{1,0:T(8,128)(2,1)}, u32[]{:S(2)}, u32[]{:S(2)}) collective-permute-start(bf16[768,384]{1,0:T(8,128)(2,1)} %collective-permute-done.12.refs_15_.refs_5_), channel_id=1, source_target_pairs={{0,32},{1,9},{2,34},{3,11},{4,36},{5,13},{6,38},{7,15},{8,40},{9,1... | collective-permute-start | bytes 1769480 | tf_op jit(solution)/shard_map/ppermute | solution.py:29
  67.7 13.7 %collective-permute-start.21 = (bf16[768,384]{1,0:T(8,128)(2,1)S(1)}, bf16[768,384]{1,0:T(8,128)(2,1)}, u32[]{:S(2)}, u32[]{:S(2)}) collective-permute-start(bf16[768,384]{1,0:T(8,128)(2,1)S(1)} %collective-permute-done.17.refs_20_.refs_10_), channel_id=1, source_target_pairs={{0,96},{1,25},{2,98},{3,27},{4,100},{5,29},{6,102},{7,31},{8,104},... | collective-permute-start | bytes 1769480 | tf_op jit(solution)/shard_map/ppermute | solution.py:29
  69.7 15.6 %collective-permute-start.22 = (bf16[768,384]{1,0:T(8,128)(2,1)}, bf16[768,384]{1,0:T(8,128)(2,1)}, u32[]{:S(2)}, u32[]{:S(2)}) collective-permute-start(bf16[768,384]{1,0:T(8,128)(2,1)} %collective-permute-done.18.refs_21_.refs_11_), channel_id=1, source_target_pairs={{0,96},{1,25},{2,98},{3,27},{4,100},{5,29},{6,102},{7,31},{8,104},... | collective-permute-start | bytes 1769480 | tf_op jit(solution)/shard_map/ppermute | solution.py:29
  96.3 12.3 %collective-permute-start.23 = (bf16[2,240,384]{2,1,0:T(8,128)(2,1)}, bf16[2,240,384]{2,1,0:T(8,128)(2,1)S(1)}, u32[]{:S(2)}, u32[]{:S(2)}) collective-permute-start(bf16[2,240,384]{2,1,0:T(8,128)(2,1)} %get-tuple-element.39.refs_5_), channel_id=1, source_target_pairs={{0,8},{8,16},{16,24},{24,32},{32,40},{40,48},{48,56},{56,64},{64,7... | collective-permute-start | bytes 1105928 | tf_op jit(solution)/shard_map/ppermute | solution.py:55
  98.6 17.4 %collective-permute-start.25 = (bf16[2,240,384]{2,1,0:T(8,128)(2,1)}, bf16[2,240,384]{2,1,0:T(8,128)(2,1)S(1)}, u32[]{:S(2)}, u32[]{:S(2)}) collective-permute-start(bf16[2,240,384]{2,1,0:T(8,128)(2,1)} %get-tuple-element.40.refs_6_), channel_id=1, source_target_pairs={{0,8},{8,16},{16,24},{24,32},{32,40},{40,48},{48,56},{56,64},{64,7... | collective-permute-start | bytes 1105928 | tf_op jit(solution)/shard_map/ppermute | solution.py:55
  98.7 20.4 %collective-permute-start.27 = (bf16[2,240,384]{2,1,0:T(8,128)(2,1)}, bf16[2,240,384]{2,1,0:T(8,128)(2,1)S(1)}, u32[]{:S(2)}, u32[]{:S(2)}) collective-permute-start(bf16[2,240,384]{2,1,0:T(8,128)(2,1)} %get-tuple-element.39.refs_5_), channel_id=1, source_target_pairs={{0,120},{8,0},{16,8},{24,16},{32,24},{40,32},{48,40},{56,48},{64,5... | collective-permute-start | bytes 1105928 | tf_op jit(solution)/shard_map/ppermute | solution.py:55
  100.6 18.5 %collective-permute-start.29 = (bf16[2,240,384]{2,1,0:T(8,128)(2,1)}, bf16[2,240,384]{2,1,0:T(8,128)(2,1)S(1)}, u32[]{:S(2)}, u32[]{:S(2)}) collective-permute-start(bf16[2,240,384]{2,1,0:T(8,128)(2,1)} %get-tuple-element.40.refs_6_), channel_id=1, source_target_pairs={{0,120},{8,0},{16,8},{24,16},{32,24},{40,32},{48,40},{56,48},{64,5... | collective-permute-start | bytes 1105928 | tf_op jit(solution)/shard_map/ppermute | solution.py:55
  108.6 20.4 %collective-permute-start.24 = (bf16[2,240,384]{2,1,0:T(8,128)(2,1)S(1)}, bf16[2,240,384]{2,1,0:T(8,128)(2,1)S(1)}, u32[]{:S(2)}, u32[]{:S(2)}) collective-permute-start(bf16[2,240,384]{2,1,0:T(8,128)(2,1)S(1)} %collective-permute-done.23.refs_3_), channel_id=1, source_target_pairs={{0,8},{8,16},{16,24},{24,32},{32,40},{40,48},{48,56},{56,64},{64,7... | collective-permute-start | bytes 1105928 | tf_op jit(solution)/shard_map/ppermute | solution.py:55
  116.0 13.6 %collective-permute-start.26 = (bf16[2,240,384]{2,1,0:T(8,128)(2,1)S(1)}, bf16[2,240,384]{2,1,0:T(8,128)(2,1)S(1)}, u32[]{:S(2)}, u32[]{:S(2)}) collective-permute-start(bf16[2,240,384]{2,1,0:T(8,128)(2,1)S(1)} %collective-permute-done.25.refs_4_), channel_id=1, source_target_pairs={{0,8},{8,16},{16,24},{24,32},{32,40},{40,48},{48,56},{56,64},{64,7... | collective-permute-start | bytes 1105928 | tf_op jit(solution)/shard_map/ppermute | solution.py:55
  119.1 11.9 %collective-permute-start.28 = (bf16[2,240,384]{2,1,0:T(8,128)(2,1)S(1)}, bf16[2,240,384]{2,1,0:T(8,128)(2,1)S(1)}, u32[]{:S(2)}, u32[]{:S(2)}) collective-permute-start(bf16[2,240,384]{2,1,0:T(8,128)(2,1)S(1)} %collective-permute-done.27.refs_7_), channel_id=1, source_target_pairs={{0,120},{8,0},{16,8},{24,16},{32,24},{40,32},{48,40},{56,48},{64,5... | collective-permute-start | bytes 1105928 | tf_op jit(solution)/shard_map/ppermute | solution.py:55
  119.1 15.9 %collective-permute-start.30 = (bf16[2,240,384]{2,1,0:T(8,128)(2,1)S(1)}, bf16[2,240,384]{2,1,0:T(8,128)(2,1)S(1)}, u32[]{:S(2)}, u32[]{:S(2)}) collective-permute-start(bf16[2,240,384]{2,1,0:T(8,128)(2,1)S(1)} %collective-permute-done.29.refs_8_), channel_id=1, source_target_pairs={{0,120},{8,0},{16,8},{24,16},{32,24},{40,32},{48,40},{56,48},{64,5... | collective-permute-start | bytes 1105928 | tf_op jit(solution)/shard_map/ppermute | solution.py:55
  (39 other events, 615.8 us)

commit v5 on v4

--- a/solution.py
+++ b/solution.py
@@ -106,12 +106,14 @@
     return (centered * lax.rsqrt(spread + 1e-06) * gain).astype(jnp.bfloat16)
 
 
-def modulate(tokens, pos_ref, own_refs, other_refs, out_ref):
+def modulate(tokens, pos_ref, own_refs, other_refs, out_ref, arriving):
     width = own_refs[0].shape[2]
     z = pos_ref[4]
     core = pos_ref[5]
     way = pos_ref[6]
     for slot in range(2):
+        for copy in arriving[slot]:
+            copy.wait()
         total = jnp.zeros((tokens, width), jnp.float32)
         square = jnp.zeros((tokens, width), jnp.float32)
         for ref in (*own_refs, *other_refs):
@@ -144,9 +146,13 @@
     k_ref, v_ref, x_ref, held, modulated, weight, held_sems, x_sem, sems = refs[24:]
     states = [held.at[part] for part in range(8)]
     arriving = [
-        pltpu.make_async_copy(given[part], states[part], held_sems.at[part]) for part in range(8)
+        [
+            pltpu.make_async_copy(given[part].at[slot], states[part].at[slot], held_sems.at[slot, part])
+            for part in range(8)
+        ]
+        for slot in range(2)
     ]
-    for copy in arriving:
+    for copy in sum(arriving, []):
         copy.start()
     copies = [
         shard_copies(shard_places(shards, part * 192), pos_ref, weight, part * 384, sems.at[part])
@@ -154,9 +160,7 @@
     ]
     for copy in sum(copies, []):
         copy.start()
-    for copy in arriving:
-        copy.wait()
-    modulate(tokens, pos_ref, states[:SIDE], states[SIDE:], modulated)
+    modulate(tokens, pos_ref, states[:SIDE], states[SIDE:], modulated, arriving)
     x_copy = pltpu.make_async_copy(modulated, x_ref, x_sem)
     x_copy.start()
     x = modulated[...].reshape(2 * PADDED, D)
@@ -273,12 +277,12 @@
         out_ref[slot] = (mix / total).astype(jnp.bfloat16)
 
 
-def out_kernel(tokens, pos_ref, x_ref, weight, keep_ref, send_ref):
+def out_kernel(tokens, pos_ref, x_ref, weight, keep_ref, near_ref, far_ref):
     x = x_ref[...].reshape(2 * PADDED, 384)
     z = pos_ref[4]
     core = pos_ref[5]
     way = pos_ref[6]
-    for ref, at_core, along in ((send_ref, 1 - core, -way), (keep_ref, core, way)):
+    for refs, at_core, along in (((near_ref, far_ref), 1 - core, -way), ((keep_ref,), core, way)):
         for hop in range(SIDE):
             owner = wrap(z, hop * along) * 2 + at_core
             rows = weight[pl.ds(pl.multiple_of(owner * 384, 384), 384), :]
@@ -286,7 +290,8 @@
                 x, rows, (((1,), (1,)), ((), ())), preferred_element_type=jnp.float32
             ).astype(jnp.bfloat16)
             for slot in range(2):
-                ref[2 * hop + slot] = part[slot * PADDED : slot * PADDED + tokens]
+                ref, at = (refs[0], hop) if len(refs) == 1 else (refs[hop // 2], hop % 2)
+                ref[2 * at + slot] = part[slot * PADDED : slot * PADDED + tokens]
 
 
 SMEM = pl.BlockSpec(memory_space=pltpu.SMEM)
@@ -390,7 +395,7 @@
             pltpu.VMEM((8, 2, PADDED, width), jnp.bfloat16),
             pltpu.VMEM((2, PADDED, D), jnp.bfloat16),
             pltpu.VMEM((D, 2 * width), jnp.bfloat16),
-            pltpu.SemaphoreType.DMA((8,)),
+            pltpu.SemaphoreType.DMA((2, 8)),
             pltpu.SemaphoreType.DMA,
             pltpu.SemaphoreType.DMA((2, 16)),
         ],
@@ -448,9 +453,9 @@
             flops=6 * 3 * 4 * 480 * 256 * 256, bytes_accessed=6 << 20, transcendentals=18 * 480 * 256
         ),
     )(plan, pos, queries, far_kv[0], far_kv[2], far_kv[1], far_kv[3], mix, total, top)
-    keep, send = call(
+    keep, send_near, send_far = call(
         lambda *refs: out_kernel(tokens, *refs),
-        [struct((2 * SIDE, tokens, width))] * 2,
+        [struct((2 * SIDE, tokens, width))] + [struct((SIDE, tokens, width))] * 2,
         [SMEM, VMEM, VMEM],
         [],
         "out_projection",
@@ -458,15 +463,17 @@
         D * width * 2 + PADDED * D * 4,
     )(pos, mixed, out_whole)
 
-    swapped = other_core(send)
-    chip = [
-        keep[2 * hop : 2 * hop + 2].astype(jnp.float32) + swapped[2 * hop : 2 * hop + 2].astype(jnp.float32)
-        for hop in range(SIDE)
-    ]
-    onward = z_step(chip[2].astype(jnp.bfloat16), 1)
-    back = z_step(chip[3].astype(jnp.bfloat16), -1)
-    forth = z_step((chip[1] + onward.astype(jnp.float32)).astype(jnp.bfloat16), 1)
-    attended = chip[0] + back.astype(jnp.float32) + forth.astype(jnp.float32)
+    swapped_far = other_core(send_far)
+    swapped_near = other_core(send_near)
+
+    def on_chip(hop):
+        swapped = (swapped_near, swapped_far)[hop // 2][hop % 2 * 2 : hop % 2 * 2 + 2]
+        return keep[2 * hop : 2 * hop + 2].astype(jnp.float32) + swapped.astype(jnp.float32)
+
+    onward = z_step(on_chip(2).astype(jnp.bfloat16), 1)
+    back = z_step(on_chip(3).astype(jnp.bfloat16), -1)
+    forth = z_step((on_chip(1) + onward.astype(jnp.float32)).astype(jnp.bfloat16), 1)
+    attended = on_chip(0) + back.astype(jnp.float32) + forth.astype(jnp.float32)
     gate = mods[:, None, 2 * width :]
     updated = (states.astype(jnp.float32) + gate * attended).astype(jnp.bfloat16)
     spare = (first_slot + jnp.arange(2) == slots)[:, None, None]

time: 171 us -> 169 us (0.988)
  waiting for transfers between devices: 60.8 us -> 58.5 us
    ppermute x5 -> x6, waiting for transfers between devices: 3.13 us -> 1.3 us  [other_core(): return lax.ppermute(array, 'row', pairs)]
  transfers between devices with their start and end apart: 37 -> 38, of which waited for: 18 -> 18; matrix products, arithmetic and copies ran while one was open for 4% -> 5% of each run, Pallas kernels for 10% -> 10%
where the time goes in v5:
time: 169 us; the launch traced here: 168 us
  starting transfers between devices  59.7 us (35%)
  waiting for transfers between devices  58.5 us (35%)
  Pallas kernels  35.2 us (21%)
  local copies, waits for them, and re-layouts  9.71 us (6%)
  other arithmetic  4.47 us (3%)
    ppermute x21, waiting for transfers between devices, torus_step(): return lax.ppermute(array, ('frame', 'row'), pairs)  44.2 us
    ppermute x21, starting transfers between devices, torus_step(): return lax.ppermute(array, ('frame', 'row'), pairs)  28.9 us
    ppermute x9, starting transfers between devices, next_frame(): lax.ppermute(array, 'frame', [(i, (i + by) % peers) for i in range(peers)])  13.7 us
    pallas_call x1, Pallas kernels, per_device(): pl.pallas_call(lambda *refs: key_value_kernel(tokens, *refs), out_shape=[...  10.3 us
    all_to_all x1, starting transfers between devices, per_device(): lax.all_to_all(sums.reshape(slots // 2, 2, 3 * width), 'frame', 0, 0, til...  8.76 us
    pallas_call x1, Pallas kernels, per_device(): pl.pallas_call(lambda *refs: near_kernel(tokens, *refs), out_shape=[struc...  8.62 us
    ppermute x9, waiting for transfers between devices, next_frame(): lax.ppermute(array, 'frame', [(i, (i + by) % peers) for i in range(peers)])  7.95 us
    pallas_call x1, Pallas kernels, per_device(): call(query_kernel, [struct((2, PADDED, width)), struct((D, width))], [SME...  7.83 us
  transfers between devices with their start and end apart: 38, of which 18 were waited for; matrix products, arithmetic and copies ran while one was open for 5% of the time, Pallas kernels for 10%

profile of v5, /device:TPU:30, one launch (start us, length us, event | category | flops | bytes accessed | tf_op | source)
XLA Modules:
  0.0 168.2 jit_solution(1761377933184166919)
XLA Ops:
  5.1 7.1 %all-to-all-start = ((s32[16,2,3]{2,1,0:T(2,128)}), s32[16,2,3]{2,1,0:T(2,128)S(1)}, u32[]{:S(2)}, u32[]{:S(2)}) async-start(s32[16,2,3]{2,1,0:T(2,128)} %broadcast_in_dim.49), calls=%async_computation | async-start | bytes 32768 | tf_op jit(solution)/shard_map/all_to_all | solution.py:74
  12.8 3.5 %all-to-all-done = s32[16,2,3]{2,1,0:T(2,128)S(1)} async-done(((s32[16,2,3]{2,1,0:T(2,128)}), s32[16,2,3]{2,1,0:T(2,128)S(1)}, u32[]{:S(2)}, u32[]{:S(2)}) %all-to-all-start) | async-done | bytes 416 | tf_op jit(solution)/shard_map/all_to_all | solution.py:74
  19.4 8.8 %all-to-all-start.1 = ((f32[16,2,1152]{2,1,0:T(2,128)}), f32[16,2,1152]{2,1,0:T(2,128)}, u32[]{:S(2)}, u32[]{:S(2)}) async-start(f32[16,2,1152]{2,1,0:T(2,128)} %reshape.58), calls=%async_computation.1 | async-start | bytes 294912 | tf_op jit(solution)/shard_map/all_to_all | solution.py:357
  35.9 2.2 %collective-permute-start.5 = (bf16[2,240,384]{2,1,0:T(8,128)(2,1)S(1)}, bf16[2,240,384]{2,1,0:T(8,128)(2,1)S(1)}, u32[]{:S(2)}, u32[]{:S(2)}) collective-permute-start(bf16[2,240,384]{2,1,0:T(8,128)(2,1)S(1)} %dynamic_update_slice.3.refs_2_), channel_id=1, source_target_pairs={{0,6},{1,3},{2,0},{3,5},{4,2},{5,7},{6,4},{7,1},{8,14},{9,11},{10,... | collective-permute-start | bytes 1105928 | tf_op jit(solution)/shard_map/ppermute | solution.py:29
  40.3 2.2 %collective-permute-start.12 = (bf16[768,384]{1,0:T(8,128)(2,1)S(1)}, bf16[768,384]{1,0:T(8,128)(2,1)}, u32[]{:S(2)}, u32[]{:S(2)}) collective-permute-start(bf16[768,384]{1,0:T(8,128)(2,1)S(1)} %collective-permute-done.1.refs_11_.refs_1_), channel_id=1, source_target_pairs={{0,32},{1,9},{2,34},{3,11},{4,36},{5,13},{6,38},{7,15},{8,40},{9,1... | collective-permute-start | bytes 1769480 | tf_op jit(solution)/shard_map/ppermute | solution.py:29
  42.5 3.3 %collective-permute-done.4.refs_3_ = bf16[2,240,384]{2,1,0:T(8,128)(2,1)S(1)} collective-permute-done((bf16[2,240,384]{2,1,0:T(8,128)(2,1)S(1)}, bf16[2,240,384]{2,1,0:T(8,128)(2,1)S(1)}, u32[]{:S(2)}, u32[]{:S(2)}) %collective-permute-start.4) | collective-permute-done | bytes 368672 | tf_op jit(solution)/shard_map/ppermute | solution.py:29
  49.9 4.6 %collective-permute-done.3.refs_13_.refs_3_ = bf16[768,384]{1,0:T(8,128)(2,1)} collective-permute-done((bf16[768,384]{1,0:T(8,128)(2,1)S(1)}, bf16[768,384]{1,0:T(8,128)(2,1)}, u32[]{:S(2)}, u32[]{:S(2)}) %collective-permute-start.3) | collective-permute-done | bytes 589856 | tf_op jit(solution)/shard_map/ppermute | solution.py:29
  56.9 6.3 %collective-permute-done.16.refs_19_.refs_9_ = bf16[768,384]{1,0:T(8,128)(2,1)S(1)} collective-permute-done((bf16[768,384]{1,0:T(8,128)(2,1)S(1)}, bf16[768,384]{1,0:T(8,128)(2,1)S(1)}, u32[]{:S(2)}, u32[]{:S(2)}) %collective-permute-start.16) | collective-permute-done | bytes 589856 | tf_op jit(solution)/shard_map/ppermute | solution.py:29
  64.4 2.9 %collective-permute-start.14 = (bf16[768,384]{1,0:T(8,128)(2,1)}, bf16[768,384]{1,0:T(8,128)(2,1)}, u32[]{:S(2)}, u32[]{:S(2)}) collective-permute-start(bf16[768,384]{1,0:T(8,128)(2,1)} %collective-permute-done.3.refs_13_.refs_3_), channel_id=1, source_target_pairs={{0,32},{1,9},{2,34},{3,11},{4,36},{5,13},{6,38},{7,15},{8,40},{9,1... | collective-permute-start | bytes 1769480 | tf_op jit(solution)/shard_map/ppermute | solution.py:29
  71.2 3.9 %collective-permute-done.14.refs_17_.refs_7_ = bf16[768,384]{1,0:T(8,128)(2,1)} collective-permute-done((bf16[768,384]{1,0:T(8,128)(2,1)}, bf16[768,384]{1,0:T(8,128)(2,1)}, u32[]{:S(2)}, u32[]{:S(2)}) %collective-permute-start.14) | collective-permute-done | bytes 589856 | tf_op jit(solution)/shard_map/ppermute | solution.py:29
  75.0 6.3 %collective-permute-done.20.refs_23_.refs_13_ = bf16[768,384]{1,0:T(8,128)(2,1)} collective-permute-done((bf16[768,384]{1,0:T(8,128)(2,1)}, bf16[768,384]{1,0:T(8,128)(2,1)}, u32[]{:S(2)}, u32[]{:S(2)}) %collective-permute-start.20) | collective-permute-done | bytes 589856 | tf_op jit(solution)/shard_map/ppermute | solution.py:29
  81.4 3.9 %collective-permute-done.22.refs_25_.refs_15_ = bf16[768,384]{1,0:T(8,128)(2,1)} collective-permute-done((bf16[768,384]{1,0:T(8,128)(2,1)}, bf16[768,384]{1,0:T(8,128)(2,1)}, u32[]{:S(2)}, u32[]{:S(2)}) %collective-permute-start.22) | collective-permute-done | bytes 589856 | tf_op jit(solution)/shard_map/ppermute | solution.py:29
  85.3 10.3 %keys_values.1 = (bf16[2,240,384]{2,1,0:T(8,128)(2,1)}, bf16[2,240,384]{2,1,0:T(8,128)(2,1)}, bf16[2,240,3072]{2,1,0:T(8,128)(2,1)}) custom-call(s32[10]{0:T(128)} %concatenate.26.refs_0_.pos_ref.refs_1_, f32[1,64]{1,0:T(1,128)} %bitcast.42, bf16[2,240,384]{2,1,0:T(8,128)(2,1)} %copy-done.14, bf16[2,240,384]{2,1,0:T(8,128)(2,1)} %copy-done.18, ...), custom_call_target="tpu_custom_call" | custom-call | flops 2264924160 | bytes 7667712 | tf_op jit(solution)/shard_map/keys_values/pallas_call | solution.py:389
  95.6 2.3 %collective-permute-start.23 = (bf16[2,240,384]{2,1,0:T(8,128)(2,1)}, bf16[2,240,384]{2,1,0:T(8,128)(2,1)S(1)}, u32[]{:S(2)}, u32[]{:S(2)}) collective-permute-start(bf16[2,240,384]{2,1,0:T(8,128)(2,1)} %get-tuple-element.40.refs_5_), channel_id=1, source_target_pairs={{0,8},{8,16},{16,24},{24,32},{32,40},{40,48},{48,56},{56,64},{64,7... | collective-permute-start | bytes 1105928 | tf_op jit(solution)/shard_map/ppermute | solution.py:55
  100.0 7.8 %queries.1 = (bf16[2,240,384]{2,1,0:T(8,128)(2,1)}, bf16[3072,384]{1,0:T(8,128)(2,1)}) custom-call(s32[10]{0:T(128)} %concatenate.26.refs_0_.pos_ref.refs_1_, bf16[2,240,3072]{2,1,0:T(8,128)(2,1)} %get-tuple-element.38.x_ref, f32[1,64]{1,0:T(1,128)} %bitcast.43, bf16[768,384]{1,0:T(8,128)(2,1)} %copy-done.5, bf16[768,384]{1,0:T(8,128)(2,1)} %copy-done.6, ...), custom_call_target="tpu_custom_call" | custom-call | flops 1132462080 | bytes 7667712 | tf_op jit(solution)/shard_map/queries/pallas_call | solution.py:408
  107.9 5.4 %collective-permute-start.24 = (bf16[2,240,384]{2,1,0:T(8,128)(2,1)S(1)}, bf16[2,240,384]{2,1,0:T(8,128)(2,1)S(1)}, u32[]{:S(2)}, u32[]{:S(2)}) collective-permute-start(bf16[2,240,384]{2,1,0:T(8,128)(2,1)S(1)} %collective-permute-done.23.refs_3_), channel_id=1, source_target_pairs={{0,8},{8,16},{16,24},{24,32},{32,40},{40,48},{48,56},{56,64},{64,7... | collective-permute-start | bytes 1105928 | tf_op jit(solution)/shard_map/ppermute | solution.py:55
  115.3 3.0 %collective-permute-start.26 = (bf16[2,240,384]{2,1,0:T(8,128)(2,1)S(1)}, bf16[2,240,384]{2,1,0:T(8,128)(2,1)S(1)}, u32[]{:S(2)}, u32[]{:S(2)}) collective-permute-start(bf16[2,240,384]{2,1,0:T(8,128)(2,1)S(1)} %collective-permute-done.25.refs_4_), channel_id=1, source_target_pairs={{0,8},{8,16},{16,24},{24,32},{32,40},{40,48},{48,56},{56,64},{64,7... | collective-permute-start | bytes 1105928 | tf_op jit(solution)/shard_map/ppermute | solution.py:55
  119.7 8.6 %attention_near.1 = (f32[2,240,384]{2,1,0:T(8,128)S(1)}, f32[2,240,384]{2,1,0:T(8,128)S(1)}, f32[2,240,384]{2,1,0:T(8,128)S(1)}) custom-call(s32[32,3]{1,0:T(8,128)S(1)} %copy.75.refs_0_, s32[10]{0:T(128)S(1)} %copy-done, bf16[2,240,384]{2,1,0:T(8,128)(2,1)S(1)} %copy-done.4, bf16[2,240,384]{2,1,0:T(8,128)(2,1)S(1)} %collective-permute-done.23.refs_3_, ...), custom_call_target="tpu_custom_call" | custom-call | flops 4529848320 | bytes 6291456 | tf_op jit(solution)/shard_map/attention_near/pallas_call | solution.py:424
  130.3 3.9 %collective-permute-done.30.refs_6_ = bf16[2,240,384]{2,1,0:T(8,128)(2,1)S(1)} collective-permute-done((bf16[2,240,384]{2,1,0:T(8,128)(2,1)S(1)}, bf16[2,240,384]{2,1,0:T(8,128)(2,1)S(1)}, u32[]{:S(2)}, u32[]{:S(2)}) %collective-permute-start.30) | collective-permute-done | bytes 368672 | tf_op jit(solution)/shard_map/ppermute | solution.py:55
  134.2 5.9 %attention_far.1.refs_1_ = bf16[2,240,384]{2,1,0:T(8,128)(2,1)S(1)} custom-call(s32[32,3]{1,0:T(8,128)S(1)} %copy.75.refs_0_, s32[10]{0:T(128)S(1)} %copy-done, bf16[2,240,384]{2,1,0:T(8,128)(2,1)S(1)} %copy-done.4, bf16[2,240,384]{2,1,0:T(8,128)(2,1)S(1)} %collective-permute-done.24.refs_3_, bf16[2,240,384]{2,1,0:T(8,128)(2,1)S(1)} %collective-permute-done.26.refs_4_, ...), custom_call_target="tpu_custom_call" | custom-call | flops 2264924160 | bytes 6291456 | tf_op jit(solution)/shard_map/attention_far/pallas_call | solution.py:440
  140.1 2.5 %out_projection.1 = (bf16[8,225,384]{2,1,0:T(8,128)(2,1)S(1)}, bf16[4,225,384]{2,1,0:T(8,128)(2,1)S(1)}, bf16[4,225,384]{2,1,0:T(8,128)(2,1)S(1)}) custom-call(s32[10]{0:T(128)S(1)} %copy-done, bf16[2,240,384]{2,1,0:T(8,128)(2,1)S(1)} %attention_far.1.refs_1_, bf16[3072,384]{1,0:T(8,128)(2,1)S(1)} %copy-done.1), custom_call_target="tpu_custom_call" | custom-call | flops 1132462080 | bytes 5308416 | tf_op jit(solution)/shard_map/out_projection/pallas_call | solution.py:456
  147.8 2.2 %collective-permute-start.33 = (bf16[2,225,384]{2,1,0:T(8,128)(2,1)S(1)}, bf16[2,225,384]{2,1,0:T(8,128)(2,1)S(1)}, u32[]{:S(2)}, u32[]{:S(2)}) collective-permute-start(bf16[2,225,384]{2,1,0:T(8,128)(2,1)S(1)} %get-tuple-element.49), channel_id=1, source_target_pairs={{0,6},{1,3},{2,0},{3,5},{4,2},{5,7},{6,4},{7,1},{8,14},{9,11},{10,... | collective-permute-start | bytes 1036808 | tf_op jit(solution)/shard_map/ppermute | solution.py:29
  150.5 6.4 %collective-permute-done.34 = bf16[2,225,384]{2,1,0:T(8,128)(2,1)S(1)} collective-permute-done((bf16[2,225,384]{2,1,0:T(8,128)(2,1)S(1)}, bf16[2,225,384]{2,1,0:T(8,128)(2,1)S(1)}, u32[]{:S(2)}, u32[]{:S(2)}) %collective-permute-start.34) | collective-permute-done | bytes 345632 | tf_op jit(solution)/shard_map/ppermute | solution.py:29
  158.6 8.3 %collective-permute-done.35 = bf16[2,225,384]{2,1,0:T(8,128)(2,1)S(1)} collective-permute-done((bf16[2,225,384]{2,1,0:T(8,128)(2,1)}, bf16[2,225,384]{2,1,0:T(8,128)(2,1)S(1)}, u32[]{:S(2)}, u32[]{:S(2)}) %collective-permute-start.35) | collective-permute-done | bytes 345632 | tf_op jit(solution)/shard_map/ppermute | solution.py:29
  (150 shorter events, 46.0 us)
Async XLA Ops:
  2.2 30.3 %collective-permute-start.1 = (bf16[768,384]{1,0:T(8,128)(2,1)S(1)}, bf16[768,384]{1,0:T(8,128)(2,1)S(1)}, u32[]{:S(2)}, u32[]{:S(2)}) collective-permute-start(bf16[768,384]{1,0:T(8,128)(2,1)S(1)} %pad_maximum_fusion.refs_10_.refs_0_), channel_id=1, source_target_pairs={{0,8},{1,33},{2,10},{3,35},{4,12},{5,37},{6,14},{7,39},{8,16},{9,4... | collective-permute-start | bytes 1769480 | tf_op jit(solution)/shard_map/ppermute | solution.py:29
  2.5 30.0 %collective-permute-start.2 = (bf16[768,384]{1,0:T(8,128)(2,1)S(1)}, bf16[768,384]{1,0:T(8,128)(2,1)S(1)}, u32[]{:S(2)}, u32[]{:S(2)}) collective-permute-start(bf16[768,384]{1,0:T(8,128)(2,1)S(1)} %pad_maximum_fusion.refs_10_.refs_0_), channel_id=1, source_target_pairs={{0,24},{1,97},{2,26},{3,99},{4,28},{5,101},{6,30},{7,103},{8,0},{9... | collective-permute-start | bytes 1769480 | tf_op jit(solution)/shard_map/ppermute | solution.py:29
  5.1 11.2 %all-to-all-start = ((s32[16,2,3]{2,1,0:T(2,128)}), s32[16,2,3]{2,1,0:T(2,128)S(1)}, u32[]{:S(2)}, u32[]{:S(2)}) async-start(s32[16,2,3]{2,1,0:T(2,128)} %broadcast_in_dim.49), calls=%async_computation | async-start | bytes 32768 | tf_op jit(solution)/shard_map/all_to_all | solution.py:74
  17.9 12.3 %collective-permute-start = (bf16[225,384]{1,0:T(8,128)(2,1)S(1)}, bf16[225,384]{1,0:T(8,128)(2,1)S(1)}, u32[]{:S(2)}, u32[]{:S(2)}) collective-permute-start(bf16[225,384]{1,0:T(8,128)(2,1)S(1)} %bitcast.38), channel_id=1, source_target_pairs={{0,120},{8,0},{16,8},{24,16},{32,24},{40,32},{48,40},{56,48},{64,5... | collective-permute-start | bytes 518408 | tf_op jit(solution)/shard_map/ppermute | solution.py:55
  19.4 13.1 %all-to-all-start.1 = ((f32[16,2,1152]{2,1,0:T(2,128)}), f32[16,2,1152]{2,1,0:T(2,128)}, u32[]{:S(2)}, u32[]{:S(2)}) async-start(f32[16,2,1152]{2,1,0:T(2,128)} %reshape.58), calls=%async_computation.1 | async-start | bytes 294912 | tf_op jit(solution)/shard_map/all_to_all | solution.py:357
  28.2 12.1 %collective-permute-start.11 = (bf16[768,384]{1,0:T(8,128)(2,1)S(1)}, bf16[768,384]{1,0:T(8,128)(2,1)S(1)}, u32[]{:S(2)}, u32[]{:S(2)}) collective-permute-start(bf16[768,384]{1,0:T(8,128)(2,1)S(1)} %pad_maximum_fusion.refs_10_.refs_0_), channel_id=1, source_target_pairs={{0,32},{1,9},{2,34},{3,11},{4,36},{5,13},{6,38},{7,15},{8,40},{9,1... | collective-permute-start | bytes 1769480 | tf_op jit(solution)/shard_map/ppermute | solution.py:29
  28.7 13.8 %collective-permute-start.15 = (bf16[768,384]{1,0:T(8,128)(2,1)S(1)}, bf16[768,384]{1,0:T(8,128)(2,1)S(1)}, u32[]{:S(2)}, u32[]{:S(2)}) collective-permute-start(bf16[768,384]{1,0:T(8,128)(2,1)S(1)} %pad_maximum_fusion.refs_10_.refs_0_), channel_id=1, source_target_pairs={{0,96},{1,25},{2,98},{3,27},{4,100},{5,29},{6,102},{7,31},{8,104},... | collective-permute-start | bytes 1769480 | tf_op jit(solution)/shard_map/ppermute | solution.py:29
  33.9 11.9 %collective-permute-start.4 = (bf16[2,240,384]{2,1,0:T(8,128)(2,1)S(1)}, bf16[2,240,384]{2,1,0:T(8,128)(2,1)S(1)}, u32[]{:S(2)}, u32[]{:S(2)}) collective-permute-start(bf16[2,240,384]{2,1,0:T(8,128)(2,1)S(1)} %dynamic_update_slice.3.refs_2_), channel_id=1, source_target_pairs={{0,2},{1,7},{2,4},{3,1},{4,6},{5,3},{6,0},{7,5},{8,10},{9,15},{10,... | collective-permute-start | bytes 1105928 | tf_op jit(solution)/shard_map/ppermute | solution.py:29
  38.1 16.4 %collective-permute-start.3 = (bf16[768,384]{1,0:T(8,128)(2,1)S(1)}, bf16[768,384]{1,0:T(8,128)(2,1)}, u32[]{:S(2)}, u32[]{:S(2)}) collective-permute-start(bf16[768,384]{1,0:T(8,128)(2,1)S(1)} %collective-permute-done.1.refs_11_.refs_1_), channel_id=1, source_target_pairs={{0,8},{1,33},{2,10},{3,35},{4,12},{5,37},{6,14},{7,39},{8,16},{9,4... | collective-permute-start | bytes 1769480 | tf_op jit(solution)/shard_map/ppermute | solution.py:29
  40.3 14.2 %collective-permute-start.12 = (bf16[768,384]{1,0:T(8,128)(2,1)S(1)}, bf16[768,384]{1,0:T(8,128)(2,1)}, u32[]{:S(2)}, u32[]{:S(2)}) collective-permute-start(bf16[768,384]{1,0:T(8,128)(2,1)S(1)} %collective-permute-done.1.refs_11_.refs_1_), channel_id=1, source_target_pairs={{0,32},{1,9},{2,34},{3,11},{4,36},{5,13},{6,38},{7,15},{8,40},{9,1... | collective-permute-start | bytes 1769480 | tf_op jit(solution)/shard_map/ppermute | solution.py:29
  46.7 16.6 %collective-permute-start.16 = (bf16[768,384]{1,0:T(8,128)(2,1)S(1)}, bf16[768,384]{1,0:T(8,128)(2,1)S(1)}, u32[]{:S(2)}, u32[]{:S(2)}) collective-permute-start(bf16[768,384]{1,0:T(8,128)(2,1)S(1)} %collective-permute-done.1.refs_11_.refs_1_), channel_id=1, source_target_pairs={{0,96},{1,25},{2,98},{3,27},{4,100},{5,29},{6,102},{7,31},{8,104},... | collective-permute-start | bytes 1769480 | tf_op jit(solution)/shard_map/ppermute | solution.py:29
  48.1 15.1 %collective-permute-start.13 = (bf16[768,384]{1,0:T(8,128)(2,1)S(1)}, bf16[768,384]{1,0:T(8,128)(2,1)S(1)}, u32[]{:S(2)}, u32[]{:S(2)}) collective-permute-start(bf16[768,384]{1,0:T(8,128)(2,1)S(1)} %collective-permute-done.2.refs_12_.refs_2_), channel_id=1, source_target_pairs={{0,32},{1,9},{2,34},{3,11},{4,36},{5,13},{6,38},{7,15},{8,40},{9,1... | collective-permute-start | bytes 1769480 | tf_op jit(solution)/shard_map/ppermute | solution.py:29
  54.5 15.2 %collective-permute-start.18 = (bf16[768,384]{1,0:T(8,128)(2,1)}, bf16[768,384]{1,0:T(8,128)(2,1)}, u32[]{:S(2)}, u32[]{:S(2)}) collective-permute-start(bf16[768,384]{1,0:T(8,128)(2,1)} %collective-permute-done.3.refs_13_.refs_3_), channel_id=1, source_target_pairs={{0,96},{1,25},{2,98},{3,27},{4,100},{5,29},{6,102},{7,31},{8,104},... | collective-permute-start | bytes 1769480 | tf_op jit(solution)/shard_map/ppermute | solution.py:29
  67.3 14.0 %collective-permute-start.20 = (bf16[768,384]{1,0:T(8,128)(2,1)}, bf16[768,384]{1,0:T(8,128)(2,1)}, u32[]{:S(2)}, u32[]{:S(2)}) collective-permute-start(bf16[768,384]{1,0:T(8,128)(2,1)} %collective-permute-done.12.refs_15_.refs_5_), channel_id=1, source_target_pairs={{0,32},{1,9},{2,34},{3,11},{4,36},{5,13},{6,38},{7,15},{8,40},{9,1... | collective-permute-start | bytes 1769480 | tf_op jit(solution)/shard_map/ppermute | solution.py:29
  67.7 13.7 %collective-permute-start.21 = (bf16[768,384]{1,0:T(8,128)(2,1)S(1)}, bf16[768,384]{1,0:T(8,128)(2,1)}, u32[]{:S(2)}, u32[]{:S(2)}) collective-permute-start(bf16[768,384]{1,0:T(8,128)(2,1)S(1)} %collective-permute-done.17.refs_20_.refs_10_), channel_id=1, source_target_pairs={{0,96},{1,25},{2,98},{3,27},{4,100},{5,29},{6,102},{7,31},{8,104},... | collective-permute-start | bytes 1769480 | tf_op jit(solution)/shard_map/ppermute | solution.py:29
  69.7 15.6 %collective-permute-start.22 = (bf16[768,384]{1,0:T(8,128)(2,1)}, bf16[768,384]{1,0:T(8,128)(2,1)}, u32[]{:S(2)}, u32[]{:S(2)}) collective-permute-start(bf16[768,384]{1,0:T(8,128)(2,1)} %collective-permute-done.18.refs_21_.refs_11_), channel_id=1, source_target_pairs={{0,96},{1,25},{2,98},{3,27},{4,100},{5,29},{6,102},{7,31},{8,104},... | collective-permute-start | bytes 1769480 | tf_op jit(solution)/shard_map/ppermute | solution.py:29
  95.6 12.3 %collective-permute-start.23 = (bf16[2,240,384]{2,1,0:T(8,128)(2,1)}, bf16[2,240,384]{2,1,0:T(8,128)(2,1)S(1)}, u32[]{:S(2)}, u32[]{:S(2)}) collective-permute-start(bf16[2,240,384]{2,1,0:T(8,128)(2,1)} %get-tuple-element.40.refs_5_), channel_id=1, source_target_pairs={{0,8},{8,16},{16,24},{24,32},{32,40},{40,48},{48,56},{56,64},{64,7... | collective-permute-start | bytes 1105928 | tf_op jit(solution)/shard_map/ppermute | solution.py:55
  97.9 17.4 %collective-permute-start.25 = (bf16[2,240,384]{2,1,0:T(8,128)(2,1)}, bf16[2,240,384]{2,1,0:T(8,128)(2,1)S(1)}, u32[]{:S(2)}, u32[]{:S(2)}) collective-permute-start(bf16[2,240,384]{2,1,0:T(8,128)(2,1)} %get-tuple-element.41.refs_6_), channel_id=1, source_target_pairs={{0,8},{8,16},{16,24},{24,32},{32,40},{40,48},{48,56},{56,64},{64,7... | collective-permute-start | bytes 1105928 | tf_op jit(solution)/shard_map/ppermute | solution.py:55
  98.0 20.4 %collective-permute-start.27 = (bf16[2,240,384]{2,1,0:T(8,128)(2,1)}, bf16[2,240,384]{2,1,0:T(8,128)(2,1)S(1)}, u32[]{:S(2)}, u32[]{:S(2)}) collective-permute-start(bf16[2,240,384]{2,1,0:T(8,128)(2,1)} %get-tuple-element.40.refs_5_), channel_id=1, source_target_pairs={{0,120},{8,0},{16,8},{24,16},{32,24},{40,32},{48,40},{56,48},{64,5... | collective-permute-start | bytes 1105928 | tf_op jit(solution)/shard_map/ppermute | solution.py:55
  99.9 18.5 %collective-permute-start.29 = (bf16[2,240,384]{2,1,0:T(8,128)(2,1)}, bf16[2,240,384]{2,1,0:T(8,128)(2,1)S(1)}, u32[]{:S(2)}, u32[]{:S(2)}) collective-permute-start(bf16[2,240,384]{2,1,0:T(8,128)(2,1)} %get-tuple-element.41.refs_6_), channel_id=1, source_target_pairs={{0,120},{8,0},{16,8},{24,16},{32,24},{40,32},{48,40},{56,48},{64,5... | collective-permute-start | bytes 1105928 | tf_op jit(solution)/shard_map/ppermute | solution.py:55
  107.9 20.4 %collective-permute-start.24 = (bf16[2,240,384]{2,1,0:T(8,128)(2,1)S(1)}, bf16[2,240,384]{2,1,0:T(8,128)(2,1)S(1)}, u32[]{:S(2)}, u32[]{:S(2)}) collective-permute-start(bf16[2,240,384]{2,1,0:T(8,128)(2,1)S(1)} %collective-permute-done.23.refs_3_), channel_id=1, source_target_pairs={{0,8},{8,16},{16,24},{24,32},{32,40},{40,48},{48,56},{56,64},{64,7... | collective-permute-start | bytes 1105928 | tf_op jit(solution)/shard_map/ppermute | solution.py:55
  115.3 13.6 %collective-permute-start.26 = (bf16[2,240,384]{2,1,0:T(8,128)(2,1)S(1)}, bf16[2,240,384]{2,1,0:T(8,128)(2,1)S(1)}, u32[]{:S(2)}, u32[]{:S(2)}) collective-permute-start(bf16[2,240,384]{2,1,0:T(8,128)(2,1)S(1)} %collective-permute-done.25.refs_4_), channel_id=1, source_target_pairs={{0,8},{8,16},{16,24},{24,32},{32,40},{40,48},{48,56},{56,64},{64,7... | collective-permute-start | bytes 1105928 | tf_op jit(solution)/shard_map/ppermute | solution.py:55
  118.4 11.9 %collective-permute-start.28 = (bf16[2,240,384]{2,1,0:T(8,128)(2,1)S(1)}, bf16[2,240,384]{2,1,0:T(8,128)(2,1)S(1)}, u32[]{:S(2)}, u32[]{:S(2)}) collective-permute-start(bf16[2,240,384]{2,1,0:T(8,128)(2,1)S(1)} %collective-permute-done.27.refs_7_), channel_id=1, source_target_pairs={{0,120},{8,0},{16,8},{24,16},{32,24},{40,32},{48,40},{56,48},{64,5... | collective-permute-start | bytes 1105928 | tf_op jit(solution)/shard_map/ppermute | solution.py:55
  118.4 15.9 %collective-permute-start.30 = (bf16[2,240,384]{2,1,0:T(8,128)(2,1)S(1)}, bf16[2,240,384]{2,1,0:T(8,128)(2,1)S(1)}, u32[]{:S(2)}, u32[]{:S(2)}) collective-permute-start(bf16[2,240,384]{2,1,0:T(8,128)(2,1)S(1)} %collective-permute-done.29.refs_8_), channel_id=1, source_target_pairs={{0,120},{8,0},{16,8},{24,16},{32,24},{40,32},{48,40},{56,48},{64,5... | collective-permute-start | bytes 1105928 | tf_op jit(solution)/shard_map/ppermute | solution.py:55
  (40 other events, 617.3 us)

commit v6 on v5

--- a/solution.py
+++ b/solution.py
@@ -432,7 +432,7 @@
             pltpu.VMEM((6, KEYS, 2 * PAIR), jnp.bfloat16),
         ],
         name="attention_near",
-        compiler_params=params,
+        compiler_params=pltpu.CompilerParams(vmem_limit_bytes=60 << 20),
         cost_estimate=pl.CostEstimate(
             flops=6 * 6 * 4 * 480 * 256 * 256, bytes_accessed=6 << 20, transcendentals=36 * 480 * 256
         ),

time: 169 us -> 172 us (1.018)
  local copies, waits for them, and re-layouts: 9.71 us -> 15 us
  waiting for transfers between devices: 58.5 us -> 56.7 us
    unnamed x54 -> x70, local copies, waits for them, and re-layouts: 2.53 us -> 4.68 us
  transfers between devices with their start and end apart: 38 -> 38, of which waited for: 18 -> 18; matrix products, arithmetic and copies ran while one was open for 5% -> 6% of each run, Pallas kernels for 10% -> 10%
where the time goes in v6:
time: 172 us; the launch traced here: 171 us
  starting transfers between devices  58.7 us (34%)
  waiting for transfers between devices  56.7 us (33%)
  Pallas kernels  36 us (21%)
  local copies, waits for them, and re-layouts  15 us (9%)
  other arithmetic  3.89 us (2%)
    ppermute x21, waiting for transfers between devices, torus_step(): return lax.ppermute(array, ('frame', 'row'), pairs)  43 us
    ppermute x21, starting transfers between devices, torus_step(): return lax.ppermute(array, ('frame', 'row'), pairs)  29 us
    ppermute x9, starting transfers between devices, next_frame(): lax.ppermute(array, 'frame', [(i, (i + by) % peers) for i in range(peers)])  13.3 us
    pallas_call x1, Pallas kernels, per_device(): pl.pallas_call(lambda *refs: key_value_kernel(tokens, *refs), out_shape=[...  10.2 us
    pallas_call x1, Pallas kernels, per_device(): pl.pallas_call(lambda *refs: near_kernel(tokens, *refs), out_shape=[struc...  9.61 us
    all_to_all x1, starting transfers between devices, per_device(): lax.all_to_all(sums.reshape(slots // 2, 2, 3 * width), 'frame', 0, 0, til...  8.15 us
    pallas_call x1, Pallas kernels, per_device(): call(query_kernel, [struct((2, PADDED, width)), struct((D, width))], [SME...  7.74 us
    ppermute x9, waiting for transfers between devices, next_frame(): lax.ppermute(array, 'frame', [(i, (i + by) % peers) for i in range(peers)])  7.62 us
  transfers between devices with their start and end apart: 38, of which 18 were waited for; matrix products, arithmetic and copies ran while one was open for 6% of the time, Pallas kernels for 10%

profile of v6, /device:TPU:30, one launch (start us, length us, event | category | flops | bytes accessed | tf_op | source)
XLA Modules:
  0.0 171.1 jit_solution(14986594306019039038)
XLA Ops:
  5.1 7.1 %all-to-all-start = ((s32[16,2,3]{2,1,0:T(2,128)}), s32[16,2,3]{2,1,0:T(2,128)S(1)}, u32[]{:S(2)}, u32[]{:S(2)}) async-start(s32[16,2,3]{2,1,0:T(2,128)} %broadcast_in_dim.49), calls=%async_computation | async-start | bytes 32768 | tf_op jit(solution)/shard_map/all_to_all | solution.py:74
  12.8 3.5 %all-to-all-done = s32[16,2,3]{2,1,0:T(2,128)S(1)} async-done(((s32[16,2,3]{2,1,0:T(2,128)}), s32[16,2,3]{2,1,0:T(2,128)S(1)}, u32[]{:S(2)}, u32[]{:S(2)}) %all-to-all-start) | async-done | bytes 416 | tf_op jit(solution)/shard_map/all_to_all | solution.py:74
  19.4 8.2 %all-to-all-start.1 = ((f32[16,2,1152]{2,1,0:T(2,128)}), f32[16,2,1152]{2,1,0:T(2,128)S(1)}, u32[]{:S(2)}, u32[]{:S(2)}) async-start(f32[16,2,1152]{2,1,0:T(2,128)} %reshape.58), calls=%async_computation.1 | async-start | bytes 294912 | tf_op jit(solution)/shard_map/all_to_all | solution.py:357
  37.5 2.2 %collective-permute-start.3 = (bf16[768,384]{1,0:T(8,128)(2,1)S(1)}, bf16[768,384]{1,0:T(8,128)(2,1)S(1)}, u32[]{:S(2)}, u32[]{:S(2)}) collective-permute-start(bf16[768,384]{1,0:T(8,128)(2,1)S(1)} %collective-permute-done.1.refs_11_.refs_1_), channel_id=1, source_target_pairs={{0,8},{1,33},{2,10},{3,35},{4,12},{5,37},{6,14},{7,39},{8,16},{9,4... | collective-permute-start | bytes 1769480 | tf_op jit(solution)/shard_map/ppermute | solution.py:29
  39.7 2.2 %collective-permute-start.12 = (bf16[768,384]{1,0:T(8,128)(2,1)S(1)}, bf16[768,384]{1,0:T(8,128)(2,1)}, u32[]{:S(2)}, u32[]{:S(2)}) collective-permute-start(bf16[768,384]{1,0:T(8,128)(2,1)S(1)} %collective-permute-done.1.refs_11_.refs_1_), channel_id=1, source_target_pairs={{0,32},{1,9},{2,34},{3,11},{4,36},{5,13},{6,38},{7,15},{8,40},{9,1... | collective-permute-start | bytes 1769480 | tf_op jit(solution)/shard_map/ppermute | solution.py:29
  41.9 3.5 %collective-permute-done.4.refs_3_ = bf16[2,240,384]{2,1,0:T(8,128)(2,1)S(1)} collective-permute-done((bf16[2,240,384]{2,1,0:T(8,128)(2,1)}, bf16[2,240,384]{2,1,0:T(8,128)(2,1)S(1)}, u32[]{:S(2)}, u32[]{:S(2)}) %collective-permute-start.4) | collective-permute-done | bytes 368672 | tf_op jit(solution)/shard_map/ppermute | solution.py:29
  49.5 4.2 %collective-permute-done.3.refs_13_.refs_3_ = bf16[768,384]{1,0:T(8,128)(2,1)S(1)} collective-permute-done((bf16[768,384]{1,0:T(8,128)(2,1)S(1)}, bf16[768,384]{1,0:T(8,128)(2,1)S(1)}, u32[]{:S(2)}, u32[]{:S(2)}) %collective-permute-start.3) | collective-permute-done | bytes 589856 | tf_op jit(solution)/shard_map/ppermute | solution.py:29
  56.6 6.3 %collective-permute-done.16.refs_19_.refs_9_ = bf16[768,384]{1,0:T(8,128)(2,1)S(1)} collective-permute-done((bf16[768,384]{1,0:T(8,128)(2,1)S(1)}, bf16[768,384]{1,0:T(8,128)(2,1)S(1)}, u32[]{:S(2)}, u32[]{:S(2)}) %collective-permute-start.16) | collective-permute-done | bytes 589856 | tf_op jit(solution)/shard_map/ppermute | solution.py:29
  64.0 3.0 %collective-permute-start.14 = (bf16[768,384]{1,0:T(8,128)(2,1)S(1)}, bf16[768,384]{1,0:T(8,128)(2,1)}, u32[]{:S(2)}, u32[]{:S(2)}) collective-permute-start(bf16[768,384]{1,0:T(8,128)(2,1)S(1)} %collective-permute-done.3.refs_13_.refs_3_), channel_id=1, source_target_pairs={{0,32},{1,9},{2,34},{3,11},{4,36},{5,13},{6,38},{7,15},{8,40},{9,1... | collective-permute-start | bytes 1769480 | tf_op jit(solution)/shard_map/ppermute | solution.py:29
  71.9 2.4 %collective-permute-done.14.refs_17_.refs_7_ = bf16[768,384]{1,0:T(8,128)(2,1)} collective-permute-done((bf16[768,384]{1,0:T(8,128)(2,1)S(1)}, bf16[768,384]{1,0:T(8,128)(2,1)}, u32[]{:S(2)}, u32[]{:S(2)}) %collective-permute-start.14) | collective-permute-done | bytes 589856 | tf_op jit(solution)/shard_map/ppermute | solution.py:29
  74.3 6.4 %collective-permute-done.20.refs_23_.refs_13_ = bf16[768,384]{1,0:T(8,128)(2,1)} collective-permute-done((bf16[768,384]{1,0:T(8,128)(2,1)}, bf16[768,384]{1,0:T(8,128)(2,1)}, u32[]{:S(2)}, u32[]{:S(2)}) %collective-permute-start.20) | collective-permute-done | bytes 589856 | tf_op jit(solution)/shard_map/ppermute | solution.py:29
  80.8 3.8 %collective-permute-done.22.refs_25_.refs_15_ = bf16[768,384]{1,0:T(8,128)(2,1)} collective-permute-done((bf16[768,384]{1,0:T(8,128)(2,1)}, bf16[768,384]{1,0:T(8,128)(2,1)}, u32[]{:S(2)}, u32[]{:S(2)}) %collective-permute-start.22) | collective-permute-done | bytes 589856 | tf_op jit(solution)/shard_map/ppermute | solution.py:29
  84.6 10.2 %keys_values.1 = (bf16[2,240,384]{2,1,0:T(8,128)(2,1)}, bf16[2,240,384]{2,1,0:T(8,128)(2,1)}, bf16[2,240,3072]{2,1,0:T(8,128)(2,1)}) custom-call(s32[10]{0:T(128)} %concatenate.26.refs_0_.pos_ref.refs_1_, f32[1,64]{1,0:T(1,128)} %bitcast.42, bf16[2,240,384]{2,1,0:T(8,128)(2,1)} %dynamic_update_slice.3.refs_2_, bf16[2,240,384]{2,1,0:T(8,128)(2,1)} %copy-done.22, ...), custom_call_target="tpu_custom_call" | custom-call | flops 2264924160 | bytes 7667712 | tf_op jit(solution)/shard_map/keys_values/pallas_call | solution.py:389
  94.8 2.2 %collective-permute-start.23 = (bf16[2,240,384]{2,1,0:T(8,128)(2,1)}, bf16[2,240,384]{2,1,0:T(8,128)(2,1)S(1)}, u32[]{:S(2)}, u32[]{:S(2)}) collective-permute-start(bf16[2,240,384]{2,1,0:T(8,128)(2,1)} %get-tuple-element.40.refs_5_), channel_id=1, source_target_pairs={{0,8},{8,16},{16,24},{24,32},{32,40},{40,48},{48,56},{56,64},{64,7... | collective-permute-start | bytes 1105928 | tf_op jit(solution)/shard_map/ppermute | solution.py:55
  99.8 7.7 %queries.1 = (bf16[2,240,384]{2,1,0:T(8,128)(2,1)}, bf16[3072,384]{1,0:T(8,128)(2,1)}) custom-call(s32[10]{0:T(128)} %concatenate.26.refs_0_.pos_ref.refs_1_, bf16[2,240,3072]{2,1,0:T(8,128)(2,1)} %get-tuple-element.38.x_ref, f32[1,64]{1,0:T(1,128)} %bitcast.43, bf16[768,384]{1,0:T(8,128)(2,1)} %copy-done.7, bf16[768,384]{1,0:T(8,128)(2,1)} %copy-done.8, ...), custom_call_target="tpu_custom_call" | custom-call | flops 1132462080 | bytes 7667712 | tf_op jit(solution)/shard_map/queries/pallas_call | solution.py:408
  107.6 5.4 %collective-permute-start.24 = (bf16[2,240,384]{2,1,0:T(8,128)(2,1)S(1)}, bf16[2,240,384]{2,1,0:T(8,128)(2,1)S(1)}, u32[]{:S(2)}, u32[]{:S(2)}) collective-permute-start(bf16[2,240,384]{2,1,0:T(8,128)(2,1)S(1)} %collective-permute-done.23.refs_3_), channel_id=1, source_target_pairs={{0,8},{8,16},{16,24},{24,32},{32,40},{40,48},{48,56},{56,64},{64,7... | collective-permute-start | bytes 1105928 | tf_op jit(solution)/shard_map/ppermute | solution.py:55
  114.5 2.6 %collective-permute-start.26 = (bf16[2,240,384]{2,1,0:T(8,128)(2,1)S(1)}, bf16[2,240,384]{2,1,0:T(8,128)(2,1)S(1)}, u32[]{:S(2)}, u32[]{:S(2)}) collective-permute-start(bf16[2,240,384]{2,1,0:T(8,128)(2,1)S(1)} %collective-permute-done.25.refs_4_), channel_id=1, source_target_pairs={{0,8},{8,16},{16,24},{24,32},{32,40},{40,48},{48,56},{56,64},{64,7... | collective-permute-start | bytes 1105928 | tf_op jit(solution)/shard_map/ppermute | solution.py:55
  118.0 9.6 %attention_near.1 = (f32[2,240,384]{2,1,0:T(8,128)}, f32[2,240,384]{2,1,0:T(8,128)}, f32[2,240,384]{2,1,0:T(8,128)}) custom-call(s32[32,3]{1,0:T(8,128)} %copy.75.refs_0_, s32[10]{0:T(128)} %concatenate.26.refs_0_.pos_ref.refs_1_, bf16[2,240,384]{2,1,0:T(8,128)(2,1)} %get-tuple-element.39.refs_2_, bf16[2,240,384]{2,1,0:T(8,128)(2,1)} %copy-done.29, ...), custom_call_target="tpu_custom_call" | custom-call | flops 4529848320 | bytes 6291456 | tf_op jit(solution)/shard_map/attention_near/pallas_call | solution.py:424
  129.7 3.9 %collective-permute-done.30.refs_6_ = bf16[2,240,384]{2,1,0:T(8,128)(2,1)S(1)} collective-permute-done((bf16[2,240,384]{2,1,0:T(8,128)(2,1)S(1)}, bf16[2,240,384]{2,1,0:T(8,128)(2,1)S(1)}, u32[]{:S(2)}, u32[]{:S(2)}) %collective-permute-start.30) | collective-permute-done | bytes 368672 | tf_op jit(solution)/shard_map/ppermute | solution.py:55
  137.0 5.9 %attention_far.1.refs_1_ = bf16[2,240,384]{2,1,0:T(8,128)(2,1)S(1)} custom-call(s32[32,3]{1,0:T(8,128)S(1)} %copy-done, s32[10]{0:T(128)S(1)} %copy-done.1, bf16[2,240,384]{2,1,0:T(8,128)(2,1)S(1)} %copy-done.3, bf16[2,240,384]{2,1,0:T(8,128)(2,1)S(1)} %collective-permute-done.24.refs_3_, bf16[2,240,384]{2,1,0:T(8,128)(2,1)S(1)} %collective-permute-done.26.refs_4_, ...), custom_call_target="tpu_custom_call" | custom-call | flops 2264924160 | bytes 6291456 | tf_op jit(solution)/shard_map/attention_far/pallas_call | solution.py:440
  142.9 2.5 %out_projection.1 = (bf16[8,225,384]{2,1,0:T(8,128)(2,1)S(1)}, bf16[4,225,384]{2,1,0:T(8,128)(2,1)S(1)}, bf16[4,225,384]{2,1,0:T(8,128)(2,1)S(1)}) custom-call(s32[10]{0:T(128)S(1)} %copy-done.1, bf16[2,240,384]{2,1,0:T(8,128)(2,1)S(1)} %attention_far.1.refs_1_, bf16[3072,384]{1,0:T(8,128)(2,1)S(1)} %copy-done.2), custom_call_target="tpu_custom_call" | custom-call | flops 1132462080 | bytes 5308416 | tf_op jit(solution)/shard_map/out_projection/pallas_call | solution.py:456
  150.7 2.2 %collective-permute-start.33 = (bf16[2,225,384]{2,1,0:T(8,128)(2,1)S(1)}, bf16[2,225,384]{2,1,0:T(8,128)(2,1)S(1)}, u32[]{:S(2)}, u32[]{:S(2)}) collective-permute-start(bf16[2,225,384]{2,1,0:T(8,128)(2,1)S(1)} %get-tuple-element.49), channel_id=1, source_target_pairs={{0,6},{1,3},{2,0},{3,5},{4,2},{5,7},{6,4},{7,1},{8,14},{9,11},{10,... | collective-permute-start | bytes 1036808 | tf_op jit(solution)/shard_map/ppermute | solution.py:29
  153.4 6.4 %collective-permute-done.34 = bf16[2,225,384]{2,1,0:T(8,128)(2,1)S(1)} collective-permute-done((bf16[2,225,384]{2,1,0:T(8,128)(2,1)S(1)}, bf16[2,225,384]{2,1,0:T(8,128)(2,1)S(1)}, u32[]{:S(2)}, u32[]{:S(2)}) %collective-permute-start.34) | collective-permute-done | bytes 345632 | tf_op jit(solution)/shard_map/ppermute | solution.py:29
  161.5 8.3 %collective-permute-done.35 = bf16[2,225,384]{2,1,0:T(8,128)(2,1)S(1)} collective-permute-done((bf16[2,225,384]{2,1,0:T(8,128)(2,1)}, bf16[2,225,384]{2,1,0:T(8,128)(2,1)S(1)}, u32[]{:S(2)}, u32[]{:S(2)}) %collective-permute-start.35) | collective-permute-done | bytes 345632 | tf_op jit(solution)/shard_map/ppermute | solution.py:29
  (166 shorter events, 50.8 us)
Async XLA Ops:
  2.2 29.6 %collective-permute-start.1 = (bf16[768,384]{1,0:T(8,128)(2,1)S(1)}, bf16[768,384]{1,0:T(8,128)(2,1)S(1)}, u32[]{:S(2)}, u32[]{:S(2)}) collective-permute-start(bf16[768,384]{1,0:T(8,128)(2,1)S(1)} %pad_maximum_fusion.refs_10_.refs_0_), channel_id=1, source_target_pairs={{0,8},{1,33},{2,10},{3,35},{4,12},{5,37},{6,14},{7,39},{8,16},{9,4... | collective-permute-start | bytes 1769480 | tf_op jit(solution)/shard_map/ppermute | solution.py:29
  2.5 29.3 %collective-permute-start.2 = (bf16[768,384]{1,0:T(8,128)(2,1)S(1)}, bf16[768,384]{1,0:T(8,128)(2,1)S(1)}, u32[]{:S(2)}, u32[]{:S(2)}) collective-permute-start(bf16[768,384]{1,0:T(8,128)(2,1)S(1)} %pad_maximum_fusion.refs_10_.refs_0_), channel_id=1, source_target_pairs={{0,24},{1,97},{2,26},{3,99},{4,28},{5,101},{6,30},{7,103},{8,0},{9... | collective-permute-start | bytes 1769480 | tf_op jit(solution)/shard_map/ppermute | solution.py:29
  17.9 11.7 %collective-permute-start = (bf16[225,384]{1,0:T(8,128)(2,1)S(1)}, bf16[225,384]{1,0:T(8,128)(2,1)S(1)}, u32[]{:S(2)}, u32[]{:S(2)}) collective-permute-start(bf16[225,384]{1,0:T(8,128)(2,1)S(1)} %bitcast.38), channel_id=1, source_target_pairs={{0,120},{8,0},{16,8},{24,16},{32,24},{40,32},{48,40},{56,48},{64,5... | collective-permute-start | bytes 518408 | tf_op jit(solution)/shard_map/ppermute | solution.py:55
  19.4 12.4 %all-to-all-start.1 = ((f32[16,2,1152]{2,1,0:T(2,128)}), f32[16,2,1152]{2,1,0:T(2,128)S(1)}, u32[]{:S(2)}, u32[]{:S(2)}) async-start(f32[16,2,1152]{2,1,0:T(2,128)} %reshape.58), calls=%async_computation.1 | async-start | bytes 294912 | tf_op jit(solution)/shard_map/all_to_all | solution.py:357
  27.6 12.1 %collective-permute-start.11 = (bf16[768,384]{1,0:T(8,128)(2,1)S(1)}, bf16[768,384]{1,0:T(8,128)(2,1)S(1)}, u32[]{:S(2)}, u32[]{:S(2)}) collective-permute-start(bf16[768,384]{1,0:T(8,128)(2,1)S(1)} %pad_maximum_fusion.refs_10_.refs_0_), channel_id=1, source_target_pairs={{0,32},{1,9},{2,34},{3,11},{4,36},{5,13},{6,38},{7,15},{8,40},{9,1... | collective-permute-start | bytes 1769480 | tf_op jit(solution)/shard_map/ppermute | solution.py:29
  28.1 13.8 %collective-permute-start.15 = (bf16[768,384]{1,0:T(8,128)(2,1)S(1)}, bf16[768,384]{1,0:T(8,128)(2,1)S(1)}, u32[]{:S(2)}, u32[]{:S(2)}) collective-permute-start(bf16[768,384]{1,0:T(8,128)(2,1)S(1)} %pad_maximum_fusion.refs_10_.refs_0_), channel_id=1, source_target_pairs={{0,96},{1,25},{2,98},{3,27},{4,100},{5,29},{6,102},{7,31},{8,104},... | collective-permute-start | bytes 1769480 | tf_op jit(solution)/shard_map/ppermute | solution.py:29
  33.4 12.1 %collective-permute-start.4 = (bf16[2,240,384]{2,1,0:T(8,128)(2,1)}, bf16[2,240,384]{2,1,0:T(8,128)(2,1)S(1)}, u32[]{:S(2)}, u32[]{:S(2)}) collective-permute-start(bf16[2,240,384]{2,1,0:T(8,128)(2,1)} %dynamic_update_slice.3.refs_2_), channel_id=1, source_target_pairs={{0,2},{1,7},{2,4},{3,1},{4,6},{5,3},{6,0},{7,5},{8,10},{9,15},{10,... | collective-permute-start | bytes 1105928 | tf_op jit(solution)/shard_map/ppermute | solution.py:29
  37.5 16.3 %collective-permute-start.3 = (bf16[768,384]{1,0:T(8,128)(2,1)S(1)}, bf16[768,384]{1,0:T(8,128)(2,1)S(1)}, u32[]{:S(2)}, u32[]{:S(2)}) collective-permute-start(bf16[768,384]{1,0:T(8,128)(2,1)S(1)} %collective-permute-done.1.refs_11_.refs_1_), channel_id=1, source_target_pairs={{0,8},{1,33},{2,10},{3,35},{4,12},{5,37},{6,14},{7,39},{8,16},{9,4... | collective-permute-start | bytes 1769480 | tf_op jit(solution)/shard_map/ppermute | solution.py:29
  39.7 14.1 %collective-permute-start.12 = (bf16[768,384]{1,0:T(8,128)(2,1)S(1)}, bf16[768,384]{1,0:T(8,128)(2,1)}, u32[]{:S(2)}, u32[]{:S(2)}) collective-permute-start(bf16[768,384]{1,0:T(8,128)(2,1)S(1)} %collective-permute-done.1.refs_11_.refs_1_), channel_id=1, source_target_pairs={{0,32},{1,9},{2,34},{3,11},{4,36},{5,13},{6,38},{7,15},{8,40},{9,1... | collective-permute-start | bytes 1769480 | tf_op jit(solution)/shard_map/ppermute | solution.py:29
  46.3 16.6 %collective-permute-start.16 = (bf16[768,384]{1,0:T(8,128)(2,1)S(1)}, bf16[768,384]{1,0:T(8,128)(2,1)S(1)}, u32[]{:S(2)}, u32[]{:S(2)}) collective-permute-start(bf16[768,384]{1,0:T(8,128)(2,1)S(1)} %collective-permute-done.1.refs_11_.refs_1_), channel_id=1, source_target_pairs={{0,96},{1,25},{2,98},{3,27},{4,100},{5,29},{6,102},{7,31},{8,104},... | collective-permute-start | bytes 1769480 | tf_op jit(solution)/shard_map/ppermute | solution.py:29
  47.8 15.1 %collective-permute-start.13 = (bf16[768,384]{1,0:T(8,128)(2,1)S(1)}, bf16[768,384]{1,0:T(8,128)(2,1)S(1)}, u32[]{:S(2)}, u32[]{:S(2)}) collective-permute-start(bf16[768,384]{1,0:T(8,128)(2,1)S(1)} %collective-permute-done.2.refs_12_.refs_2_), channel_id=1, source_target_pairs={{0,32},{1,9},{2,34},{3,11},{4,36},{5,13},{6,38},{7,15},{8,40},{9,1... | collective-permute-start | bytes 1769480 | tf_op jit(solution)/shard_map/ppermute | solution.py:29
  53.8 15.5 %collective-permute-start.18 = (bf16[768,384]{1,0:T(8,128)(2,1)S(1)}, bf16[768,384]{1,0:T(8,128)(2,1)}, u32[]{:S(2)}, u32[]{:S(2)}) collective-permute-start(bf16[768,384]{1,0:T(8,128)(2,1)S(1)} %collective-permute-done.3.refs_13_.refs_3_), channel_id=1, source_target_pairs={{0,96},{1,25},{2,98},{3,27},{4,100},{5,29},{6,102},{7,31},{8,104},... | collective-permute-start | bytes 1769480 | tf_op jit(solution)/shard_map/ppermute | solution.py:29
  66.9 13.8 %collective-permute-start.20 = (bf16[768,384]{1,0:T(8,128)(2,1)}, bf16[768,384]{1,0:T(8,128)(2,1)}, u32[]{:S(2)}, u32[]{:S(2)}) collective-permute-start(bf16[768,384]{1,0:T(8,128)(2,1)} %collective-permute-done.12.refs_15_.refs_5_), channel_id=1, source_target_pairs={{0,32},{1,9},{2,34},{3,11},{4,36},{5,13},{6,38},{7,15},{8,40},{9,1... | collective-permute-start | bytes 1769480 | tf_op jit(solution)/shard_map/ppermute | solution.py:29
  67.0 13.7 %collective-permute-start.21 = (bf16[768,384]{1,0:T(8,128)(2,1)S(1)}, bf16[768,384]{1,0:T(8,128)(2,1)}, u32[]{:S(2)}, u32[]{:S(2)}) collective-permute-start(bf16[768,384]{1,0:T(8,128)(2,1)S(1)} %collective-permute-done.17.refs_20_.refs_10_), channel_id=1, source_target_pairs={{0,96},{1,25},{2,98},{3,27},{4,100},{5,29},{6,102},{7,31},{8,104},... | collective-permute-start | bytes 1769480 | tf_op jit(solution)/shard_map/ppermute | solution.py:29
  69.3 15.2 %collective-permute-start.22 = (bf16[768,384]{1,0:T(8,128)(2,1)}, bf16[768,384]{1,0:T(8,128)(2,1)}, u32[]{:S(2)}, u32[]{:S(2)}) collective-permute-start(bf16[768,384]{1,0:T(8,128)(2,1)} %collective-permute-done.18.refs_21_.refs_11_), channel_id=1, source_target_pairs={{0,96},{1,25},{2,98},{3,27},{4,100},{5,29},{6,102},{7,31},{8,104},... | collective-permute-start | bytes 1769480 | tf_op jit(solution)/shard_map/ppermute | solution.py:29
  94.8 12.7 %collective-permute-start.23 = (bf16[2,240,384]{2,1,0:T(8,128)(2,1)}, bf16[2,240,384]{2,1,0:T(8,128)(2,1)S(1)}, u32[]{:S(2)}, u32[]{:S(2)}) collective-permute-start(bf16[2,240,384]{2,1,0:T(8,128)(2,1)} %get-tuple-element.40.refs_5_), channel_id=1, source_target_pairs={{0,8},{8,16},{16,24},{24,32},{32,40},{40,48},{48,56},{56,64},{64,7... | collective-permute-start | bytes 1105928 | tf_op jit(solution)/shard_map/ppermute | solution.py:55
  97.0 17.5 %collective-permute-start.25 = (bf16[2,240,384]{2,1,0:T(8,128)(2,1)}, bf16[2,240,384]{2,1,0:T(8,128)(2,1)S(1)}, u32[]{:S(2)}, u32[]{:S(2)}) collective-permute-start(bf16[2,240,384]{2,1,0:T(8,128)(2,1)} %get-tuple-element.41.refs_6_), channel_id=1, source_target_pairs={{0,8},{8,16},{16,24},{24,32},{32,40},{40,48},{48,56},{56,64},{64,7... | collective-permute-start | bytes 1105928 | tf_op jit(solution)/shard_map/ppermute | solution.py:55
  97.1 20.0 %collective-permute-start.27 = (bf16[2,240,384]{2,1,0:T(8,128)(2,1)}, bf16[2,240,384]{2,1,0:T(8,128)(2,1)S(1)}, u32[]{:S(2)}, u32[]{:S(2)}) collective-permute-start(bf16[2,240,384]{2,1,0:T(8,128)(2,1)} %get-tuple-element.40.refs_5_), channel_id=1, source_target_pairs={{0,120},{8,0},{16,8},{24,16},{32,24},{40,32},{48,40},{56,48},{64,5... | collective-permute-start | bytes 1105928 | tf_op jit(solution)/shard_map/ppermute | solution.py:55
  99.1 18.1 %collective-permute-start.29 = (bf16[2,240,384]{2,1,0:T(8,128)(2,1)}, bf16[2,240,384]{2,1,0:T(8,128)(2,1)S(1)}, u32[]{:S(2)}, u32[]{:S(2)}) collective-permute-start(bf16[2,240,384]{2,1,0:T(8,128)(2,1)} %get-tuple-element.41.refs_6_), channel_id=1, source_target_pairs={{0,120},{8,0},{16,8},{24,16},{32,24},{40,32},{48,40},{56,48},{64,5... | collective-permute-start | bytes 1105928 | tf_op jit(solution)/shard_map/ppermute | solution.py:55
  107.6 20.0 %collective-permute-start.24 = (bf16[2,240,384]{2,1,0:T(8,128)(2,1)S(1)}, bf16[2,240,384]{2,1,0:T(8,128)(2,1)S(1)}, u32[]{:S(2)}, u32[]{:S(2)}) collective-permute-start(bf16[2,240,384]{2,1,0:T(8,128)(2,1)S(1)} %collective-permute-done.23.refs_3_), channel_id=1, source_target_pairs={{0,8},{8,16},{16,24},{24,32},{32,40},{40,48},{48,56},{56,64},{64,7... | collective-permute-start | bytes 1105928 | tf_op jit(solution)/shard_map/ppermute | solution.py:55
  114.5 13.7 %collective-permute-start.26 = (bf16[2,240,384]{2,1,0:T(8,128)(2,1)S(1)}, bf16[2,240,384]{2,1,0:T(8,128)(2,1)S(1)}, u32[]{:S(2)}, u32[]{:S(2)}) collective-permute-start(bf16[2,240,384]{2,1,0:T(8,128)(2,1)S(1)} %collective-permute-done.25.refs_4_), channel_id=1, source_target_pairs={{0,8},{8,16},{16,24},{24,32},{32,40},{40,48},{48,56},{56,64},{64,7... | collective-permute-start | bytes 1105928 | tf_op jit(solution)/shard_map/ppermute | solution.py:55
  117.1 12.5 %collective-permute-start.28 = (bf16[2,240,384]{2,1,0:T(8,128)(2,1)S(1)}, bf16[2,240,384]{2,1,0:T(8,128)(2,1)S(1)}, u32[]{:S(2)}, u32[]{:S(2)}) collective-permute-start(bf16[2,240,384]{2,1,0:T(8,128)(2,1)S(1)} %collective-permute-done.27.refs_7_), channel_id=1, source_target_pairs={{0,120},{8,0},{16,8},{24,16},{32,24},{40,32},{48,40},{56,48},{64,5... | collective-permute-start | bytes 1105928 | tf_op jit(solution)/shard_map/ppermute | solution.py:55
  117.2 16.5 %collective-permute-start.30 = (bf16[2,240,384]{2,1,0:T(8,128)(2,1)S(1)}, bf16[2,240,384]{2,1,0:T(8,128)(2,1)S(1)}, u32[]{:S(2)}, u32[]{:S(2)}) collective-permute-start(bf16[2,240,384]{2,1,0:T(8,128)(2,1)S(1)} %collective-permute-done.29.refs_8_), channel_id=1, source_target_pairs={{0,120},{8,0},{16,8},{24,16},{32,24},{40,32},{48,40},{56,48},{64,5... | collective-permute-start | bytes 1105928 | tf_op jit(solution)/shard_map/ppermute | solution.py:55
  148.6 11.2 %collective-permute-start.34 = (bf16[2,225,384]{2,1,0:T(8,128)(2,1)S(1)}, bf16[2,225,384]{2,1,0:T(8,128)(2,1)S(1)}, u32[]{:S(2)}, u32[]{:S(2)}) collective-permute-start(bf16[2,225,384]{2,1,0:T(8,128)(2,1)S(1)} %get-tuple-element.50), channel_id=1, source_target_pairs={{0,2},{1,7},{2,4},{3,1},{4,6},{5,3},{6,0},{7,5},{8,10},{9,15},{10,... | collective-permute-start | bytes 1036808 | tf_op jit(solution)/shard_map/ppermute | solution.py:29
  (48 other events, 634.6 us)
